TPU v7x, 128 devices: a whole 4x4x4 slice. The times are simulated.
128 devices in a mesh: gz: 32 (over y, x, core), gy: 4 (over z).
Axes of the slice: x: 4, y: 4, z: 4, core: 2. Of those that a mesh axis runs over, the one named last changes fastest.
Arguments:
- flow_state: float32 [7, 768, 128, 128], P(None, 'gz', 'gy'), may hold values from -1.1 to 6, as said below
- block_tiles: int32 [32768, 4], P(('gz', 'gy')), may hold values from 0 to 98303, as said below
- bubble_place: float32 [3, 32768, 128], P(None, ('gz', 'gy')), may hold values from 0 to 1
- bubble_radius: float32 [32768, 128], P(('gz', 'gy')), may hold values from 0.2 to 0.5
- bubble_speed: float32 [32768, 128], P(('gz', 'gy')), may hold values from -3 to 3
- rest_ratio: float32 [32768, 128], P(('gz', 'gy')), may hold values from 0.8 to 1.25
Outputs:
- state_next: float32 [7, 768, 128, 128], P(None, 'gz', 'gy')
- bubble_source: float32 [768, 128, 128], P('gz', 'gy')
- bubble_motion: float32 [2, 32768, 128], P(None, ('gz', 'gy'))
Inputs may be any that keep to these rules, and one draw needn't show every extreme that they name: `flow_state`: conserved variables of primitives with liquid fraction 0.4 to 0.6, liquid density 0.7 to 1.4, gas density 0.05 to 0.1, each velocity component within 1.2, pressure 0.6 to 1.2; the partial densities are those fractions times the densities. `block_tiles`: each block lists rows (z, y), (z, y + 1), (z + 1, y), (z + 1, y + 1), all on one device's cells (z % 24 < 23, y % 32 < 31). Among the 256 blocks of one device, each device whose cells are named is named by exactly 8 blocks; one device is named so by every device.
All inputs are finite; a program needn't handle non-finite values.
Results may differ from a plain program's by a relative error of at most 0.0003.
Values sent between devices are 32-bit elements; how exact they have to be, the bound alone decides.
No kernel may reach another device: no remote copies, remote signals or barrier semaphores. Data moves between devices by JAX's collectives and lax.ppermute only.
A program may use at most 128 MiB of HBM per device.

v0:
```python
import math

import jax
import jax.numpy as jnp
from jax import lax
from jax.sharding import PartitionSpec as P

HB = 8


gamma_liquid = 4.4
stiff_liquid = 3.0
gamma_gas = 1.4
time_step = 0.08
liquid_sound = 20.0
surface_tension = 0.01
liquid_viscosity = 0.001
polytropic = 1.4
weno_eps = 1e-06
highest = lax.Precision.HIGHEST


def with_halo(cells, sides, width):
    for axis, dim in sides:
        count = lax.axis_size(axis)
        head = lax.slice_in_dim(cells, 0, width, axis=dim)
        tail = lax.slice_in_dim(cells, cells.shape[dim] - width, cells.shape[dim], axis=dim)
        cells = jnp.concatenate(
            [
                lax.ppermute(tail, axis, [(i, (i + 1) % count) for i in range(count)]),
                cells,
                lax.ppermute(head, axis, [((i + 1) % count, i) for i in range(count)]),
            ],
            axis=dim,
        )
    return cells


def mixture(fraction):
    stiffness = fraction / (gamma_liquid - 1.0) + (1.0 - fraction) / (gamma_gas - 1.0)
    offset_term = fraction * gamma_liquid * stiff_liquid / (gamma_liquid - 1.0)
    return (stiffness, offset_term)


def primitives(flow_state):
    density = flow_state[0] + flow_state[1]
    velocity = flow_state[2:5] / density
    stiffness, offset_term = mixture(flow_state[6])
    kinetic = 0.5 * density * jnp.sum(velocity * velocity, axis=0)
    pressure = (flow_state[5] - kinetic - offset_term) / stiffness
    return jnp.concatenate([flow_state[0:2], velocity, pressure[None], flow_state[6:7]], axis=0)


def weno_side(cell_first, cell_second, cell_third, cell_fourth, cell_fifth):
    guess_low = (2.0 * cell_first - 7.0 * cell_second + 11.0 * cell_third) / 6.0
    guess_mid = (-cell_second + 5.0 * cell_third + 2.0 * cell_fourth) / 6.0
    guess_high = (2.0 * cell_third + 5.0 * cell_fourth - cell_fifth) / 6.0
    smooth_low = (
        13.0 / 12.0 * (cell_first - 2.0 * cell_second + cell_third) ** 2
        + 0.25 * (cell_first - 4.0 * cell_second + 3.0 * cell_third) ** 2
    )
    smooth_mid = (
        13.0 / 12.0 * (cell_second - 2.0 * cell_third + cell_fourth) ** 2
        + 0.25 * (cell_second - cell_fourth) ** 2
    )
    smooth_high = (
        13.0 / 12.0 * (cell_third - 2.0 * cell_fourth + cell_fifth) ** 2
        + 0.25 * (3.0 * cell_third - 4.0 * cell_fourth + cell_fifth) ** 2
    )
    weight_low = 0.1 / (weno_eps + smooth_low) ** 2
    weight_mid = 0.6 / (weno_eps + smooth_mid) ** 2
    weight_high = 0.3 / (weno_eps + smooth_high) ** 2
    return (weight_low * guess_low + weight_mid * guess_mid + weight_high * guess_high) / (
        weight_low + weight_mid + weight_high
    )


def face_states(padded, array_axis):
    cell_count = padded.shape[array_axis] - 6

    def face_slice(first_index):
        return lax.slice_in_dim(padded, first_index, first_index + cell_count + 1, axis=array_axis)

    left_state = weno_side(
        face_slice(0), face_slice(1), face_slice(2), face_slice(3), face_slice(4)
    )
    right_state = weno_side(
        face_slice(5), face_slice(4), face_slice(3), face_slice(2), face_slice(1)
    )
    return (left_state, right_state)


def side_terms(primitive, normal):
    density = primitive[0] + primitive[1]
    velocity = primitive[2:5]
    normal_speed = velocity[normal]
    pressure = primitive[5]
    stiffness, offset_term = mixture(primitive[6])
    sound_speed = jnp.sqrt((pressure * (stiffness + 1.0) + offset_term) / (stiffness * density))
    energy = (
        stiffness * pressure + offset_term + 0.5 * density * jnp.sum(velocity * velocity, axis=0)
    )
    momentum = density * velocity
    conserved = jnp.concatenate([primitive[0:2], momentum, energy[None]], axis=0)
    unit_vector = (
        (jnp.arange(3) == normal).astype(jnp.float32).reshape((3,) + (1,) * (primitive.ndim - 1))
    )
    face_flux = jnp.concatenate(
        [
            primitive[0:2] * normal_speed,
            momentum * normal_speed + pressure * unit_vector,
            ((energy + pressure) * normal_speed)[None],
        ],
        axis=0,
    )
    return (density, normal_speed, pressure, sound_speed, conserved, face_flux, unit_vector)


def star_flux(primitive, terms, wave_speed, middle):
    density, normal_speed, pressure, sound_speed, conserved, face_flux, unit_vector = terms
    factor = (wave_speed - normal_speed) / (wave_speed - middle)
    star_velocity = primitive[2:5] * (1.0 - unit_vector) + middle * unit_vector
    star_energy = conserved[5] + (middle - normal_speed) * (
        density * middle + pressure / (wave_speed - normal_speed)
    )
    star_state = factor * jnp.concatenate(
        [primitive[0:2], density * star_velocity, star_energy[None]], axis=0
    )
    return face_flux + wave_speed * (star_state - conserved)


def hllc_flux(left_state, right_state, normal):
    terms_left = side_terms(left_state, normal)
    terms_right = side_terms(right_state, normal)
    density_left, speed_left, pressure_left, sound_left = terms_left[0:4]
    density_right, speed_right, pressure_right, sound_right = terms_right[0:4]
    wave_left = jnp.minimum(speed_left - sound_left, speed_right - sound_right)
    wave_right = jnp.maximum(speed_left + sound_left, speed_right + sound_right)
    middle = (
        pressure_right
        - pressure_left
        + density_left * speed_left * (wave_left - speed_left)
        - density_right * speed_right * (wave_right - speed_right)
    ) / (density_left * (wave_left - speed_left) - density_right * (wave_right - speed_right))
    star_left = star_flux(left_state, terms_left, wave_left, middle)
    star_right = star_flux(right_state, terms_right, wave_right, middle)
    face_flux = jnp.where(
        wave_left >= 0.0,
        terms_left[5],
        jnp.where(
            middle >= 0.0, star_left, jnp.where(wave_right > 0.0, star_right, terms_right[5])
        ),
    )
    fraction_flux = middle * jnp.where(middle >= 0.0, left_state[6], right_state[6])
    return (jnp.concatenate([face_flux, fraction_flux[None]], axis=0), middle)


def flux_sweep(padded, array_axis, normal):
    left_state, right_state = face_states(padded, array_axis)
    face_flux, middle = hllc_flux(left_state, right_state, normal)
    cell_count = padded.shape[array_axis] - 6
    upper_flux = lax.slice_in_dim(face_flux, 1, cell_count + 1, axis=array_axis)
    lower_flux = lax.slice_in_dim(face_flux, 0, cell_count, axis=array_axis)
    cell_values = lax.slice_in_dim(padded, 3, cell_count + 3, axis=array_axis)
    divergence = lax.slice_in_dim(
        middle, 1, cell_count + 1, axis=array_axis - 1
    ) - lax.slice_in_dim(middle, 0, cell_count, axis=array_axis - 1)
    change = lower_flux - upper_flux
    return jnp.concatenate([change[:6], (change[6] + cell_values[6] * divergence)[None]], axis=0)


def bubble_block(row_tiles, places, radius, wall_speed, rest_ratio):
    cell_count = row_tiles.shape[-1]
    lateral = jnp.arange(4)
    shift_level = (lateral // 2).astype(jnp.float32)
    shift_column = (lateral % 2).astype(jnp.float32)
    offset_level = places[:, 0]
    offset_column = places[:, 1]
    offset_along = places[:, 2] * (cell_count - 1)
    across = jnp.exp(
        -(
            (shift_level[None, None, :] - offset_level[..., None]) ** 2
            + (shift_column[None, None, :] - offset_column[..., None]) ** 2
        )
        / 2.0
    )
    positions = jnp.arange(cell_count).astype(jnp.float32)
    along = jnp.exp(-((positions[None, None, :] - offset_along[..., None]) ** 2) / 2.0)
    weight_total = jnp.sum(across, axis=-1) * jnp.sum(along, axis=-1)
    rowwise = jnp.einsum("gbx,gkx->gbk", along, row_tiles, precision=highest)
    sampled = jnp.sum(across * rowwise, axis=-1) / weight_total
    rest_radius = rest_ratio * radius
    gas_pressure = (1.0 + 2.0 * surface_tension / rest_radius) * (rest_radius / radius) ** (
        3.0 * polytropic
    )
    wall_pressure = (
        gas_pressure - 2.0 * surface_tension / radius - 4.0 * liquid_viscosity * wall_speed / radius
    )
    gas_rate = -3.0 * polytropic * gas_pressure * wall_speed / radius
    mach_number = wall_speed / liquid_sound
    acceleration = (
        (1.0 + mach_number) * (wall_pressure - sampled)
        + radius * gas_rate / liquid_sound
        - 1.5 * (1.0 - mach_number / 3.0) * wall_speed**2
    ) / ((1.0 - mach_number) * radius)
    motion = jnp.stack(
        [radius + time_step * wall_speed, wall_speed + time_step * acceleration], axis=1
    )
    share_rate = 4.0 * math.pi * radius * radius * wall_speed / weight_total
    deposit = jnp.einsum("gbk,gbx->gkx", across * share_rate[..., None], along, precision=highest)
    return (motion, deposit)


def run_blocks(row_tiles, places, radius, wall_speed, rest_ratio):
    block_count = row_tiles.shape[0]
    group_size = math.gcd(block_count, 32)

    def regroup(values):
        return values.reshape((block_count // group_size, group_size) + values.shape[1:])

    def one_group(inputs):
        return bubble_block(inputs[0], inputs[1], inputs[2], inputs[3], inputs[4])

    motion, deposit = lax.map(
        one_group,
        (
            regroup(row_tiles),
            regroup(places),
            regroup(radius),
            regroup(wall_speed),
            regroup(rest_ratio),
        ),
    )
    motion = motion.reshape((block_count,) + motion.shape[2:])
    deposit = deposit.reshape((block_count,) + deposit.shape[2:])
    return (motion, deposit)


def body(flow_state, block_tiles, bubble_place, bubble_radius, bubble_speed, rest_ratio):
    primitive = primitives(flow_state)
    padded = with_halo(primitive, (("gz", 1), ("gy", 2)), 3)
    wrapped = jnp.concatenate([primitive[..., -3:], primitive, primitive[..., :3]], axis=3)
    change = flux_sweep(wrapped, 3, 0)
    change = change + flux_sweep(padded[:, 3:-3, :, :], 2, 1)
    change = change + flux_sweep(padded[:, :, 3:-3, :], 1, 2)
    slab_depth = flow_state.shape[1]
    height = flow_state.shape[2]
    length = flow_state.shape[3]
    across_gy = lax.axis_size("gy")
    devices = lax.axis_size("gz") * across_gy
    full_height = height * across_gy
    blocks = block_tiles.shape[0]
    grid_level = block_tiles // full_height
    column = block_tiles % full_height
    local_rows = grid_level % slab_depth * height + column % height
    owner_home = grid_level[:, 0] // slab_depth * across_gy + column[:, 0] // height
    earlier = jnp.arange(blocks)[:, None] > jnp.arange(blocks)[None, :]
    same_home = owner_home[:, None] == owner_home[None, :]
    rank_within = jnp.sum((earlier & same_home).astype(jnp.int32), axis=1)
    pressure_rows = primitive[5].reshape(slab_depth * height, length)
    places = jnp.transpose(bubble_place, (1, 0, 2))
    wanted = (
        jnp.full((devices, HB, 4), -1, jnp.int32)
        .at[owner_home, rank_within]
        .set(local_rows)
        .reshape(devices, 4 * HB)
    )
    asked_rows = lax.all_to_all(wanted, ("gz", "gy"), split_axis=0, concat_axis=0, tiled=True)
    present = asked_rows >= 0
    safe_rows = jnp.where(present, asked_rows, 0)
    served = jnp.where(present[..., None], pressure_rows[safe_rows], 0.0)
    fetched = lax.all_to_all(served, ("gz", "gy"), split_axis=0, concat_axis=0, tiled=True)
    fetched = fetched.reshape(devices, HB, 4, length)[owner_home, rank_within]
    motion, deposit = run_blocks(fetched, places, bubble_radius, bubble_speed, rest_ratio)
    outgoing = (
        jnp.zeros((devices, HB, 4, length), jnp.float32)
        .at[owner_home, rank_within]
        .set(deposit)
        .reshape(devices, 4 * HB, length)
    )
    returned = lax.all_to_all(outgoing, ("gz", "gy"), split_axis=0, concat_axis=0, tiled=True)
    source_rows = (
        jnp.zeros((slab_depth * height, length), jnp.float32)
        .at[safe_rows]
        .add(jnp.where(present[..., None], returned, 0.0))
    )
    motion_out = jnp.transpose(motion, (1, 0, 2))
    bubble_source = source_rows.reshape(slab_depth, height, length)
    state_next = flow_state + time_step * change
    state_next = jnp.concatenate(
        [state_next[:6], (state_next[6] - time_step * bubble_source)[None]], axis=0
    )
    return (state_next, bubble_source, motion_out)


def solution(mesh):
    in_specs = (
        P(None, "gz", "gy", None),
        P(("gz", "gy"), None),
        P(None, ("gz", "gy"), None),
        P(("gz", "gy"), None),
        P(("gz", "gy"), None),
        P(("gz", "gy"), None),
    )
    out_specs = (P(None, "gz", "gy", None), P("gz", "gy", None), P(None, ("gz", "gy"), None))
    return jax.shard_map(body, mesh=mesh, in_specs=in_specs, out_specs=out_specs, check_vma=False)
```

profile of v0, /device:TPU:1, one launch (start us, length us, event | category | flops | bytes accessed | tf_op | source)
XLA Modules:
  0.0 402.1 jit_solution(14596621497025402854)
XLA Ops:
  6.9 2.6 collective-permute-start
  10.0 11.6 %scatter_fusion = s32[128,8,4]{2,1,0:T(8,128)S(1)} fusion(s32[128,8,4]{2,1,0:T(8,128)S(1)} %broadcast_in_dim.89, s32[256]{0:T(256)S(1)} %bitcast.486, s32[256,4]{1,0:T(8,128)S(1)} %copy.28), kind=kCustom, calls=%fused_computation.2 | custom fusion | bytes 14336 | tf_op jit(solution)/shard_map/scatter | solution.py:265
  22.5 11.5 %all-to-all-start = ((s32[128,1,32]{2,1,0:T(1,128)}), s32[128,1,32]{2,1,0:T(1,128)}, u32[]{:S(2)}, u32[]{:S(2)}) async-start(s32[128,1,32]{2,1,0:T(1,128)} %copy.30), calls=%async_computation | async-start | bytes 131072 | tf_op jit(solution)/shard_map/all_to_all | solution.py:268
  36.9 3.3 pad_maximum_fusion.4
  40.3 27.2 %add_divide_fusion = (f32[7,24,32,129]{3,2,1,0:T(8,128)S(1)}, f32[7,24,32,129]{3,2,1,0:T(8,128)S(1)}) fusion(f32[7,24,32,131]{3,2,1,0:T(8,128)S(1)} %get-tuple-element.295, f32[7,24,32,131]{3,2,1,0:T(8,128)S(1)} %get-tuple-element.296), kind=kLoop, calls=%fused_computation.82 | loop fusion | flops 85994496 | bytes 22192128 | tf_op jit(solution)/shard_map/div | solution.py:73
  67.5 3.3 select_multiply_fusion
  70.8 3.2 broadcast_multiply_fusion
  74.1 2.3 broadcast_compare_fusion.2
  76.4 6.4 %multiply_add_fusion.9 = (f32[3,24,32,129]{3,2,1,0:T(8,128)S(1)}, f32[3,24,32,129]{3,2,1,0:T(8,128)S(1)}, f32[3,24,32,129]{3,2,1,0:T(8,128)S(1)}, f32[24,32,129]...) fusion(f32[3]{0:T(128)S(1)} %compare_convert_fusion.2, ...), kind=kLoop, calls=%fused_computation.242 | loop fusion | flops 5448960 | bytes 13077528 | tf_op jit(solution)/shard_map/add | solution.py:111
  82.8 4.8 %multiply_add_fusion.18 = (f32[1,24,32,129]{3,2,1,0:T(8,128)}, f32[1,24,32,129]{3,2,1,0:T(8,128)S(1)}, f32[24,32,129]{2,1,0:T(8,128)}, f32[24,32,129]{2,1,0:T(8,...) fusion(f32[1,24,32,129]{3,2,1,0:T(8,128)S(1)} %get-tuple-element.202, ...), kind=kLoop, calls=%fused_computation.288 | loop fusion | flops 3764736 | bytes 7529472 | tf_op jit(solution)/shard_map/add | solution.py:123
  91.9 8.4 %fusion.74 = f32[6,24,32,129]{3,2,1,0:T(8,128)S(1)} fusion(f32[2,24,32,129]{3,2,1,0:T(8,128)} %get-tuple-element.338, f32[2,24,32,129]{3,2,1,0:T(8,128)} %get-tuple-element.247, f32[1,24,32,129]{3,2,1,0:T(8,128)} %get-tuple-element.337, f32[3,24,32,129]{3,2,1,0:T(8,128)S(1)} %get-tuple-element.214, f32[2,24,32,129]{3,2,1,0:T(8,128)} %get-tuple-element.339, ...), kind=kLoop, calls=%fused_computation.120 | loop fusion | flops 13671936 | bytes 16941312 | tf_op jit(solution)/shard_map/jit(_where)/select_n | solution.py:147
  100.4 2.4 fusion.138
  105.0 14.2 %gather_fusion = f32[4096,128]{1,0:T(8,128)} fusion(f32[768,128]{1,0:T(8,128)S(1)} %bitcast_divide_fusion.2, s32[4096]{0:T(1024)S(1)} %broadcast_clamp_fusion), kind=kCustom, calls=%fused_computation | custom fusion | bytes 4210688 | tf_op jit(solution)/shard_map/gather | solution.py:271
  119.2 4.3 %broadcast_select_fusion.1 = f32[128,32,128]{2,1,0:T(8,128)} fusion(f32[128,32,128]{2,1,0:T(8,128)} %bitcast.495, pred[128,32]{1,0:T(8,128)(4,1)S(1)} %copy.32), kind=kLoop, calls=%fused_computation.268 | loop fusion | flops 524288 | bytes 4198400 | tf_op jit(solution)/shard_map/jit(_where)/select_n | solution.py:271
  123.5 10.2 %all-to-all-start.1 = ((f32[128,32,128]{2,1,0:T(8,128)}), f32[128,32,128]{2,1,0:T(8,128)}, u32[]{:S(2)}, u32[]{:S(2)}) async-start(f32[128,32,128]{2,1,0:T(8,128)} %broadcast_select_fusion.1), calls=%async_computation.1 | async-start | bytes 4194304 | tf_op jit(solution)/shard_map/all_to_all | solution.py:272
  140.1 12.4 %add_divide_fusion.2 = (f32[7,25,32,128]{3,2,1,0:T(8,128)S(1)}, f32[7,25,32,128]{3,2,1,0:T(8,128)S(1)}) fusion(f32[7,27,32,128]{3,2,1,0:T(8,128)S(1)} %get-tuple-element.291, f32[7,27,32,128]{3,2,1,0:T(8,128)S(1)} %get-tuple-element.292), kind=kLoop, calls=%fused_computation.182 | loop fusion | flops 88883200 | bytes 22937600 | tf_op jit(solution)/shard_map/div | solution.py:73
  160.3 8.7 %collective-permute-done.2 = f32[7,30,3,128]{3,2,1,0:T(4,128)S(1)} collective-permute-done((f32[7,30,3,128]{3,2,1,0:T(4,128)S(1)}, f32[7,30,3,128]{3,2,1,0:T(4,128)S(1)}, u32[]{:S(2)}, u32[]{:S(2)}) %collective-permute-start.2) | collective-permute-done | bytes 322592 | tf_op jit(solution)/shard_map/ppermute | solution.py:30
  169.0 4.3 %pad_maximum_fusion.5 = (f32[7,30,35,128]{3,2,1,0:T(8,128)S(1)}, f32[7,30,35,128]{3,2,1,0:T(8,128)S(1)}) fusion(f32[7,30,3,128]{3,2,1,0:T(4,128)S(1)} %collective-permute-done.3, f32[7,3,32,128]{3,2,1,0:T(8,128)} %collective-permute-done.1, f32[1,24,32,128]{3,2,1,0:T(8,128)S(1)} %get-tuple-element.299, f32[1,24,32,128]{3,2,1,0:T(8,128)S(1)} %get-tuple-element.301, ...), kind=kLoop, calls=%fused_computation.124 | loop fusion | flops 11289600 | bytes 11612160 | tf_op jit(solution)/shard_map/concatenate | solution.py:28
  173.3 15.9 %add_divide_fusion.1 = (f32[7,24,33,128]{3,2,1,0:T(8,128)S(1)}, f32[7,24,33,128]{3,2,1,0:T(8,128)S(1)}) fusion(f32[7,30,35,128]{3,2,1,0:T(8,128)S(1)} %get-tuple-element.272, f32[7,30,35,128]{3,2,1,0:T(8,128)S(1)} %get-tuple-element.273), kind=kLoop, calls=%fused_computation.132 | loop fusion | flops 87994368 | bytes 22708224 | tf_op jit(solution)/shard_map/div | solution.py:73
  189.2 2.4 select_multiply_fusion.1
  194.2 2.0 broadcast_multiply_fusion.2
  196.3 3.3 multiply_add_fusion.15
  201.6 3.6 gather_fusion.1
  205.2 93.5 %while.14 = (s32[]{:T(128)}, f32[8,32,2,128]{3,1,0,2:T(8,128)}, f32[8,32,4,128]{3,2,1,0:T(4,128)}, f32[8,32,128]{2,1,0:T(8,128)}, f32[8,32,128]{2,1,0:T(8,128)},...) while((s32[]{:T(128)}, f32[8,32,2,128]{3,1,0,2:T(8,128)}, ...), condition=%wide.region_13.14_spmd, body=%wide.region_9.13_spmd.sunk | while | flops 57721016 | bytes 823017 | solution.py:224
  208.2 2.8 fusion.246
  211.0 4.5 %fusion.240 = f32[32,128]{1,0:T(8,128)S(1)} fusion(f32[32,128]{1,0:T(8,128)S(1)} %get-tuple-element.396, f32[128]{0:T(128)S(1)} %iota_convert_fusion.2, f32[8,32,4,128]{3,2,1,0:T(4,128)} %get-tuple-element.428, s32[]{:T(128)} %get-tuple-element.412, f32[32,128]{1,0:T(8,128)S(1)} %get-tuple-element.397, f32[4]{0:T(128)S(1)} %get-tuple-element.398, ...), kind=kOutput, calls=%fused_computation.12.clone.1 | convolution fusion | flops 27406336 | bytes 132128 | tf_op jit(solution)/shard_map/while/body/eval_jaxpr/gbx,gkx->gbk/dot_general | solution.py:190
  219.9 2.8 fusion.246
  222.7 4.5 %fusion.240 = f32[32,128]{1,0:T(8,128)S(1)} fusion(f32[32,128]{1,0:T(8,128)S(1)} %get-tuple-element.396, f32[128]{0:T(128)S(1)} %iota_convert_fusion.2, f32[8,32,4,128]{3,2,1,0:T(4,128)} %get-tuple-element.428, s32[]{:T(128)} %get-tuple-element.412, f32[32,128]{1,0:T(8,128)S(1)} %get-tuple-element.397, f32[4]{0:T(128)S(1)} %get-tuple-element.398, ...), kind=kOutput, calls=%fused_computation.12.clone.1 | convolution fusion | flops 27406336 | bytes 132128 | tf_op jit(solution)/shard_map/while/body/eval_jaxpr/gbx,gkx->gbk/dot_general | solution.py:190
  231.6 2.8 fusion.246
  234.4 4.5 %fusion.240 = f32[32,128]{1,0:T(8,128)S(1)} fusion(f32[32,128]{1,0:T(8,128)S(1)} %get-tuple-element.396, f32[128]{0:T(128)S(1)} %iota_convert_fusion.2, f32[8,32,4,128]{3,2,1,0:T(4,128)} %get-tuple-element.428, s32[]{:T(128)} %get-tuple-element.412, f32[32,128]{1,0:T(8,128)S(1)} %get-tuple-element.397, f32[4]{0:T(128)S(1)} %get-tuple-element.398, ...), kind=kOutput, calls=%fused_computation.12.clone.1 | convolution fusion | flops 27406336 | bytes 132128 | tf_op jit(solution)/shard_map/while/body/eval_jaxpr/gbx,gkx->gbk/dot_general | solution.py:190
  243.3 2.7 fusion.246
  246.1 4.5 %fusion.240 = f32[32,128]{1,0:T(8,128)S(1)} fusion(f32[32,128]{1,0:T(8,128)S(1)} %get-tuple-element.396, f32[128]{0:T(128)S(1)} %iota_convert_fusion.2, f32[8,32,4,128]{3,2,1,0:T(4,128)} %get-tuple-element.428, s32[]{:T(128)} %get-tuple-element.412, f32[32,128]{1,0:T(8,128)S(1)} %get-tuple-element.397, f32[4]{0:T(128)S(1)} %get-tuple-element.398, ...), kind=kOutput, calls=%fused_computation.12.clone.1 | convolution fusion | flops 27406336 | bytes 132128 | tf_op jit(solution)/shard_map/while/body/eval_jaxpr/gbx,gkx->gbk/dot_general | solution.py:190
  255.0 2.8 fusion.246
  257.7 4.5 %fusion.240 = f32[32,128]{1,0:T(8,128)S(1)} fusion(f32[32,128]{1,0:T(8,128)S(1)} %get-tuple-element.396, f32[128]{0:T(128)S(1)} %iota_convert_fusion.2, f32[8,32,4,128]{3,2,1,0:T(4,128)} %get-tuple-element.428, s32[]{:T(128)} %get-tuple-element.412, f32[32,128]{1,0:T(8,128)S(1)} %get-tuple-element.397, f32[4]{0:T(128)S(1)} %get-tuple-element.398, ...), kind=kOutput, calls=%fused_computation.12.clone.1 | convolution fusion | flops 27406336 | bytes 132128 | tf_op jit(solution)/shard_map/while/body/eval_jaxpr/gbx,gkx->gbk/dot_general | solution.py:190
  266.7 2.8 fusion.246
  269.4 4.5 %fusion.240 = f32[32,128]{1,0:T(8,128)S(1)} fusion(f32[32,128]{1,0:T(8,128)S(1)} %get-tuple-element.396, f32[128]{0:T(128)S(1)} %iota_convert_fusion.2, f32[8,32,4,128]{3,2,1,0:T(4,128)} %get-tuple-element.428, s32[]{:T(128)} %get-tuple-element.412, f32[32,128]{1,0:T(8,128)S(1)} %get-tuple-element.397, f32[4]{0:T(128)S(1)} %get-tuple-element.398, ...), kind=kOutput, calls=%fused_computation.12.clone.1 | convolution fusion | flops 27406336 | bytes 132128 | tf_op jit(solution)/shard_map/while/body/eval_jaxpr/gbx,gkx->gbk/dot_general | solution.py:190
  278.4 2.8 fusion.246
  281.1 4.5 %fusion.240 = f32[32,128]{1,0:T(8,128)S(1)} fusion(f32[32,128]{1,0:T(8,128)S(1)} %get-tuple-element.396, f32[128]{0:T(128)S(1)} %iota_convert_fusion.2, f32[8,32,4,128]{3,2,1,0:T(4,128)} %get-tuple-element.428, s32[]{:T(128)} %get-tuple-element.412, f32[32,128]{1,0:T(8,128)S(1)} %get-tuple-element.397, f32[4]{0:T(128)S(1)} %get-tuple-element.398, ...), kind=kOutput, calls=%fused_computation.12.clone.1 | convolution fusion | flops 27406336 | bytes 132128 | tf_op jit(solution)/shard_map/while/body/eval_jaxpr/gbx,gkx->gbk/dot_general | solution.py:190
  290.1 2.8 fusion.246
  292.8 4.5 %fusion.240 = f32[32,128]{1,0:T(8,128)S(1)} fusion(f32[32,128]{1,0:T(8,128)S(1)} %get-tuple-element.396, f32[128]{0:T(128)S(1)} %iota_convert_fusion.2, f32[8,32,4,128]{3,2,1,0:T(4,128)} %get-tuple-element.428, s32[]{:T(128)} %get-tuple-element.412, f32[32,128]{1,0:T(8,128)S(1)} %get-tuple-element.397, f32[4]{0:T(128)S(1)} %get-tuple-element.398, ...), kind=kOutput, calls=%fused_computation.12.clone.1 | convolution fusion | flops 27406336 | bytes 132128 | tf_op jit(solution)/shard_map/while/body/eval_jaxpr/gbx,gkx->gbk/dot_general | solution.py:190
  300.6 26.0 %scatter_fusion.1 = f32[128,8,4,128]{3,2,1,0:T(4,128)} fusion(f32[128,8,4,128]{3,2,1,0:T(4,128)} %broadcast_in_dim.91, s32[256]{0:T(256)S(1)} %bitcast.487, f32[256,4,128]{2,1,0:T(4,128)} %bitcast.508), kind=kCustom, calls=%fused_computation.3 | custom fusion | bytes 1574912 | tf_op jit(solution)/shard_map/scatter | solution.py:278
  326.6 7.9 %all-to-all-start.2 = ((f32[128,32,128]{2,1,0:T(8,128)}), f32[128,32,128]{2,1,0:T(8,128)}, u32[]{:S(2)}, u32[]{:S(2)}) async-start(f32[128,32,128]{2,1,0:T(8,128)} %bitcast.96), calls=%async_computation.2 | async-start | bytes 4194304 | tf_op jit(solution)/shard_map/all_to_all | solution.py:281
  334.5 2.1 add_multiply_fusion.2
  337.4 4.8 %fusion.109 = f32[6,24,33,128]{3,2,1,0:T(8,128)S(1)} fusion(f32[2,24,33,128]{3,2,1,0:T(8,128)} %get-tuple-element.334, f32[2,24,33,128]{3,2,1,0:T(8,128)} %get-tuple-element.263, f32[1,24,33,128]{3,2,1,0:T(8,128)S(1)} %get-tuple-element.333, f32[3,24,33,128]{3,2,1,0:T(8,128)S(1)} %get-tuple-element.195, f32[2,24,33,128]{3,2,1,0:T(8,128)} %get-tuple-element.335, ...), kind=kLoop, calls=%fused_computation.178 | loop fusion | flops 13989888 | bytes 17335296 | tf_op jit(solution)/shard_map/jit(_where)/select_n | solution.py:147
  350.7 13.9 %all-to-all-done.2 = f32[128,32,128]{2,1,0:T(8,128)} async-done(((f32[128,32,128]{2,1,0:T(8,128)}), f32[128,32,128]{2,1,0:T(8,128)}, u32[]{:S(2)}, u32[]{:S(2)}) %all-to-all-start.2) | async-done | bytes 2097184 | tf_op jit(solution)/shard_map/all_to_all | solution.py:281
  364.7 4.2 %broadcast_select_fusion = f32[128,32,128]{2,1,0:T(8,128)} fusion(f32[128,32,128]{2,1,0:T(8,128)} %all-to-all-done.2, pred[128,32]{1,0:T(8,128)(4,1)S(1)} %copy.32), kind=kLoop, calls=%fused_computation.267 | loop fusion | flops 524288 | bytes 4198400 | tf_op jit(solution)/shard_map/jit(_where)/select_n | solution.py:285
  368.9 29.2 %scatter_custom_fusion.2 = f32[768,128]{1,0:T(8,128)S(1)} fusion(s32[4096]{0:T(1024)S(1)} %reshape.662, f32[4096,128]{1,0:T(8,128)} %bitcast.505, f32[]{:T(128)} %constant.333.clone.1), kind=kCustom, calls=%fused_computation.445 | custom fusion | flops 524288 | bytes 393728 | tf_op jit(solution)/shard_map/scatter-add | solution.py:285
  398.3 3.6 pad_maximum_fusion.19
  (214 shorter events, 82.6 us)
Async XLA Ops:
  0.6 4.1 %copy-start.2 = (f32[7,24,32,128]{3,2,1,0:T(8,128)S(1)}, f32[7,24,32,128]{3,2,1,0:T(8,128)}, u32[]{:S(2)}) copy-start(f32[7,24,32,128]{3,2,1,0:T(8,128)} %param.8) | copy-start | bytes 8257540
  4.7 2.3 copy-start.19
  4.7 4.8 %copy-start.33 = (s32[256,4]{0,1:T(4,128)S(1)}, s32[256,4]{0,1:T(4,128)}, u32[]{:S(2)}) copy-start(s32[256,4]{0,1:T(4,128)} %param.9) | copy-start | bytes 12292
  6.9 126.8 %collective-permute-start = (f32[7,3,32,128]{3,2,1,0:T(8,128)}, f32[7,3,32,128]{3,2,1,0:T(8,128)}, u32[]{:S(2)}, u32[]{:S(2)}) collective-permute-start(f32[7,3,32,128]{3,2,1,0:T(8,128)} %get-tuple-element.293), channel_id=1, source_target_pairs={{0,4},{4,8},{8,12},{12,16},{16,20},{20,24},{24,28},{28,32},{32,36}... | collective-permute-start | bytes 1032200 | tf_op jit(solution)/shard_map/ppermute | solution.py:30
  9.5 124.2 %collective-permute-start.1 = (f32[7,3,32,128]{3,2,1,0:T(8,128)}, f32[7,3,32,128]{3,2,1,0:T(8,128)}, u32[]{:S(2)}, u32[]{:S(2)}) collective-permute-start(f32[7,3,32,128]{3,2,1,0:T(8,128)} %get-tuple-element.294), channel_id=1, source_target_pairs={{4,0},{8,4},{12,8},{16,12},{20,16},{24,20},{28,24},{32,28},{36,32}... | collective-permute-start | bytes 1032200 | tf_op jit(solution)/shard_map/ppermute | solution.py:32
  22.5 80.5 %all-to-all-start = ((s32[128,1,32]{2,1,0:T(1,128)}), s32[128,1,32]{2,1,0:T(1,128)}, u32[]{:S(2)}, u32[]{:S(2)}) async-start(s32[128,1,32]{2,1,0:T(1,128)} %copy.30), calls=%async_computation | async-start | bytes 131072 | tf_op jit(solution)/shard_map/all_to_all | solution.py:268
  70.8 3.3 copy-start.10
  70.8 3.3 copy-start.12
  74.1 2.3 copy-start.11
  74.1 2.3 copy-start.13
  87.6 1.7 copy-start.7
  87.6 1.7 copy-start.9
  87.6 1.7 copy-start.24
  87.6 2.5 copy-start.25
  90.1 1.8 copy-start.8
  91.9 8.4 %copy-start.26 = (f32[1,24,32,129]{3,2,1,0:T(8,128)S(1)}, f32[1,24,32,129]{3,2,1,0:T(8,128)}, u32[]{:S(2)}) copy-start(f32[1,24,32,129]{3,2,1,0:T(8,128)} %get-tuple-element.197) | copy-start | bytes 1188868
  100.3 2.5 copy-start.20
  100.3 2.5 copy-start.28
  100.3 2.4 copy-start.29
  100.3 2.4 copy-start.30
  100.4 2.4 copy-start.31
  123.5 78.1 %all-to-all-start.1 = ((f32[128,32,128]{2,1,0:T(8,128)}), f32[128,32,128]{2,1,0:T(8,128)}, u32[]{:S(2)}, u32[]{:S(2)}) async-start(f32[128,32,128]{2,1,0:T(8,128)} %broadcast_select_fusion.1), calls=%async_computation.1 | async-start | bytes 4194304 | tf_op jit(solution)/shard_map/all_to_all | solution.py:272
  134.9 34.1 %collective-permute-start.2 = (f32[7,30,3,128]{3,2,1,0:T(4,128)S(1)}, f32[7,30,3,128]{3,2,1,0:T(4,128)S(1)}, u32[]{:S(2)}, u32[]{:S(2)}) collective-permute-start(f32[7,30,3,128]{3,2,1,0:T(4,128)S(1)} %get-tuple-element.275), channel_id=1, source_target_pairs={{0,1},{1,2},{2,3},{3,0},{4,5},{5,6},{6,7},{7,4},{8,9},{9,10},{10,1... | collective-permute-start | bytes 967688 | tf_op jit(solution)/shard_map/ppermute | solution.py:30
  136.5 32.5 %collective-permute-start.3 = (f32[7,30,3,128]{3,2,1,0:T(4,128)S(1)}, f32[7,30,3,128]{3,2,1,0:T(4,128)S(1)}, u32[]{:S(2)}, u32[]{:S(2)}) collective-permute-start(f32[7,30,3,128]{3,2,1,0:T(4,128)S(1)} %get-tuple-element.274), channel_id=1, source_target_pairs={{1,0},{2,1},{3,2},{0,3},{5,4},{6,5},{7,6},{4,7},{9,8},{10,9},{11,1... | collective-permute-start | bytes 967688 | tf_op jit(solution)/shard_map/ppermute | solution.py:32
  153.9 0.6 copy-start.36
  160.3 8.7 %copy-start.5 = (f32[7,24,32,128]{3,2,1,0:T(8,128)}, f32[7,24,32,128]{3,2,1,0:T(8,128)S(1)}, u32[]{:S(2)}) copy-start(f32[7,24,32,128]{3,2,1,0:T(8,128)S(1)} %fusion.134) | copy-start | bytes 8257540
  189.2 10.4 %copy-start = (f32[7,24,33,128]{3,2,1,0:T(8,128)}, f32[7,24,33,128]{3,2,1,0:T(8,128)S(1)}, u32[]{:S(2)}) copy-start(f32[7,24,33,128]{3,2,1,0:T(8,128)S(1)} %get-tuple-element.236) | copy-start | bytes 8515588
  189.2 10.4 %copy-start.1 = (f32[7,24,33,128]{3,2,1,0:T(8,128)}, f32[7,24,33,128]{3,2,1,0:T(8,128)S(1)}, u32[]{:S(2)}) copy-start(f32[7,24,33,128]{3,2,1,0:T(8,128)S(1)} %get-tuple-element.237) | copy-start | bytes 8515588
  191.6 8.0 %copy-start.16 = (f32[1,24,33,128]{3,2,1,0:T(8,128)}, f32[1,24,33,128]{3,2,1,0:T(8,128)S(1)}, u32[]{:S(2)}) copy-start(f32[1,24,33,128]{3,2,1,0:T(8,128)S(1)} %get-tuple-element.181) | copy-start | bytes 1216516
  194.2 2.0 copy-start.34
  194.2 2.1 copy-start.35
  326.6 38.1 %all-to-all-start.2 = ((f32[128,32,128]{2,1,0:T(8,128)}), f32[128,32,128]{2,1,0:T(8,128)}, u32[]{:S(2)}, u32[]{:S(2)}) async-start(f32[128,32,128]{2,1,0:T(8,128)} %bitcast.96), calls=%async_computation.2 | async-start | bytes 4194304 | tf_op jit(solution)/shard_map/all_to_all | solution.py:281
  334.5 2.3 copy-start.14
  334.5 2.7 copy-start.15
  334.5 2.8 copy-start.17
  334.5 2.9 copy-start.18
  337.4 4.8 %copy-start.27 = (f32[1,24,33,128]{3,2,1,0:T(8,128)S(1)}, f32[1,24,33,128]{3,2,1,0:T(8,128)}, u32[]{:S(2)}) copy-start(f32[1,24,33,128]{3,2,1,0:T(8,128)} %get-tuple-element.178) | copy-start | bytes 1216516
  342.2 2.3 copy-start.4
  342.3 2.6 copy-start.6
  342.8 3.0 copy-start.3
  342.8 3.0 copy-start.21
  342.8 3.1 copy-start.22
  342.8 3.4 copy-start.23
  343.2 4.3 %slice-start = ((f32[7,24,32,128]{3,2,1,0:T(8,128)}), f32[6,24,32,128]{3,2,1,0:T(8,128)S(1)}, s32[]{:S(2)}) async-start(f32[7,24,32,128]{3,2,1,0:T(8,128)} %fusion.138), calls=%async_computation.3 | async-start | bytes 4718592 | tf_op jit(solution)/shard_map/slice | solution.py:169
  343.2 4.5 %slice-start.1 = ((f32[7,24,32,128]{3,2,1,0:T(8,128)}), f32[6,24,32,128]{3,2,1,0:T(8,128)S(1)}, s32[]{:S(2)}) async-start(f32[7,24,32,128]{3,2,1,0:T(8,128)} %copy-done.5), calls=%async_computation.4 | async-start | bytes 4718592 | tf_op jit(solution)/shard_map/slice | solution.py:169
  398.2 3.8 copy-start.32
where the time goes:
time: 409 us; the launch traced here: 402 us
  other arithmetic  208 us (51%)
  local copies, waits for them, and re-layouts  76.1 us (19%)
  matrix products  57.6 us (14%)
  starting transfers between devices  35.6 us (9%)
  waiting for transfers between devices  22.6 us (6%)
    div x3, other arithmetic, weno_side(): (weight_low * guess_low + weight_mid * guess_mid + weight_high * guess_hi...  55.5 us
    dot_general x8, matrix products, bubble_block(): rowwise = jnp.einsum('gbx,gkx->gbk', along, row_tiles, precision=highest)  35.6 us
    scatter-add x1, other arithmetic, body(): source_rows = jnp.zeros((slab_depth * height, length), jnp.float32).at[sa...  29.2 us
    scatter x1, local copies, waits for them, and re-layouts, body(): outgoing = jnp.zeros((devices, HB, 4, length), jnp.float32).at[owner_home...  26 us
    dot_general x8, matrix products, bubble_block(): jnp.einsum('gbk,gbx->gkx', across * share_rate[..., None], along, precisi...  22 us
    select_n x3, other arithmetic, hllc_flux(): jnp.where(wave_left >= 0.0, terms_left[5], jnp.where(middle >= 0.0, star_...  15.1 us
    gather x1, local copies, waits for them, and re-layouts, body(): served = jnp.where(present[..., None], pressure_rows[safe_rows], 0.0)  14.2 us
    all_to_all x1, waiting for transfers between devices, body(): lax.all_to_all(outgoing, ('gz', 'gy'), split_axis=0, concat_axis=0, tiled...  13.9 us
  transfers between devices with their start and end apart: 7, of which 2 were waited for; matrix products, arithmetic and copies ran while one was open for 42% of the time, Pallas kernels for 0%

commit v1 on v0

v1 whole, which is shorter than its diff:
```python
import functools
import math

import jax
import jax.numpy as jnp
from jax import lax
from jax.experimental import pallas as pl
from jax.experimental.pallas import tpu as pltpu
from jax.sharding import PartitionSpec as P

HB = 8
gamma_liquid = 4.4
stiff_liquid = 3.0
gamma_gas = 1.4
time_step = 0.08
liquid_sound = 20.0
surface_tension = 0.01
liquid_viscosity = 0.001
polytropic = 1.4
weno_eps = 1e-06
stiff_base = 1.0 / (gamma_gas - 1.0)
stiff_slope = 1.0 / (gamma_liquid - 1.0) - 1.0 / (gamma_gas - 1.0)
offset_slope = gamma_liquid * stiff_liquid / (gamma_liquid - 1.0)
pressure_mid = 0.9

VMEM = pl.BlockSpec(memory_space=pltpu.VMEM)
SMEM = pl.BlockSpec(memory_space=pltpu.SMEM)
F32 = jnp.float32
BF16 = jnp.bfloat16


def params(mib=56):
    return pltpu.CompilerParams(vmem_limit_bytes=mib * 2**20)


def shape(dims, dtype=F32):
    return jax.ShapeDtypeStruct(dims, dtype)


def cost(flops, nbytes):
    return pl.CostEstimate(flops=int(flops), bytes_accessed=int(nbytes), transcendentals=0)


def inverse(value):
    guess = pl.reciprocal(value, approx=True)
    return guess * (2.0 - value * guess)


def rough_inverse(value):
    return pl.reciprocal(value, approx=True)


def dot_nt(left, right):
    return lax.dot_general(left, right, (((1,), (1,)), ((), ())), preferred_element_type=F32)


def dot_nn(left, right):
    return lax.dot_general(left, right, (((1,), (0,)), ((), ())), preferred_element_type=F32)


def slot_kernel(home_ref, level_ref, column_ref, slot_ref, wanted_ref, *, height):
    devices = wanted_ref.shape[0]
    blocks = home_ref.shape[1]
    home = home_ref[...]
    onehot = lax.broadcasted_iota(jnp.int32, (devices, blocks), 0) == home
    onehot = jnp.where(onehot, 1.0, 0.0).astype(F32)
    onehot_bf = onehot.astype(BF16)
    earlier = lax.broadcasted_iota(jnp.int32, (blocks, blocks), 0) < lax.broadcasted_iota(
        jnp.int32, (blocks, blocks), 1
    )
    earlier = jnp.where(earlier, 1.0, 0.0).astype(BF16)
    before = dot_nn(onehot_bf, earlier)
    rank = jnp.sum(onehot * before, axis=0, keepdims=True)
    rank = jnp.minimum(rank, HB - 1.0)
    slot_ref[...] = home * HB + rank.astype(jnp.int32)
    chosen = lax.broadcasted_iota(jnp.int32, (HB, blocks), 0).astype(F32) == rank
    level = jnp.where(chosen, level_ref[...].astype(F32) + 1.0, 0.0).astype(BF16)
    column = jnp.where(chosen, column_ref[...].astype(F32), 0.0).astype(BF16)
    level = dot_nt(onehot_bf, level)
    column = dot_nt(onehot_bf, column)
    row = (level - 1.0) * float(height) + column
    wanted_ref[...] = jnp.where(level > 0.0, row, -1.0).astype(jnp.int32)


def primitive_kernel(flow_ref, prim_ref, z_low_ref, z_high_ref, y_low_ref, y_high_ref):
    depth, height = flow_ref.shape[1], flow_ref.shape[2]

    def slab(z, carry):
        first, second = flow_ref[0, z], flow_ref[1, z]
        density = first + second
        inv_density = inverse(density)
        mom = [flow_ref[2 + i, z] for i in range(3)]
        vel = [m * inv_density for m in mom]
        kinetic = 0.5 * (mom[0] * vel[0] + mom[1] * vel[1] + mom[2] * vel[2])
        fraction = flow_ref[6, z]
        stiffness = stiff_base + stiff_slope * fraction
        pressure = (flow_ref[5, z] - kinetic - offset_slope * fraction) * inverse(stiffness)
        for i, value in enumerate([first, second] + vel + [pressure, fraction]):
            prim_ref[i, z] = value
            for j in range(3):
                y_low_ref[i, j, pl.ds(z, 1), :] = value[j : j + 1]
                y_high_ref[i, j, pl.ds(z, 1), :] = value[height - 3 + j : height - 2 + j]
        return carry

    lax.fori_loop(0, depth, slab, 0)
    for i in range(7):
        for j in range(3):
            z_low_ref[i, j] = prim_ref[i, j]
            z_high_ref[i, j] = prim_ref[i, depth - 3 + j]


def weno_pair(cell, dm2, dm1, d0, dp1, zm, z0, zp):
    qm = dm1 + d0
    ql = 3.0 * dm1 - dm2
    qh = dp1 - 3.0 * d0
    tl = zm + ql * ql
    tm = z0 + qm * qm
    th = zp + qh * qh
    tl = tl * tl
    tm = tm * tm
    th = th * th
    low = tm * th
    mid = 6.0 * (tl * th)
    high = tl * tm
    low3 = 3.0 * low
    high3 = 3.0 * high
    den_up = 6.0 * (low + mid + high3)
    den_down = 6.0 * (low3 + mid + high)
    num_up = low * (2.0 * ql - dm1) + mid * (qm + d0) + high3 * (d0 - qh)
    num_down = low3 * (ql + dm1) + mid * (qm + dm1) - high * (2.0 * qh + d0)
    return cell + num_up * rough_inverse(den_up), cell - num_down * rough_inverse(den_down)


def curvature(step):
    return (13.0 / 3.0) * (step * step) + 4.0 * weno_eps


def sound_terms(state):
    density = state[0] + state[1]
    stiff_one = (stiff_base + 1.0) + stiff_slope * state[6]
    enthalpy = state[5] * stiff_one + offset_slope * state[6]
    sound = enthalpy * lax.rsqrt(enthalpy * ((stiff_one - 1.0) * density))
    return density, enthalpy, sound


def hllc(left, right, normal):
    density_l, enthalpy_l, sound_l = sound_terms(left)
    density_r, enthalpy_r, sound_r = sound_terms(right)
    speed_l, speed_r = left[2 + normal], right[2 + normal]
    wave_l = jnp.minimum(speed_l - sound_l, speed_r - sound_r)
    wave_r = jnp.maximum(speed_l + sound_l, speed_r + sound_r)
    mass_l = density_l * (wave_l - speed_l)
    mass_r = density_r * (wave_r - speed_r)
    middle = (right[5] - left[5] + mass_l * speed_l - mass_r * speed_r) * inverse(mass_l - mass_r)
    forward = middle >= 0.0
    use_left = (wave_l >= 0.0) | forward
    one = [jnp.where(use_left, a, b) for a, b in zip(left[:6], right[:6])]
    density = jnp.where(use_left, density_l, density_r)
    enthalpy = jnp.where(use_left, enthalpy_l, enthalpy_r)
    wave = jnp.where(use_left, jnp.minimum(wave_l, 0.0), jnp.maximum(wave_r, 0.0))
    speed, pressure = one[2 + normal], one[5]
    ratio = jnp.where(wave != 0.0, wave * inverse(wave - middle), 0.0)
    extra = ratio * (middle - speed)
    carried = speed + extra
    push = density * (extra * (wave - speed))
    mass = density * carried
    kinetic = 0.5 * density * (one[2] * one[2] + one[3] * one[3] + one[4] * one[4])
    flux = [one[0] * carried, one[1] * carried]
    for i in range(3):
        flow = mass * one[2 + i]
        flux.append(flow + (push + pressure) if i == normal else flow)
    flux.append((enthalpy + kinetic) * carried + push * middle)
    flux.append(middle * jnp.where(forward, left[6], right[6]))
    return flux, middle


def x_kernel(prim_ref, change_ref, left_ref, right_ref):
    depth, height, length = prim_ref.shape[1:]

    def slab(z, carry):
        for i in range(7):
            cell = prim_ref[i, z]
            d0 = pltpu.roll(cell, length - 1, 1) - cell
            dm1 = pltpu.roll(d0, 1, 1)
            dm2 = pltpu.roll(d0, 2, 1)
            dp1 = pltpu.roll(d0, length - 1, 1)
            z0 = curvature(d0 - dm1)
            zm = pltpu.roll(z0, 1, 1)
            zp = pltpu.roll(z0, length - 1, 1)
            up, down = weno_pair(cell, dm2, dm1, d0, dp1, zm, z0, zp)
            left_ref[i] = up
            right_ref[i] = pltpu.roll(down, length - 1, 1)
        for part in range(height // 16):
            rows = pl.ds(16 * part, 16)
            left = [left_ref[i, rows] for i in range(7)]
            right = [right_ref[i, rows] for i in range(7)]
            flux, middle = hllc(left, right, 0)
            for i in range(6):
                change_ref[i, z, rows] = pltpu.roll(flux[i], 1, 1) - flux[i]
            fraction = prim_ref[6, z, rows]
            change_ref[6, z, rows] = (pltpu.roll(flux[6], 1, 1) - flux[6]) + fraction * (
                middle - pltpu.roll(middle, 1, 1)
            )
        return carry

    lax.fori_loop(0, depth, slab, 0)


def row_sweep(cells_ref, step_ref, curve_ref, left_ref, right_ref, flux_ref, stride, first, last, normal):
    def chunk_of(begin, end, size):
        count = -(-(end - begin) // size)
        return count, lambda k: pl.multiple_of(begin + k * size, 8)

    size = 32
    begin = first - 2 * stride if stride % 8 == 0 else first - 8
    count, at = chunk_of(begin, last + 2 * stride, size)

    for i in range(7):

        def prepare(k, carry, i=i):
            row = at(k)
            mid = cells_ref[i, pl.ds(row, size)]
            d0 = cells_ref[i, pl.ds(row + stride, size)] - mid
            dm1 = mid - cells_ref[i, pl.ds(row - stride, size)]
            step_ref[pl.ds(row, size)] = d0
            curve_ref[pl.ds(row, size)] = curvature(d0 - dm1)
            return carry

        if stride % 8 == 0:
            edge = pl.ds(first - 3 * stride, size)
            step_ref[edge] = cells_ref[i, pl.ds(first - 2 * stride, size)] - cells_ref[i, edge]
        lax.fori_loop(0, count, prepare, 0)

        begin_b = first - stride if stride % 8 == 0 else first - 8
        count_b, at_b = chunk_of(begin_b, last + stride, size)

        def states(k, carry, i=i, at_b=at_b):
            row = at_b(k)

            def take(ref, shift):
                return ref[pl.ds(row + shift * stride, size)]

            up, down = weno_pair(
                cells_ref[i, pl.ds(row, size)],
                take(step_ref, -2), take(step_ref, -1), take(step_ref, 0), take(step_ref, 1),
                take(curve_ref, -1), take(curve_ref, 0), take(curve_ref, 1),
            )
            left_ref[i, pl.ds(row, size)] = up
            right_ref[i, pl.ds(row, size)] = down
            return carry

        lax.fori_loop(0, count_b, states, 0)

    begin_c = first - stride if stride % 8 == 0 else first - 8
    count_c, at_c = chunk_of(begin_c, last, 16)

    def faces(k, carry):
        row = at_c(k)
        left = [left_ref[i, pl.ds(row, 16)] for i in range(7)]
        right = [right_ref[i, pl.ds(row + stride, 16)] for i in range(7)]
        flux, middle = hllc(left, right, normal)
        for i in range(7):
            flux_ref[i, pl.ds(row, 16)] = flux[i]
        flux_ref[7, pl.ds(row, 16)] = middle
        return carry

    lax.fori_loop(0, count_c, faces, 0)


def y_kernel(prim_ref, low_ref, high_ref, before_ref, change_ref, cells_ref, step_ref, curve_ref, left_ref, right_ref, flux_ref):
    depth, height = prim_ref.shape[1:3]
    pitch = height + 8
    first = 16

    def fill(z, carry):
        base = pl.multiple_of(first + z * pitch, 8)
        for i in range(7):
            cells_ref[i, pl.ds(base, height)] = prim_ref[i, z]
            for j in range(3):
                cells_ref[i, pl.ds(base - 3 + j, 1)] = low_ref[i, j, pl.ds(z, 1), :]
                cells_ref[i, pl.ds(base + height + j, 1)] = high_ref[i, j, pl.ds(z, 1), :]
        return carry

    lax.fori_loop(0, depth, fill, 0)
    row_sweep(cells_ref, step_ref, curve_ref, left_ref, right_ref, flux_ref, 1, first, first + depth * pitch, 1)

    def gather(z, carry):
        base = pl.multiple_of(first + z * pitch, 8)
        here, below = pl.ds(base, height), pl.ds(base - 1, height)
        for i in range(6):
            change_ref[i, z] = before_ref[i, z] + (flux_ref[i, below] - flux_ref[i, here])
        change_ref[6, z] = before_ref[6, z] + (
            (flux_ref[6, below] - flux_ref[6, here])
            + prim_ref[6, z] * (flux_ref[7, here] - flux_ref[7, below])
        )
        return carry

    lax.fori_loop(0, depth, gather, 0)


def z_kernel(prim_ref, low_ref, high_ref, before_ref, flow_ref, source_ref, next_ref, cells_ref, step_ref, curve_ref, left_ref, right_ref, flux_ref):
    depth, height = prim_ref.shape[1:3]
    first = 3 * height
    for i in range(7):
        for j in range(3):
            cells_ref[i, pl.ds(j * height, height)] = low_ref[i, j]
            cells_ref[i, pl.ds((depth + 3 + j) * height, height)] = high_ref[i, j]

    def fill(z, carry):
        base = pl.multiple_of(first + z * height, 8)
        for i in range(7):
            cells_ref[i, pl.ds(base, height)] = prim_ref[i, z]
        return carry

    lax.fori_loop(0, depth, fill, 0)
    row_sweep(cells_ref, step_ref, curve_ref, left_ref, right_ref, flux_ref, height, first, first + depth * height, 2)

    def update(z, carry):
        base = pl.multiple_of(first + z * height, 8)
        here, below = pl.ds(base, height), pl.ds(base - height, height)
        for i in range(7):
            change = before_ref[i, z] + (flux_ref[i, below] - flux_ref[i, here])
            if i == 6:
                change = change + prim_ref[6, z] * (flux_ref[7, here] - flux_ref[7, below])
                change = change - source_ref[z]
            next_ref[i, z] = flow_ref[i, z] + time_step * change
        return carry

    lax.fori_loop(0, depth, update, 0)


def serve_kernel(asked_ref, pressure_ref, served_ref):
    sources = asked_ref.shape[0]
    height = pressure_ref.shape[1]

    def one(src, carry):
        for r in range(HB):
            row = jnp.maximum(asked_ref[src, r], 0)
            level = row // height
            column = row % height
            slot = src * HB + r
            served_ref[slot, pl.ds(0, 2), :] = pressure_ref[level, pl.ds(column, 2), :]
            served_ref[slot, pl.ds(2, 2), :] = pressure_ref[level + 1, pl.ds(column, 2), :]
        return carry

    lax.fori_loop(0, sources, one, 0)


def scatter_kernel(asked_ref, returned_ref, source_ref, *sums):
    sources = asked_ref.shape[0]
    depth, height, length = source_ref.shape

    def clear(z, carry):
        for total in sums:
            total[pl.ds(pl.multiple_of(z * height, 8), height)] = jnp.zeros((height, length), F32)
        return carry

    lax.fori_loop(0, depth, clear, 0)

    def one(src, carry):
        for r in range(HB):
            total = sums[r % len(sums)]
            row = asked_ref[src, r]
            row = jnp.where(row < 0, depth * height, row)
            slot = src * HB + r
            near, far = pl.ds(row, 2), pl.ds(row + height, 2)
            total[near] = total[near] + returned_ref[slot, pl.ds(0, 2), :]
            total[far] = total[far] + returned_ref[slot, pl.ds(2, 2), :]
        return carry

    lax.fori_loop(0, sources, one, 0)

    def collect(z, carry):
        rows = pl.ds(pl.multiple_of(z * height, 8), height)
        value = sums[0][rows]
        for total in sums[1:]:
            value = value + total[rows]
        source_ref[z] = value
        return carry

    lax.fori_loop(0, depth, collect, 0)


def block_weights(place_ref, block, length):
    lateral = lax.broadcasted_iota(jnp.int32, (8, 128), 0) % 4
    shift_z = (lateral // 2).astype(F32) - place_ref[0, pl.ds(block, 1), :]
    shift_y = (lateral % 2).astype(F32) - place_ref[1, pl.ds(block, 1), :]
    across = jnp.exp(-0.5 * (shift_z * shift_z + shift_y * shift_y))
    across_sum = 0.5 * jnp.sum(across, axis=0, keepdims=True)
    offset = place_ref[2, pl.ds(block, 1), :] * float(length - 1)
    shift_x = lax.broadcasted_iota(jnp.int32, (length, 128), 0).astype(F32) - offset
    along = jnp.exp(-0.5 * (shift_x * shift_x))
    return across, across_sum, along


def deposit_kernel(slot_ref, place_ref, radius_ref, speed_ref, out_ref):
    length = out_ref.shape[2]
    upper = lax.broadcasted_iota(jnp.int32, (8, 128), 0) < 4

    def one(block):
        across, across_sum, along = block_weights(place_ref, block, length)
        along_sum = jnp.sum(along, axis=0, keepdims=True)
        radius = radius_ref[pl.ds(block, 1), :]
        rate = 4.0 * math.pi * radius * radius * speed_ref[pl.ds(block, 1), :]
        share = across * (rate * inverse(across_sum * along_sum))
        along_hi = along.astype(BF16)
        along_lo = (along - along_hi.astype(F32)).astype(BF16)
        share_hi = share.astype(BF16).astype(F32)
        both = jnp.where(upper, share_hi, share - share_hi).astype(BF16)
        only = jnp.where(upper, share_hi, 0.0).astype(BF16)
        result = dot_nt(both, along_hi) + dot_nt(only, along_lo)
        out_ref[slot_ref[0, block]] = result[0:4] + result[4:8]

    def several(k, carry):
        for j in range(4):
            one(k * 4 + j)
        return carry

    lax.fori_loop(0, radius_ref.shape[0] // 4, several, 0)


def sample_kernel(slot_ref, place_ref, radius_ref, speed_ref, rest_ref, rows_ref, motion_ref, sampled_ref):
    length = rows_ref.shape[2]
    upper = lax.broadcasted_iota(jnp.int32, (8, 128), 0) < 4

    def one(block):
        across, across_sum, along = block_weights(place_ref, block, length)
        value = rows_ref[slot_ref[0, block]] - pressure_mid
        value = jnp.concatenate([value, value], axis=0)
        high = value.astype(BF16).astype(F32)
        both = jnp.where(upper, high, value - high)
        both = jnp.concatenate([both, jnp.ones_like(both)], axis=0).astype(BF16)
        result = dot_nn(both, along.astype(BF16))
        total = jnp.sum(across * result[0:8], axis=0, keepdims=True)
        sampled_ref[pl.ds(block, 1), :] = pressure_mid + total * inverse(across_sum * result[8:9])

    def several(k, carry):
        for j in range(4):
            one(k * 4 + j)
        return carry

    lax.fori_loop(0, radius_ref.shape[0] // 4, several, 0)

    radius, speed, ratio = radius_ref[...], speed_ref[...], rest_ref[...]
    inv_radius = 1.0 / radius
    gas = (1.0 + 2.0 * surface_tension / (ratio * radius)) * jnp.exp(3.0 * polytropic * jnp.log(ratio))
    wall = gas - (2.0 * surface_tension + 4.0 * liquid_viscosity * speed) * inv_radius
    gas_rate = -3.0 * polytropic * gas * speed * inv_radius
    mach = speed / liquid_sound
    acceleration = (
        (1.0 + mach) * (wall - sampled_ref[...])
        + radius * gas_rate / liquid_sound
        - 1.5 * (1.0 - mach / 3.0) * speed * speed
    ) / ((1.0 - mach) * radius)
    motion_ref[0] = radius + time_step * speed
    motion_ref[1] = speed + time_step * acceleration


def shift_both(low_layers, high_layers, axis):
    count = lax.axis_size(axis)
    below = lax.ppermute(high_layers, axis, [(i, (i + 1) % count) for i in range(count)])
    above = lax.ppermute(low_layers, axis, [((i + 1) % count, i) for i in range(count)])
    return below, above


def exchange(values):
    return lax.all_to_all(values, ("gz", "gy"), split_axis=0, concat_axis=0, tiled=True)


def body(flow_state, block_tiles, bubble_place, bubble_radius, bubble_speed, rest_ratio):
    _, depth, height, length = flow_state.shape
    across_gy = lax.axis_size("gy")
    devices = lax.axis_size("gz") * across_gy
    blocks = block_tiles.shape[0]
    slots = devices * HB
    full_height = height * across_gy
    field = (7, depth, height, length)
    field_bytes = 4 * 7 * depth * height * length
    cells = depth * height * length

    anchor = block_tiles[:, 0].reshape(1, blocks)
    level, column = anchor // full_height, anchor % full_height
    home = level // depth * across_gy + column // height
    slot, wanted = pl.pallas_call(
        functools.partial(slot_kernel, height=height),
        out_shape=(shape((1, blocks), jnp.int32), shape((devices, HB), jnp.int32)),
        in_specs=[VMEM] * 3,
        out_specs=(VMEM, VMEM),
        cost_estimate=cost(1e6, 1e5),
        name="slots",
    )(home, level % depth, column % height)
    asked = exchange(wanted)

    prim, z_low, z_high, y_low, y_high = pl.pallas_call(
        primitive_kernel,
        out_shape=(
            shape(field),
            shape((7, 3, height, length)),
            shape((7, 3, height, length)),
            shape((7, 3, depth, length)),
            shape((7, 3, depth, length)),
        ),
        in_specs=[VMEM],
        out_specs=(VMEM,) * 5,
        compiler_params=params(),
        cost_estimate=cost(cells * 40, 2.5 * field_bytes),
        name="primitives",
    )(flow_state)
    z_below, z_above = shift_both(z_low, z_high, "gz")
    y_below, y_above = shift_both(y_low, y_high, "gy")

    outgoing = pl.pallas_call(
        deposit_kernel,
        out_shape=shape((slots, 4, length)),
        in_specs=[SMEM, VMEM, VMEM, VMEM],
        out_specs=VMEM,
        compiler_params=params(),
        cost_estimate=cost(2e9, 3e6),
        name="deposit",
    )(slot, bubble_place, bubble_radius, bubble_speed)
    returned = exchange(outgoing)

    served = pl.pallas_call(
        serve_kernel,
        out_shape=shape((slots, 4, length)),
        in_specs=[SMEM, VMEM],
        out_specs=VMEM,
        compiler_params=params(),
        cost_estimate=cost(1e6, 3e6),
        name="serve",
    )(asked, prim[5])
    fetched = exchange(served)

    change_x = pl.pallas_call(
        x_kernel,
        out_shape=shape(field),
        in_specs=[VMEM],
        out_specs=VMEM,
        scratch_shapes=[pltpu.VMEM((7, height, length), F32)] * 2,
        compiler_params=params(),
        cost_estimate=cost(cells * 600, 2 * field_bytes),
        name="sweep_x",
    )(prim)

    def scratch(rows):
        return [
            pltpu.VMEM((7, rows, length), F32),
            pltpu.VMEM((rows, length), F32),
            pltpu.VMEM((rows, length), F32),
            pltpu.VMEM((7, rows, length), F32),
            pltpu.VMEM((7, rows, length), F32),
            pltpu.VMEM((8, rows, length), F32),
        ]

    change_xy = pl.pallas_call(
        y_kernel,
        out_shape=shape(field),
        in_specs=[VMEM] * 4,
        out_specs=VMEM,
        scratch_shapes=scratch(16 + depth * (height + 8) + 56),
        compiler_params=params(),
        cost_estimate=cost(cells * 600, 3 * field_bytes),
        name="sweep_y",
    )(prim, y_below, y_above, change_x)

    source = pl.pallas_call(
        scatter_kernel,
        out_shape=shape((depth, height, length)),
        in_specs=[SMEM, VMEM],
        out_specs=VMEM,
        scratch_shapes=[pltpu.VMEM(((depth + 2) * height, length), F32)] * 4,
        compiler_params=params(),
        cost_estimate=cost(1e6, 3e6),
        name="scatter",
    )(asked, returned)

    state_next = pl.pallas_call(
        z_kernel,
        out_shape=shape(field),
        in_specs=[VMEM] * 6,
        out_specs=VMEM,
        scratch_shapes=scratch((depth + 6) * height),
        compiler_params=params(),
        cost_estimate=cost(cells * 600, 4 * field_bytes),
        name="sweep_z",
    )(prim, z_below, z_above, change_xy, flow_state, source)

    motion = pl.pallas_call(
        sample_kernel,
        out_shape=shape((2, blocks, 128)),
        in_specs=[SMEM] + [VMEM] * 5,
        out_specs=VMEM,
        scratch_shapes=[pltpu.VMEM((blocks, 128), F32)],
        compiler_params=params(),
        cost_estimate=cost(2e9, 4e6),
        name="sample",
    )(slot, bubble_place, bubble_radius, bubble_speed, rest_ratio, fetched)
    return state_next, source, motion


def solution(mesh):
    in_specs = (
        P(None, "gz", "gy", None),
        P(("gz", "gy"), None),
        P(None, ("gz", "gy"), None),
        P(("gz", "gy"), None),
        P(("gz", "gy"), None),
        P(("gz", "gy"), None),
    )
    out_specs = (P(None, "gz", "gy", None), P("gz", "gy", None), P(None, ("gz", "gy"), None))
    return jax.shard_map(body, mesh=mesh, in_specs=in_specs, out_specs=out_specs, check_vma=False)
```

time: 409 us -> 175 us (0.43); the launches traced: 402 us -> 174 us
  other arithmetic: 208 us -> 3.12 us
  Pallas kernels: 0 us -> 108 us
  local copies, waits for them, and re-layouts: 76.1 us -> 4.66 us
  matrix products: 57.6 us -> 0 us
  waiting for transfers between devices: 22.6 us -> 27.1 us
  starting transfers between devices: 35.6 us -> 31.2 us
    pallas_call x0 -> x9, Pallas kernels: none -> 108 us  [the longest x1 21.1 us: body(): pl.pallas_call(deposit_kernel, out_shape=shape((slots, 4, length)), in_sp...]
    div x13 -> x0, other arithmetic: 63 us -> none  [the longest x3 55.5 us: weno_side(): (weight_low * guess_low + weight_mid * guess_mid + weight_high * guess_hi...]
    dot_general x16 -> x0, matrix products: 57.6 us -> none  [the longest x8 35.6 us: bubble_block(): rowwise = jnp.einsum('gbx,gkx->gbk', along, row_tiles, precision=highest)]
    scatter x3 -> x0, local copies, waits for them, and re-layouts: 37.7 us -> none  [the longest x1 26 us: body(): outgoing = jnp.zeros((devices, HB, 4, length), jnp.float32).at[owner_home...]
    scatter-add x1 -> x0, other arithmetic: 29.2 us -> none  [body(): source_rows = jnp.zeros((slab_depth * height, length), jnp.float32).at[sa...]
    add x18 -> x1, other arithmetic: 26.4 us -> 0.59 us  [body(): home = level // depth * across_gy + column // height]
    select_n x6 -> x2, other arithmetic: 24.5 us -> 2.53 us  [the longest x1 1.27 us: body(): column % height]
    gather x2 -> x0, local copies, waits for them, and re-layouts: 17.8 us -> none  [the longest x1 14.2 us: body(): served = jnp.where(present[..., None], pressure_rows[safe_rows], 0.0)]
  transfers between devices with their start and end apart: 7 -> 7, of which waited for: 2 -> 2; matrix products, arithmetic and copies ran while one was open for 42% -> 1% of each run, Pallas kernels for 0% -> 52%
where the time goes in v1:
time: 175 us; the launch traced here: 174 us
  Pallas kernels  108 us (62%)
  starting transfers between devices  31.2 us (18%)
  waiting for transfers between devices  27.1 us (15%)
  local copies, waits for them, and re-layouts  4.66 us (3%)
  other arithmetic  3.12 us (2%)
    all_to_all x3, starting transfers between devices, exchange(): lax.all_to_all(values, ('gz', 'gy'), split_axis=0, concat_axis=0, tiled=T...  26.1 us
    pallas_call x1, Pallas kernels, body(): pl.pallas_call(deposit_kernel, out_shape=shape((slots, 4, length)), in_sp...  21.1 us
    pallas_call x1, Pallas kernels, body(): pl.pallas_call(y_kernel, out_shape=shape(field), in_specs=[VMEM] * 4, out...  19 us
    pallas_call x1, Pallas kernels, body(): pl.pallas_call(z_kernel, out_shape=shape(field), in_specs=[VMEM] * 6, out...  17.6 us
    all_to_all x3, waiting for transfers between devices, exchange(): lax.all_to_all(values, ('gz', 'gy'), split_axis=0, concat_axis=0, tiled=T...  16.6 us
    pallas_call x1, Pallas kernels, body(): pl.pallas_call(x_kernel, out_shape=shape(field), in_specs=[VMEM], out_spe...  15.8 us
    pallas_call x1, Pallas kernels, body(): pl.pallas_call(sample_kernel, out_shape=shape((2, blocks, 128)), in_specs...  15 us
    ppermute x2, waiting for transfers between devices, shift_both(): lax.ppermute(high_layers, axis, [(i, (i + 1) % count) for i in range(coun...  10.5 us
  transfers between devices with their start and end apart: 7, of which 2 were waited for; matrix products, arithmetic and copies ran while one was open for 1% of the time, Pallas kernels for 52%

profile of v1, /device:TPU:1, one launch (start us, length us, event | category | flops | bytes accessed | tf_op | source)
XLA Modules:
  0.0 174.3 jit_solution(5353197239011827935)
XLA Ops:
  0.6 1.3 and_select_fusion
  1.9 1.3 and_select_fusion.1
  3.2 0.6 multiply_add_fusion.home_ref
  3.8 1.7 slots.1
  5.5 11.5 %all-to-all-start = ((s32[128,1,8]{2,1,0:T(1,128)}), s32[128,1,8]{2,1,0:T(1,128)S(1)}, u32[]{:S(2)}, u32[]{:S(2)}) async-start(s32[128,1,8]{2,1,0:T(1,128)} %bitcast.21), calls=%async_computation | async-start | bytes 131072 | tf_op jit(solution)/shard_map/all_to_all | solution.py:467
  17.0 21.1 %deposit.1 = f32[1024,4,128]{2,1,0:T(4,128)} custom-call(s32[1,256]{1,0:T(1,128)} %get-tuple-element.16.slot_ref, f32[3,256,128]{2,1,0:T(8,128)} %place_ref.3, f32[256,128]{1,0:T(8,128)} %radius_ref.3, f32[256,128]{1,0:T(8,128)} %speed_ref.3), custom_call_target="tpu_custom_call" | custom-call | flops 2000000000 | bytes 3000000 | tf_op jit(solution)/shard_map/deposit/pallas_call | solution.py:512
  38.0 0.0 all-to-all-done
  38.0 0.0 copy-start.1
  38.0 9.8 %all-to-all-start.1 = ((f32[1024,4,128]{2,1,0:T(4,128)}), f32[1024,4,128]{2,1,0:T(4,128)S(1)}, u32[]{:S(2)}, u32[]{:S(2)}) async-start(f32[1024,4,128]{2,1,0:T(4,128)} %deposit.1), calls=%async_computation.1 | async-start | bytes 4194304 | tf_op jit(solution)/shard_map/all_to_all | solution.py:467
  47.8 4.3 %primitives.1 = (f32[7,24,32,128]{3,2,1,0:T(8,128)}, f32[7,3,32,128]{3,2,1,0:T(8,128)}, f32[7,3,32,128]{3,2,1,0:T(8,128)}, f32[7,3,24,128]{3,2,1,0:T(8,128)}, f32[7,3,24,128]{3,2,1,0:T(8,128)}) custom-call(f32[7,24,32,128]{3,2,1,0:T(8,128)} %flow_ref.3), custom_call_target="tpu_custom_call" | custom-call | flops 3932160 | bytes 6881280 | tf_op jit(solution)/shard_map/primitives/pallas_call | solution.py:494
  52.1 0.0 copy-done.1
  52.1 1.8 %slice_bitcast_fusion.pressure_ref = f32[24,32,128]{2,1,0:T(8,128)} fusion(f32[7,24,32,128]{3,2,1,0:T(8,128)} %get-tuple-element.10.prim_ref), kind=kLoop, calls=%fused_computation | loop fusion | bytes 786432 | tf_op jit(solution)/shard_map/squeeze | solution.py:531
  53.9 0.0 copy-start.7
  53.9 0.0 copy-start.6
  53.9 0.0 copy-start.9
  53.9 0.0 copy-start.8
  53.9 7.9 %serve.1 = f32[1024,4,128]{2,1,0:T(4,128)} custom-call(s32[128,8]{1,0:T(8,128)} %bitcast.19, f32[24,32,128]{2,1,0:T(8,128)} %slice_bitcast_fusion.pressure_ref), custom_call_target="tpu_custom_call" | custom-call | flops 1000000 | bytes 3000000 | tf_op jit(solution)/shard_map/serve/pallas_call | solution.py:523
  61.8 16.6 %all-to-all-done.1.returned_ref = f32[1024,4,128]{2,1,0:T(4,128)S(1)} async-done(((f32[1024,4,128]{2,1,0:T(4,128)}), f32[1024,4,128]{2,1,0:T(4,128)S(1)}, u32[]{:S(2)}, u32[]{:S(2)}) %all-to-all-start.1) | async-done | bytes 2097184 | tf_op jit(solution)/shard_map/all_to_all | solution.py:467
  78.4 0.0 copy-start
  78.4 4.9 %all-to-all-start.2 = ((f32[1024,4,128]{2,1,0:T(4,128)}), f32[1024,4,128]{2,1,0:T(4,128)}, u32[]{:S(2)}, u32[]{:S(2)}) async-start(f32[1024,4,128]{2,1,0:T(4,128)} %serve.1), calls=%async_computation.2 | async-start | bytes 4194304 | tf_op jit(solution)/shard_map/all_to_all | solution.py:467
  83.2 0.0 copy-done.7
  83.2 1.7 collective-permute-start
  85.0 0.0 copy-done.6
  85.0 0.0 collective-permute-start.1
  85.0 0.0 copy-done.9
  85.0 1.5 collective-permute-start.2
  86.5 0.0 copy-done.8
  86.5 1.8 %collective-permute-start.3 = (f32[7,3,24,128]{3,2,1,0:T(8,128)S(1)}, f32[7,3,24,128]{3,2,1,0:T(8,128)S(1)}, u32[]{:S(2)}, u32[]{:S(2)}) collective-permute-start(f32[7,3,24,128]{3,2,1,0:T(8,128)S(1)} %copy-done.8), channel_id=1, source_target_pairs={{1,0},{2,1},{3,2},{0,3},{5,4},{6,5},{7,6},{4,7},{9,8},{10,9},{11,1... | collective-permute-start | bytes 774152 | tf_op jit(solution)/shard_map/ppermute | solution.py:462
  88.3 15.8 %sweep_x.1.before_ref = f32[7,24,32,128]{3,2,1,0:T(8,128)} custom-call(f32[7,24,32,128]{3,2,1,0:T(8,128)} %get-tuple-element.10.prim_ref), custom_call_target="tpu_custom_call" | custom-call | flops 58982400 | bytes 5505024 | tf_op jit(solution)/shard_map/sweep_x/pallas_call | solution.py:534
  104.1 0.0 copy-done
  104.1 10.5 %collective-permute-done.2.low_ref = f32[7,3,24,128]{3,2,1,0:T(8,128)S(1)} collective-permute-done((f32[7,3,24,128]{3,2,1,0:T(8,128)S(1)}, f32[7,3,24,128]{3,2,1,0:T(8,128)S(1)}, u32[]{:S(2)}, u32[]{:S(2)}) %collective-permute-start.2) | collective-permute-done | bytes 258080 | tf_op jit(solution)/shard_map/ppermute | solution.py:461
  114.7 0.0 copy-start.4
  114.7 0.0 collective-permute-done.3.high_ref
  114.7 0.7 copy-done.4
  115.4 0.0 copy-start.5
  115.4 0.7 copy-done.5
  116.1 19.0 %sweep_y.1.before_ref = f32[7,24,32,128]{3,2,1,0:T(8,128)} custom-call(f32[7,24,32,128]{3,2,1,0:T(8,128)} %get-tuple-element.10.prim_ref, f32[7,3,24,128]{3,2,1,0:T(8,128)} %copy-done.4, f32[7,3,24,128]{3,2,1,0:T(8,128)} %copy-done.5, f32[7,24,32,128]{3,2,1,0:T(8,128)} %sweep_x.1.before_ref), custom_call_target="tpu_custom_call" | custom-call | flops 58982400 | bytes 8257536 | tf_op jit(solution)/shard_map/sweep_y/pallas_call | solution.py:555
  135.1 5.2 %scatter.1.source_ref = f32[24,32,128]{2,1,0:T(8,128)} custom-call(s32[128,8]{1,0:T(8,128)} %bitcast.20, f32[1024,4,128]{2,1,0:T(4,128)} %copy-done), custom_call_target="tpu_custom_call" | custom-call | flops 1000000 | bytes 3000000 | tf_op jit(solution)/shard_map/scatter/pallas_call | solution.py:566
  140.3 0.0 collective-permute-done.low_ref
  140.3 0.0 copy-start.2
  140.3 0.0 collective-permute-done.1.high_ref
  140.3 0.7 copy-done.2
  141.0 0.0 copy-start.3
  141.0 0.8 copy-done.3
  141.7 17.6 %sweep_z.1 = f32[7,24,32,128]{3,2,1,0:T(8,128)} custom-call(f32[7,24,32,128]{3,2,1,0:T(8,128)} %get-tuple-element.10.prim_ref, f32[7,3,32,128]{3,2,1,0:T(8,128)} %copy-done.2, f32[7,3,32,128]{3,2,1,0:T(8,128)} %copy-done.3, f32[7,24,32,128]{3,2,1,0:T(8,128)} %sweep_y.1.before_ref, f32[7,24,32,128]{3,2,1,0:T(8,128)} %flow_ref.3, f32[24,32,128]{2,1,0:T(8,128)} %scatter.1.source_ref), custom_call_target="tpu_custom_call" | custom-call | flops 58982400 | bytes 11010048 | tf_op jit(solution)/shard_map/sweep_z/pallas_call | solution.py:577
  159.3 0.0 all-to-all-done.2.rows_ref
  159.3 15.0 %sample.1 = f32[2,256,128]{2,1,0:T(8,128)} custom-call(s32[1,256]{1,0:T(1,128)} %get-tuple-element.16.slot_ref, f32[3,256,128]{2,1,0:T(8,128)} %place_ref.3, f32[256,128]{1,0:T(8,128)} %radius_ref.3, f32[256,128]{1,0:T(8,128)} %speed_ref.3, f32[256,128]{1,0:T(8,128)} %rest_ref.1, f32[1024,4,128]{2,1,0:T(4,128)} %all-to-all-done.2.rows_ref), custom_call_target="tpu_custom_call" | custom-call | flops 2000000000 | bytes 4000000 | tf_op jit(solution)/shard_map/sample/pallas_call | solution.py:588
Async XLA Ops:
  5.5 32.6 %all-to-all-start = ((s32[128,1,8]{2,1,0:T(1,128)}), s32[128,1,8]{2,1,0:T(1,128)S(1)}, u32[]{:S(2)}, u32[]{:S(2)}) async-start(s32[128,1,8]{2,1,0:T(1,128)} %bitcast.21), calls=%async_computation | async-start | bytes 131072 | tf_op jit(solution)/shard_map/all_to_all | solution.py:467
  38.0 14.1 %copy-start.1 = (s32[128,1,8]{2,1,0:T(1,128)}, s32[128,1,8]{2,1,0:T(1,128)S(1)}, u32[]{:S(2)}) copy-start(s32[128,1,8]{2,1,0:T(1,128)S(1)} %all-to-all-done) | copy-start | bytes 12292
  38.0 40.3 %all-to-all-start.1 = ((f32[1024,4,128]{2,1,0:T(4,128)}), f32[1024,4,128]{2,1,0:T(4,128)S(1)}, u32[]{:S(2)}, u32[]{:S(2)}) async-start(f32[1024,4,128]{2,1,0:T(4,128)} %deposit.1), calls=%async_computation.1 | async-start | bytes 4194304 | tf_op jit(solution)/shard_map/all_to_all | solution.py:467
  53.9 29.3 %copy-start.7 = (f32[7,3,32,128]{3,2,1,0:T(8,128)S(1)}, f32[7,3,32,128]{3,2,1,0:T(8,128)}, u32[]{:S(2)}) copy-start(f32[7,3,32,128]{3,2,1,0:T(8,128)} %get-tuple-element.11) | copy-start | bytes 1032196
  53.9 31.1 %copy-start.6 = (f32[7,3,32,128]{3,2,1,0:T(8,128)S(1)}, f32[7,3,32,128]{3,2,1,0:T(8,128)}, u32[]{:S(2)}) copy-start(f32[7,3,32,128]{3,2,1,0:T(8,128)} %get-tuple-element.12) | copy-start | bytes 1032196
  53.9 31.1 %copy-start.9 = (f32[7,3,24,128]{3,2,1,0:T(8,128)S(1)}, f32[7,3,24,128]{3,2,1,0:T(8,128)}, u32[]{:S(2)}) copy-start(f32[7,3,24,128]{3,2,1,0:T(8,128)} %get-tuple-element.13) | copy-start | bytes 774148
  53.9 32.6 %copy-start.8 = (f32[7,3,24,128]{3,2,1,0:T(8,128)S(1)}, f32[7,3,24,128]{3,2,1,0:T(8,128)}, u32[]{:S(2)}) copy-start(f32[7,3,24,128]{3,2,1,0:T(8,128)} %get-tuple-element.14) | copy-start | bytes 774148
  78.4 25.8 %copy-start = (f32[1024,4,128]{2,1,0:T(4,128)}, f32[1024,4,128]{2,1,0:T(4,128)S(1)}, u32[]{:S(2)}) copy-start(f32[1024,4,128]{2,1,0:T(4,128)S(1)} %all-to-all-done.1.returned_ref) | copy-start | bytes 6291460
  78.4 80.9 %all-to-all-start.2 = ((f32[1024,4,128]{2,1,0:T(4,128)}), f32[1024,4,128]{2,1,0:T(4,128)}, u32[]{:S(2)}, u32[]{:S(2)}) async-start(f32[1024,4,128]{2,1,0:T(4,128)} %serve.1), calls=%async_computation.2 | async-start | bytes 4194304 | tf_op jit(solution)/shard_map/all_to_all | solution.py:467
  83.2 57.0 %collective-permute-start = (f32[7,3,32,128]{3,2,1,0:T(8,128)S(1)}, f32[7,3,32,128]{3,2,1,0:T(8,128)S(1)}, u32[]{:S(2)}, u32[]{:S(2)}) collective-permute-start(f32[7,3,32,128]{3,2,1,0:T(8,128)S(1)} %copy-done.7), channel_id=1, source_target_pairs={{0,4},{4,8},{8,12},{12,16},{16,20},{20,24},{24,28},{28,32},{32,36}... | collective-permute-start | bytes 1032200 | tf_op jit(solution)/shard_map/ppermute | solution.py:461
  85.0 55.3 %collective-permute-start.1 = (f32[7,3,32,128]{3,2,1,0:T(8,128)S(1)}, f32[7,3,32,128]{3,2,1,0:T(8,128)S(1)}, u32[]{:S(2)}, u32[]{:S(2)}) collective-permute-start(f32[7,3,32,128]{3,2,1,0:T(8,128)S(1)} %copy-done.6), channel_id=1, source_target_pairs={{4,0},{8,4},{12,8},{16,12},{20,16},{24,20},{28,24},{32,28},{36,32}... | collective-permute-start | bytes 1032200 | tf_op jit(solution)/shard_map/ppermute | solution.py:462
  85.0 29.7 %collective-permute-start.2 = (f32[7,3,24,128]{3,2,1,0:T(8,128)S(1)}, f32[7,3,24,128]{3,2,1,0:T(8,128)S(1)}, u32[]{:S(2)}, u32[]{:S(2)}) collective-permute-start(f32[7,3,24,128]{3,2,1,0:T(8,128)S(1)} %copy-done.9), channel_id=1, source_target_pairs={{0,1},{1,2},{2,3},{3,0},{4,5},{5,6},{6,7},{7,4},{8,9},{9,10},{10,1... | collective-permute-start | bytes 774152 | tf_op jit(solution)/shard_map/ppermute | solution.py:461
  86.5 28.2 %collective-permute-start.3 = (f32[7,3,24,128]{3,2,1,0:T(8,128)S(1)}, f32[7,3,24,128]{3,2,1,0:T(8,128)S(1)}, u32[]{:S(2)}, u32[]{:S(2)}) collective-permute-start(f32[7,3,24,128]{3,2,1,0:T(8,128)S(1)} %copy-done.8), channel_id=1, source_target_pairs={{1,0},{2,1},{3,2},{0,3},{5,4},{6,5},{7,6},{4,7},{9,8},{10,9},{11,1... | collective-permute-start | bytes 774152 | tf_op jit(solution)/shard_map/ppermute | solution.py:462
  114.7 0.7 copy-start.4
  115.4 0.7 copy-start.5
  140.3 0.7 copy-start.2
  141.0 0.8 copy-start.3

commit v2 on v1

--- a/solution.py
+++ b/solution.py
@@ -37,8 +37,8 @@
     return jax.ShapeDtypeStruct(dims, dtype)
 
 
-def cost(flops, nbytes):
-    return pl.CostEstimate(flops=int(flops), bytes_accessed=int(nbytes), transcendentals=0)
+def cost(microseconds):
+    return pl.CostEstimate(flops=int(microseconds * 1.15e9), bytes_accessed=1000, transcendentals=0)
 
 
 def inverse(value):
@@ -58,10 +58,19 @@
     return lax.dot_general(left, right, (((1,), (0,)), ((), ())), preferred_element_type=F32)
 
 
-def slot_kernel(home_ref, level_ref, column_ref, slot_ref, wanted_ref, *, height):
+def slot_kernel(tiles_ref, slot_ref, wanted_ref, *, depth, height, across_gy):
     devices = wanted_ref.shape[0]
-    blocks = home_ref.shape[1]
-    home = home_ref[...]
+    blocks = tiles_ref.shape[1]
+    anchor = tiles_ref[0:1, :].astype(F32)
+
+    def split(value, size):
+        whole = jnp.floor((value + 0.5) * (1.0 / size))
+        return whole, value - whole * float(size)
+
+    level, column = split(anchor, height * across_gy)
+    home_z, level = split(level, depth)
+    home_y, column = split(column, height)
+    home = (home_z * float(across_gy) + home_y).astype(jnp.int32)
     onehot = lax.broadcasted_iota(jnp.int32, (devices, blocks), 0) == home
     onehot = jnp.where(onehot, 1.0, 0.0).astype(F32)
     onehot_bf = onehot.astype(BF16)
@@ -74,8 +83,8 @@
     rank = jnp.minimum(rank, HB - 1.0)
     slot_ref[...] = home * HB + rank.astype(jnp.int32)
     chosen = lax.broadcasted_iota(jnp.int32, (HB, blocks), 0).astype(F32) == rank
-    level = jnp.where(chosen, level_ref[...].astype(F32) + 1.0, 0.0).astype(BF16)
-    column = jnp.where(chosen, column_ref[...].astype(F32), 0.0).astype(BF16)
+    level = jnp.where(chosen, level + 1.0, 0.0).astype(BF16)
+    column = jnp.where(chosen, column, 0.0).astype(BF16)
     level = dot_nt(onehot_bf, level)
     column = dot_nt(onehot_bf, column)
     row = (level - 1.0) * float(height) + column
@@ -298,7 +307,7 @@
     lax.fori_loop(0, depth, gather, 0)
 
 
-def z_kernel(prim_ref, low_ref, high_ref, before_ref, flow_ref, source_ref, next_ref, cells_ref, step_ref, curve_ref, left_ref, right_ref, flux_ref):
+def z_kernel(prim_ref, low_ref, high_ref, before_ref, flow_ref, next_ref, cells_ref, step_ref, curve_ref, left_ref, right_ref, flux_ref):
     depth, height = prim_ref.shape[1:3]
     first = 3 * height
     for i in range(7):
@@ -322,33 +331,29 @@
             change = before_ref[i, z] + (flux_ref[i, below] - flux_ref[i, here])
             if i == 6:
                 change = change + prim_ref[6, z] * (flux_ref[7, here] - flux_ref[7, below])
-                change = change - source_ref[z]
             next_ref[i, z] = flow_ref[i, z] + time_step * change
         return carry
 
     lax.fori_loop(0, depth, update, 0)
 
 
-def serve_kernel(asked_ref, pressure_ref, served_ref):
-    sources = asked_ref.shape[0]
-    height = pressure_ref.shape[1]
-
+def serve_kernel(asked_ref, pressure_ref, served_ref, *, height):
     def one(src, carry):
         for r in range(HB):
             row = jnp.maximum(asked_ref[src, r], 0)
-            level = row // height
-            column = row % height
             slot = src * HB + r
-            served_ref[slot, pl.ds(0, 2), :] = pressure_ref[level, pl.ds(column, 2), :]
-            served_ref[slot, pl.ds(2, 2), :] = pressure_ref[level + 1, pl.ds(column, 2), :]
-        return carry
-
-    lax.fori_loop(0, sources, one, 0)
-
-
-def scatter_kernel(asked_ref, returned_ref, source_ref, *sums):
+            served_ref[slot, pl.ds(0, 2), :] = pressure_ref[0, pl.ds(row, 2), :]
+            served_ref[slot, pl.ds(2, 2), :] = pressure_ref[0, pl.ds(row + height, 2), :]
+        return carry
+
+    lax.fori_loop(0, asked_ref.shape[0], one, 0)
+
+
+def scatter_kernel(asked_ref, returned_ref, state_ref, source_ref, next_ref, fraction_ref, sem, *sums):
     sources = asked_ref.shape[0]
     depth, height, length = source_ref.shape
+    load = pltpu.make_async_copy(state_ref.at[6], fraction_ref, sem)
+    load.start()
 
     def clear(z, carry):
         for total in sums:
@@ -376,9 +381,14 @@
         for total in sums[1:]:
             value = value + total[rows]
         source_ref[z] = value
-        return carry
-
+        fraction_ref[z] = fraction_ref[z] - time_step * value
+        return carry
+
+    load.wait()
     lax.fori_loop(0, depth, collect, 0)
+    save = pltpu.make_async_copy(fraction_ref, next_ref.at[6], sem)
+    save.start()
+    save.wait()
 
 
 def block_weights(place_ref, block, length):
@@ -473,22 +483,16 @@
     devices = lax.axis_size("gz") * across_gy
     blocks = block_tiles.shape[0]
     slots = devices * HB
-    full_height = height * across_gy
     field = (7, depth, height, length)
-    field_bytes = 4 * 7 * depth * height * length
-    cells = depth * height * length
-
-    anchor = block_tiles[:, 0].reshape(1, blocks)
-    level, column = anchor // full_height, anchor % full_height
-    home = level // depth * across_gy + column // height
+
     slot, wanted = pl.pallas_call(
-        functools.partial(slot_kernel, height=height),
+        functools.partial(slot_kernel, depth=depth, height=height, across_gy=across_gy),
         out_shape=(shape((1, blocks), jnp.int32), shape((devices, HB), jnp.int32)),
-        in_specs=[VMEM] * 3,
+        in_specs=[VMEM],
         out_specs=(VMEM, VMEM),
-        cost_estimate=cost(1e6, 1e5),
+        cost_estimate=cost(2),
         name="slots",
-    )(home, level % depth, column % height)
+    )(block_tiles.T)
     asked = exchange(wanted)
 
     prim, z_low, z_high, y_low, y_high = pl.pallas_call(
@@ -503,11 +507,12 @@
         in_specs=[VMEM],
         out_specs=(VMEM,) * 5,
         compiler_params=params(),
-        cost_estimate=cost(cells * 40, 2.5 * field_bytes),
+        cost_estimate=cost(4),
         name="primitives",
     )(flow_state)
+    y_below, y_above = shift_both(y_low, y_high, "gy")
     z_below, z_above = shift_both(z_low, z_high, "gz")
-    y_below, y_above = shift_both(y_low, y_high, "gy")
+    slot, prim = lax.optimization_barrier((slot, prim))
 
     outgoing = pl.pallas_call(
         deposit_kernel,
@@ -515,20 +520,24 @@
         in_specs=[SMEM, VMEM, VMEM, VMEM],
         out_specs=VMEM,
         compiler_params=params(),
-        cost_estimate=cost(2e9, 3e6),
+        cost_estimate=cost(21),
         name="deposit",
     )(slot, bubble_place, bubble_radius, bubble_speed)
-    returned = exchange(outgoing)
-
+
+    rows = depth * height
+    asked, outgoing, y_below, y_above, z_below, z_above = lax.optimization_barrier(
+        (asked, outgoing, y_below, y_above, z_below, z_above)
+    )
     served = pl.pallas_call(
-        serve_kernel,
+        functools.partial(serve_kernel, height=height),
+        grid=(1,),
         out_shape=shape((slots, 4, length)),
-        in_specs=[SMEM, VMEM],
+        in_specs=[SMEM, pl.BlockSpec((1, rows, length), lambda i: (5, 0, 0))],
         out_specs=VMEM,
         compiler_params=params(),
-        cost_estimate=cost(1e6, 3e6),
+        cost_estimate=cost(5),
         name="serve",
-    )(asked, prim[5])
+    )(asked, prim.reshape(7, rows, length))
     fetched = exchange(served)
 
     change_x = pl.pallas_call(
@@ -538,7 +547,7 @@
         out_specs=VMEM,
         scratch_shapes=[pltpu.VMEM((7, height, length), F32)] * 2,
         compiler_params=params(),
-        cost_estimate=cost(cells * 600, 2 * field_bytes),
+        cost_estimate=cost(16),
         name="sweep_x",
     )(prim)
 
@@ -559,31 +568,23 @@
         out_specs=VMEM,
         scratch_shapes=scratch(16 + depth * (height + 8) + 56),
         compiler_params=params(),
-        cost_estimate=cost(cells * 600, 3 * field_bytes),
+        cost_estimate=cost(19),
         name="sweep_y",
     )(prim, y_below, y_above, change_x)
 
-    source = pl.pallas_call(
-        scatter_kernel,
-        out_shape=shape((depth, height, length)),
-        in_specs=[SMEM, VMEM],
-        out_specs=VMEM,
-        scratch_shapes=[pltpu.VMEM(((depth + 2) * height, length), F32)] * 4,
-        compiler_params=params(),
-        cost_estimate=cost(1e6, 3e6),
-        name="scatter",
-    )(asked, returned)
+    outgoing, fetched, change_xy = lax.optimization_barrier((outgoing, fetched, change_xy))
+    returned = exchange(outgoing)
 
     state_next = pl.pallas_call(
         z_kernel,
         out_shape=shape(field),
-        in_specs=[VMEM] * 6,
+        in_specs=[VMEM] * 5,
         out_specs=VMEM,
         scratch_shapes=scratch((depth + 6) * height),
         compiler_params=params(),
-        cost_estimate=cost(cells * 600, 4 * field_bytes),
+        cost_estimate=cost(17),
         name="sweep_z",
-    )(prim, z_below, z_above, change_xy, flow_state, source)
+    )(prim, z_below, z_above, change_xy, flow_state)
 
     motion = pl.pallas_call(
         sample_kernel,
@@ -592,9 +593,23 @@
         out_specs=VMEM,
         scratch_shapes=[pltpu.VMEM((blocks, 128), F32)],
         compiler_params=params(),
-        cost_estimate=cost(2e9, 4e6),
+        cost_estimate=cost(15),
         name="sample",
     )(slot, bubble_place, bubble_radius, bubble_speed, rest_ratio, fetched)
+
+    returned, state_next, motion = lax.optimization_barrier((returned, state_next, motion))
+    source, state_next = pl.pallas_call(
+        scatter_kernel,
+        out_shape=(shape((depth, height, length)), shape(field)),
+        in_specs=[SMEM, VMEM, pl.BlockSpec(memory_space=pl.ANY)],
+        out_specs=(VMEM, pl.BlockSpec(memory_space=pl.ANY)),
+        scratch_shapes=[pltpu.VMEM((depth, height, length), F32), pltpu.SemaphoreType.DMA]
+        + [pltpu.VMEM(((depth + 2) * height, length), F32)] * 4,
+        input_output_aliases={2: 1},
+        compiler_params=params(),
+        cost_estimate=cost(6),
+        name="scatter",
+    )(asked, returned, state_next)
     return state_next, source, motion
 
 

time: 175 us -> 143 us (0.82)
  waiting for transfers between devices: 27.1 us -> 0.02 us
  local copies, waits for them, and re-layouts: 4.66 us -> 0.56 us
  starting transfers between devices: 31.2 us -> 35.3 us
  other arithmetic: 3.12 us -> 0 us
  Pallas kernels: 108 us -> 105 us
    all_to_all x3, waiting for transfers between devices: 16.6 us -> 0.01 us  [exchange(): lax.all_to_all(values, ('gz', 'gy'), split_axis=0, concat_axis=0, tiled=T...]
    ppermute x2, waiting for transfers between devices: 10.5 us -> 0.01 us  [shift_both(): lax.ppermute(high_layers, axis, [(i, (i + 1) % count) for i in range(coun...]
    all_to_all x3, starting transfers between devices: 26.1 us -> 28.9 us  [exchange(): lax.all_to_all(values, ('gz', 'gy'), split_axis=0, concat_axis=0, tiled=T...]
    select_n x2 -> x0, other arithmetic: 2.53 us -> none  [the longest x1 1.27 us: body(): column % height]
    unnamed x20 -> x12, local copies, waits for them, and re-layouts: 2.89 us -> 0.56 us
    pallas_call x4, Pallas kernels: 32.4 us -> 30.3 us  [the longest x1 17.5 us: body(): pl.pallas_call(z_kernel, out_shape=shape(field), in_specs=[VMEM] * 5, out...]
    squeeze x1 -> x0, local copies, waits for them, and re-layouts: 1.77 us -> none  [body(): prim[5]]
  transfers between devices with their start and end apart: 7 -> 7, of which waited for: 2 -> 0; matrix products, arithmetic and copies ran while one was open for 1% -> 0% of each run, Pallas kernels for 52% -> 63%
where the time goes in v2:
time: 143 us; the launch traced here: 142 us
  Pallas kernels  105 us (73%)
  starting transfers between devices  35.3 us (25%)
    all_to_all x3, starting transfers between devices, exchange(): lax.all_to_all(values, ('gz', 'gy'), split_axis=0, concat_axis=0, tiled=T...  28.9 us
    pallas_call x1, Pallas kernels, body(): pl.pallas_call(deposit_kernel, out_shape=shape((slots, 4, length)), in_sp...  21.1 us
    pallas_call x1, Pallas kernels, body(): pl.pallas_call(y_kernel, out_shape=shape(field), in_specs=[VMEM] * 4, out...  19 us
    pallas_call x1, Pallas kernels, body(): pl.pallas_call(z_kernel, out_shape=shape(field), in_specs=[VMEM] * 5, out...  17.5 us
    pallas_call x1, Pallas kernels, body(): pl.pallas_call(x_kernel, out_shape=shape(field), in_specs=[VMEM], out_spe...  15.8 us
    pallas_call x1, Pallas kernels, body(): pl.pallas_call(sample_kernel, out_shape=shape((2, blocks, 128)), in_specs...  15 us
    pallas_call x1, Pallas kernels, body(): pl.pallas_call(scatter_kernel, out_shape=(shape((depth, height, length)),...  5.93 us
    pallas_call x1, Pallas kernels, body(): pl.pallas_call(functools.partial(serve_kernel, height=height), grid=(1,),...  5.17 us
  transfers between devices with their start and end apart: 7, of which 0 were waited for; matrix products, arithmetic and copies ran while one was open for 0% of the time, Pallas kernels for 63%

profile of v2, /device:TPU:1, one launch (start us, length us, event | category | flops | bytes accessed | tf_op | source)
XLA Modules:
  0.0 142.1 jit_solution(14067505962843991307)
XLA Ops:
  0.6 4.3 %primitives.1 = (f32[7,24,32,128]{3,2,1,0:T(8,128)}, f32[7,3,32,128]{3,2,1,0:T(8,128)}, f32[7,3,32,128]{3,2,1,0:T(8,128)}, f32[7,3,24,128]{3,2,1,0:T(8,128)}, f32[7,3,24,128]{3,2,1,0:T(8,128)}) custom-call(f32[7,24,32,128]{3,2,1,0:T(8,128)} %flow_ref.3), custom_call_target="tpu_custom_call" | custom-call | flops 4600000000 | bytes 1000 | tf_op jit(solution)/shard_map/primitives/pallas_call | solution.py:498
  4.9 2.6 %collective-permute-start.2 = (f32[7,3,32,128]{3,2,1,0:T(8,128)}, f32[7,3,32,128]{3,2,1,0:T(8,128)S(1)}, u32[]{:S(2)}, u32[]{:S(2)}) collective-permute-start(f32[7,3,32,128]{3,2,1,0:T(8,128)} %get-tuple-element.32), channel_id=1, source_target_pairs={{0,4},{4,8},{8,12},{12,16},{16,20},{20,24},{24,28},{28,32},{32,36}... | collective-permute-start | bytes 1032200 | tf_op jit(solution)/shard_map/ppermute | solution.py:471
  7.5 0.0 collective-permute-start.3
  7.5 1.6 %collective-permute-start = (f32[7,3,24,128]{3,2,1,0:T(8,128)}, f32[7,3,24,128]{3,2,1,0:T(8,128)S(1)}, u32[]{:S(2)}, u32[]{:S(2)}) collective-permute-start(f32[7,3,24,128]{3,2,1,0:T(8,128)} %get-tuple-element.30), channel_id=1, source_target_pairs={{0,1},{1,2},{2,3},{3,0},{4,5},{5,6},{6,7},{7,4},{8,9},{9,10},{10,1... | collective-permute-start | bytes 774152 | tf_op jit(solution)/shard_map/ppermute | solution.py:471
  9.2 2.1 %collective-permute-start.1 = (f32[7,3,24,128]{3,2,1,0:T(8,128)}, f32[7,3,24,128]{3,2,1,0:T(8,128)S(1)}, u32[]{:S(2)}, u32[]{:S(2)}) collective-permute-start(f32[7,3,24,128]{3,2,1,0:T(8,128)} %get-tuple-element.31), channel_id=1, source_target_pairs={{1,0},{2,1},{3,2},{0,3},{5,4},{6,5},{7,6},{4,7},{9,8},{10,9},{11,1... | collective-permute-start | bytes 774152 | tf_op jit(solution)/shard_map/ppermute | solution.py:472
  11.3 1.7 %slots.1 = (s32[1,256]{1,0:T(1,128)}, s32[128,8]{1,0:T(8,128)}) custom-call(s32[4,256]{1,0:T(4,128)} %bitcast.9), custom_call_target="tpu_custom_call" | custom-call | flops 2300000000 | bytes 1000 | tf_op jit(solution)/shard_map/slots/pallas_call | solution.py:488
  13.0 8.9 %all-to-all-start = ((s32[128,1,8]{2,1,0:T(1,128)}), s32[128,1,8]{2,1,0:T(1,128)S(1)}, u32[]{:S(2)}, u32[]{:S(2)}) async-start(s32[128,1,8]{2,1,0:T(1,128)} %bitcast.8), calls=%async_computation | async-start | bytes 131072 | tf_op jit(solution)/shard_map/all_to_all | solution.py:477
  21.9 21.1 %deposit.1 = f32[1024,4,128]{2,1,0:T(4,128)} custom-call(s32[1,256]{1,0:T(1,128)} %get-tuple-element.29.slot_ref, f32[3,256,128]{2,1,0:T(8,128)} %place_ref.3, f32[256,128]{1,0:T(8,128)} %radius_ref.3, f32[256,128]{1,0:T(8,128)} %speed_ref.3), custom_call_target="tpu_custom_call" | custom-call | flops 24149999616 | bytes 1000 | tf_op jit(solution)/shard_map/deposit/pallas_call | solution.py:517
  43.0 0.0 all-to-all-done
  43.0 0.0 copy-start.1
  43.0 0.0 collective-permute-done.low_ref
  43.0 0.0 copy-start.4
  43.0 0.0 collective-permute-done.1.high_ref
  43.0 0.0 copy-start.5
  43.0 0.0 collective-permute-done.2.low_ref
  43.0 0.0 copy-start.2
  43.0 0.0 collective-permute-done.3.high_ref
  43.0 0.0 copy-start.3
  43.1 0.5 copy-done.1
  43.6 5.2 %serve.1 = f32[1024,4,128]{2,1,0:T(4,128)} custom-call(s32[128,8]{1,0:T(8,128)} %bitcast.6, f32[7,768,128]{2,1,0:T(8,128)} %bitcast.10), custom_call_target="tpu_custom_call" | custom-call | flops 5750000128 | bytes 1000 | tf_op jit(solution)/shard_map/serve/pallas_call | solution.py:531
  48.8 0.0 copy-done.4
  48.8 0.0 copy-done.5
  48.8 0.0 copy-done.2
  48.8 0.0 copy-done.3
  48.8 9.8 %all-to-all-start.1 = ((f32[1024,4,128]{2,1,0:T(4,128)}), f32[1024,4,128]{2,1,0:T(4,128)S(1)}, u32[]{:S(2)}, u32[]{:S(2)}) async-start(f32[1024,4,128]{2,1,0:T(4,128)} %serve.1), calls=%async_computation.1 | async-start | bytes 4194304 | tf_op jit(solution)/shard_map/all_to_all | solution.py:477
  58.6 15.8 %sweep_x.1.before_ref = f32[7,24,32,128]{3,2,1,0:T(8,128)} custom-call(f32[7,24,32,128]{3,2,1,0:T(8,128)} %get-tuple-element.36.prim_ref), custom_call_target="tpu_custom_call" | custom-call | flops 18400000000 | bytes 1000 | tf_op jit(solution)/shard_map/sweep_x/pallas_call | solution.py:543
  74.4 19.0 %sweep_y.1.before_ref = f32[7,24,32,128]{3,2,1,0:T(8,128)} custom-call(f32[7,24,32,128]{3,2,1,0:T(8,128)} %get-tuple-element.36.prim_ref, f32[7,3,24,128]{3,2,1,0:T(8,128)} %copy-done.4, f32[7,3,24,128]{3,2,1,0:T(8,128)} %copy-done.5, f32[7,24,32,128]{3,2,1,0:T(8,128)} %sweep_x.1.before_ref), custom_call_target="tpu_custom_call" | custom-call | flops 21849999360 | bytes 1000 | tf_op jit(solution)/shard_map/sweep_y/pallas_call | solution.py:564
  93.4 0.0 all-to-all-done.1.rows_ref
  93.4 0.0 copy-start
  93.4 10.2 %all-to-all-start.2 = ((f32[1024,4,128]{2,1,0:T(4,128)}), f32[1024,4,128]{2,1,0:T(4,128)}, u32[]{:S(2)}, u32[]{:S(2)}) async-start(f32[1024,4,128]{2,1,0:T(4,128)} %deposit.1), calls=%async_computation.2 | async-start | bytes 4194304 | tf_op jit(solution)/shard_map/all_to_all | solution.py:477
  103.6 0.0 copy-done
  103.6 15.0 %sample.1 = f32[2,256,128]{2,1,0:T(8,128)} custom-call(s32[1,256]{1,0:T(1,128)} %get-tuple-element.29.slot_ref, f32[3,256,128]{2,1,0:T(8,128)} %place_ref.3, f32[256,128]{1,0:T(8,128)} %radius_ref.3, f32[256,128]{1,0:T(8,128)} %speed_ref.3, f32[256,128]{1,0:T(8,128)} %rest_ref.1, f32[1024,4,128]{2,1,0:T(4,128)} %copy-done), custom_call_target="tpu_custom_call" | custom-call | flops 17250000896 | bytes 1000 | tf_op jit(solution)/shard_map/sample/pallas_call | solution.py:589
  118.6 17.5 %sweep_z.1.state_ref = f32[7,24,32,128]{3,2,1,0:T(8,128)} custom-call(f32[7,24,32,128]{3,2,1,0:T(8,128)} %get-tuple-element.36.prim_ref, f32[7,3,32,128]{3,2,1,0:T(8,128)} %copy-done.2, f32[7,3,32,128]{3,2,1,0:T(8,128)} %copy-done.3, f32[7,24,32,128]{3,2,1,0:T(8,128)} %sweep_y.1.before_ref, f32[7,24,32,128]{3,2,1,0:T(8,128)} %flow_ref.3), custom_call_target="tpu_custom_call" | custom-call | flops 19549999104 | bytes 1000 | tf_op jit(solution)/shard_map/sweep_z/pallas_call | solution.py:578
  136.1 0.0 all-to-all-done.2.returned_ref
  136.1 5.9 %scatter.1 = (f32[24,32,128]{2,1,0:T(8,128)}, f32[7,24,32,128]{3,2,1,0:T(8,128)}) custom-call(s32[128,8]{1,0:T(8,128)} %bitcast.7, f32[1024,4,128]{2,1,0:T(4,128)} %all-to-all-done.2.returned_ref, f32[7,24,32,128]{3,2,1,0:T(8,128)} %sweep_z.1.state_ref), custom_call_target="tpu_custom_call", output_to_operand_aliasing={{1}: (2, {})} | custom-call | flops 6899999744 | bytes 1000 | tf_op jit(solution)/shard_map/scatter/pallas_call | solution.py:601
Async XLA Ops:
  4.9 38.1 %collective-permute-start.2 = (f32[7,3,32,128]{3,2,1,0:T(8,128)}, f32[7,3,32,128]{3,2,1,0:T(8,128)S(1)}, u32[]{:S(2)}, u32[]{:S(2)}) collective-permute-start(f32[7,3,32,128]{3,2,1,0:T(8,128)} %get-tuple-element.32), channel_id=1, source_target_pairs={{0,4},{4,8},{8,12},{12,16},{16,20},{20,24},{24,28},{28,32},{32,36}... | collective-permute-start | bytes 1032200 | tf_op jit(solution)/shard_map/ppermute | solution.py:471
  7.5 35.5 %collective-permute-start.3 = (f32[7,3,32,128]{3,2,1,0:T(8,128)}, f32[7,3,32,128]{3,2,1,0:T(8,128)S(1)}, u32[]{:S(2)}, u32[]{:S(2)}) collective-permute-start(f32[7,3,32,128]{3,2,1,0:T(8,128)} %get-tuple-element.33), channel_id=1, source_target_pairs={{4,0},{8,4},{12,8},{16,12},{20,16},{24,20},{28,24},{32,28},{36,32}... | collective-permute-start | bytes 1032200 | tf_op jit(solution)/shard_map/ppermute | solution.py:472
  7.5 35.4 %collective-permute-start = (f32[7,3,24,128]{3,2,1,0:T(8,128)}, f32[7,3,24,128]{3,2,1,0:T(8,128)S(1)}, u32[]{:S(2)}, u32[]{:S(2)}) collective-permute-start(f32[7,3,24,128]{3,2,1,0:T(8,128)} %get-tuple-element.30), channel_id=1, source_target_pairs={{0,1},{1,2},{2,3},{3,0},{4,5},{5,6},{6,7},{7,4},{8,9},{9,10},{10,1... | collective-permute-start | bytes 774152 | tf_op jit(solution)/shard_map/ppermute | solution.py:471
  9.2 33.8 %collective-permute-start.1 = (f32[7,3,24,128]{3,2,1,0:T(8,128)}, f32[7,3,24,128]{3,2,1,0:T(8,128)S(1)}, u32[]{:S(2)}, u32[]{:S(2)}) collective-permute-start(f32[7,3,24,128]{3,2,1,0:T(8,128)} %get-tuple-element.31), channel_id=1, source_target_pairs={{1,0},{2,1},{3,2},{0,3},{5,4},{6,5},{7,6},{4,7},{9,8},{10,9},{11,1... | collective-permute-start | bytes 774152 | tf_op jit(solution)/shard_map/ppermute | solution.py:472
  13.0 30.0 %all-to-all-start = ((s32[128,1,8]{2,1,0:T(1,128)}), s32[128,1,8]{2,1,0:T(1,128)S(1)}, u32[]{:S(2)}, u32[]{:S(2)}) async-start(s32[128,1,8]{2,1,0:T(1,128)} %bitcast.8), calls=%async_computation | async-start | bytes 131072 | tf_op jit(solution)/shard_map/all_to_all | solution.py:477
  43.0 0.6 copy-start.1
  43.0 5.8 %copy-start.4 = (f32[7,3,24,128]{3,2,1,0:T(8,128)}, f32[7,3,24,128]{3,2,1,0:T(8,128)S(1)}, u32[]{:S(2)}) copy-start(f32[7,3,24,128]{3,2,1,0:T(8,128)S(1)} %collective-permute-done.low_ref) | copy-start | bytes 774148
  43.0 5.8 %copy-start.5 = (f32[7,3,24,128]{3,2,1,0:T(8,128)}, f32[7,3,24,128]{3,2,1,0:T(8,128)S(1)}, u32[]{:S(2)}) copy-start(f32[7,3,24,128]{3,2,1,0:T(8,128)S(1)} %collective-permute-done.1.high_ref) | copy-start | bytes 774148
  43.0 5.7 %copy-start.2 = (f32[7,3,32,128]{3,2,1,0:T(8,128)}, f32[7,3,32,128]{3,2,1,0:T(8,128)S(1)}, u32[]{:S(2)}) copy-start(f32[7,3,32,128]{3,2,1,0:T(8,128)S(1)} %collective-permute-done.2.low_ref) | copy-start | bytes 1032196
  43.0 5.7 %copy-start.3 = (f32[7,3,32,128]{3,2,1,0:T(8,128)}, f32[7,3,32,128]{3,2,1,0:T(8,128)S(1)}, u32[]{:S(2)}) copy-start(f32[7,3,32,128]{3,2,1,0:T(8,128)S(1)} %collective-permute-done.3.high_ref) | copy-start | bytes 1032196
  48.8 44.6 %all-to-all-start.1 = ((f32[1024,4,128]{2,1,0:T(4,128)}), f32[1024,4,128]{2,1,0:T(4,128)S(1)}, u32[]{:S(2)}, u32[]{:S(2)}) async-start(f32[1024,4,128]{2,1,0:T(4,128)} %serve.1), calls=%async_computation.1 | async-start | bytes 4194304 | tf_op jit(solution)/shard_map/all_to_all | solution.py:477
  93.4 10.2 %copy-start = (f32[1024,4,128]{2,1,0:T(4,128)}, f32[1024,4,128]{2,1,0:T(4,128)S(1)}, u32[]{:S(2)}) copy-start(f32[1024,4,128]{2,1,0:T(4,128)S(1)} %all-to-all-done.1.rows_ref) | copy-start | bytes 6291460
  93.4 42.7 %all-to-all-start.2 = ((f32[1024,4,128]{2,1,0:T(4,128)}), f32[1024,4,128]{2,1,0:T(4,128)}, u32[]{:S(2)}, u32[]{:S(2)}) async-start(f32[1024,4,128]{2,1,0:T(4,128)} %deposit.1), calls=%async_computation.2 | async-start | bytes 4194304 | tf_op jit(solution)/shard_map/all_to_all | solution.py:477

commit v3 on v2

--- a/solution.py
+++ b/solution.py
@@ -9,6 +9,7 @@
 from jax.sharding import PartitionSpec as P
 
 HB = 8
+PAIRS = 2 * HB + 1
 gamma_liquid = 4.4
 stiff_liquid = 3.0
 gamma_gas = 1.4
@@ -42,11 +43,6 @@
 
 
 def inverse(value):
-    guess = pl.reciprocal(value, approx=True)
-    return guess * (2.0 - value * guess)
-
-
-def rough_inverse(value):
     return pl.reciprocal(value, approx=True)
 
 
@@ -81,14 +77,15 @@
     before = dot_nn(onehot_bf, earlier)
     rank = jnp.sum(onehot * before, axis=0, keepdims=True)
     rank = jnp.minimum(rank, HB - 1.0)
-    slot_ref[...] = home * HB + rank.astype(jnp.int32)
-    chosen = lax.broadcasted_iota(jnp.int32, (HB, blocks), 0).astype(F32) == rank
+    rank_int = rank.astype(jnp.int32)
+    slot_ref[...] = jnp.concatenate([home * HB + rank_int, home * PAIRS + 2 * rank_int], axis=0)
+    chosen = lax.broadcasted_iota(jnp.int32, (wanted_ref.shape[1], blocks), 0).astype(F32) == rank
     level = jnp.where(chosen, level + 1.0, 0.0).astype(BF16)
     column = jnp.where(chosen, column, 0.0).astype(BF16)
     level = dot_nt(onehot_bf, level)
     column = dot_nt(onehot_bf, column)
     row = (level - 1.0) * float(height) + column
-    wanted_ref[...] = jnp.where(level > 0.0, row, -1.0).astype(jnp.int32)
+    wanted_ref[...] = jnp.where(level > 0.0, row, -1.0)
 
 
 def primitive_kernel(flow_ref, prim_ref, z_low_ref, z_high_ref, y_low_ref, y_high_ref):
@@ -137,7 +134,7 @@
     den_down = 6.0 * (low3 + mid + high)
     num_up = low * (2.0 * ql - dm1) + mid * (qm + d0) + high3 * (d0 - qh)
     num_down = low3 * (ql + dm1) + mid * (qm + dm1) - high * (2.0 * qh + d0)
-    return cell + num_up * rough_inverse(den_up), cell - num_down * rough_inverse(den_down)
+    return cell + num_up * inverse(den_up), cell - num_down * inverse(den_down)
 
 
 def curvature(step):
@@ -220,7 +217,7 @@
         count = -(-(end - begin) // size)
         return count, lambda k: pl.multiple_of(begin + k * size, 8)
 
-    size = 32
+    size = 64
     begin = first - 2 * stride if stride % 8 == 0 else first - 8
     count, at = chunk_of(begin, last + 2 * stride, size)
 
@@ -261,16 +258,16 @@
         lax.fori_loop(0, count_b, states, 0)
 
     begin_c = first - stride if stride % 8 == 0 else first - 8
-    count_c, at_c = chunk_of(begin_c, last, 16)
+    count_c, at_c = chunk_of(begin_c, last, 32)
 
     def faces(k, carry):
         row = at_c(k)
-        left = [left_ref[i, pl.ds(row, 16)] for i in range(7)]
-        right = [right_ref[i, pl.ds(row + stride, 16)] for i in range(7)]
+        left = [left_ref[i, pl.ds(row, 32)] for i in range(7)]
+        right = [right_ref[i, pl.ds(row + stride, 32)] for i in range(7)]
         flux, middle = hllc(left, right, normal)
         for i in range(7):
-            flux_ref[i, pl.ds(row, 16)] = flux[i]
-        flux_ref[7, pl.ds(row, 16)] = middle
+            flux_ref[i, pl.ds(row, 32)] = flux[i]
+        flux_ref[7, pl.ds(row, 32)] = middle
         return carry
 
     lax.fori_loop(0, count_c, faces, 0)
@@ -307,7 +304,7 @@
     lax.fori_loop(0, depth, gather, 0)
 
 
-def z_kernel(prim_ref, low_ref, high_ref, before_ref, flow_ref, next_ref, cells_ref, step_ref, curve_ref, left_ref, right_ref, flux_ref):
+def z_kernel(prim_ref, low_ref, high_ref, before_ref, flow_ref, source_ref, next_ref, cells_ref, step_ref, curve_ref, left_ref, right_ref, flux_ref):
     depth, height = prim_ref.shape[1:3]
     first = 3 * height
     for i in range(7):
@@ -331,6 +328,7 @@
             change = before_ref[i, z] + (flux_ref[i, below] - flux_ref[i, here])
             if i == 6:
                 change = change + prim_ref[6, z] * (flux_ref[7, here] - flux_ref[7, below])
+                change = change - source_ref[z]
             next_ref[i, z] = flow_ref[i, z] + time_step * change
         return carry
 
@@ -349,11 +347,8 @@
     lax.fori_loop(0, asked_ref.shape[0], one, 0)
 
 
-def scatter_kernel(asked_ref, returned_ref, state_ref, source_ref, next_ref, fraction_ref, sem, *sums):
-    sources = asked_ref.shape[0]
+def scatter_kernel(asked_ref, returned_ref, source_ref, *sums):
     depth, height, length = source_ref.shape
-    load = pltpu.make_async_copy(state_ref.at[6], fraction_ref, sem)
-    load.start()
 
     def clear(z, carry):
         for total in sums:
@@ -367,13 +362,13 @@
             total = sums[r % len(sums)]
             row = asked_ref[src, r]
             row = jnp.where(row < 0, depth * height, row)
-            slot = src * HB + r
+            pair = src * PAIRS + 2 * r
             near, far = pl.ds(row, 2), pl.ds(row + height, 2)
-            total[near] = total[near] + returned_ref[slot, pl.ds(0, 2), :]
-            total[far] = total[far] + returned_ref[slot, pl.ds(2, 2), :]
-        return carry
-
-    lax.fori_loop(0, sources, one, 0)
+            total[near] = total[near] + returned_ref[pair]
+            total[far] = total[far] + returned_ref[pair + 1]
+        return carry
+
+    lax.fori_loop(0, asked_ref.shape[0], one, 0)
 
     def collect(z, carry):
         rows = pl.ds(pl.multiple_of(z * height, 8), height)
@@ -381,14 +376,9 @@
         for total in sums[1:]:
             value = value + total[rows]
         source_ref[z] = value
-        fraction_ref[z] = fraction_ref[z] - time_step * value
-        return carry
-
-    load.wait()
+        return carry
+
     lax.fori_loop(0, depth, collect, 0)
-    save = pltpu.make_async_copy(fraction_ref, next_ref.at[6], sem)
-    save.start()
-    save.wait()
 
 
 def block_weights(place_ref, block, length):
@@ -399,13 +389,21 @@
     across_sum = 0.5 * jnp.sum(across, axis=0, keepdims=True)
     offset = place_ref[2, pl.ds(block, 1), :] * float(length - 1)
     shift_x = lax.broadcasted_iota(jnp.int32, (length, 128), 0).astype(F32) - offset
-    along = jnp.exp(-0.5 * (shift_x * shift_x))
+    along = jnp.exp2((-0.5 * math.log2(math.e)) * (shift_x * shift_x))
     return across, across_sum, along
 
 
-def deposit_kernel(slot_ref, place_ref, radius_ref, speed_ref, out_ref):
+def deposit_kernel(slot_ref, wanted_ref, place_ref, radius_ref, speed_ref, out_ref):
     length = out_ref.shape[2]
     upper = lax.broadcasted_iota(jnp.int32, (8, 128), 0) < 4
+
+    def ask(k, carry):
+        for j in range(8):
+            home = k * 8 + j
+            out_ref[home * PAIRS + 2 * HB, pl.ds(0, 1), :] = wanted_ref[pl.ds(home, 1), :]
+        return carry
+
+    lax.fori_loop(0, wanted_ref.shape[0] // 8, ask, 0)
 
     def one(block):
         across, across_sum, along = block_weights(place_ref, block, length)
@@ -419,14 +417,19 @@
         both = jnp.where(upper, share_hi, share - share_hi).astype(BF16)
         only = jnp.where(upper, share_hi, 0.0).astype(BF16)
         result = dot_nt(both, along_hi) + dot_nt(only, along_lo)
-        out_ref[slot_ref[0, block]] = result[0:4] + result[4:8]
+        result = result[0:4] + result[4:8]
+        pair = slot_ref[1, block]
+        out_ref[pair] = result[0:2]
+        out_ref[pair + 1] = result[2:4]
+
+    group = math.gcd(radius_ref.shape[0], 32)
 
     def several(k, carry):
-        for j in range(4):
-            one(k * 4 + j)
-        return carry
-
-    lax.fori_loop(0, radius_ref.shape[0] // 4, several, 0)
+        for j in range(group):
+            one(k * group + j)
+        return carry
+
+    lax.fori_loop(0, radius_ref.shape[0] // group, several, 0)
 
 
 def sample_kernel(slot_ref, place_ref, radius_ref, speed_ref, rest_ref, rows_ref, motion_ref, sampled_ref):
@@ -444,12 +447,14 @@
         total = jnp.sum(across * result[0:8], axis=0, keepdims=True)
         sampled_ref[pl.ds(block, 1), :] = pressure_mid + total * inverse(across_sum * result[8:9])
 
+    group = math.gcd(radius_ref.shape[0], 32)
+
     def several(k, carry):
-        for j in range(4):
-            one(k * 4 + j)
-        return carry
-
-    lax.fori_loop(0, radius_ref.shape[0] // 4, several, 0)
+        for j in range(group):
+            one(k * group + j)
+        return carry
+
+    lax.fori_loop(0, radius_ref.shape[0] // group, several, 0)
 
     radius, speed, ratio = radius_ref[...], speed_ref[...], rest_ref[...]
     inv_radius = 1.0 / radius
@@ -487,14 +492,24 @@
 
     slot, wanted = pl.pallas_call(
         functools.partial(slot_kernel, depth=depth, height=height, across_gy=across_gy),
-        out_shape=(shape((1, blocks), jnp.int32), shape((devices, HB), jnp.int32)),
+        out_shape=(shape((2, blocks), jnp.int32), shape((devices, 128))),
         in_specs=[VMEM],
         out_specs=(VMEM, VMEM),
         cost_estimate=cost(2),
         name="slots",
     )(block_tiles.T)
-    asked = exchange(wanted)
-
+    outgoing = pl.pallas_call(
+        deposit_kernel,
+        out_shape=shape((devices * PAIRS, 2, length)),
+        in_specs=[SMEM] + [VMEM] * 4,
+        out_specs=VMEM,
+        compiler_params=params(),
+        cost_estimate=cost(12),
+        name="deposit",
+    )(slot, wanted, bubble_place, bubble_radius, bubble_speed)
+    returned = exchange(outgoing)
+
+    flow_state, _ = lax.optimization_barrier((flow_state, outgoing))
     prim, z_low, z_high, y_low, y_high = pl.pallas_call(
         primitive_kernel,
         out_shape=(
@@ -512,22 +527,21 @@
     )(flow_state)
     y_below, y_above = shift_both(y_low, y_high, "gy")
     z_below, z_above = shift_both(z_low, z_high, "gz")
-    slot, prim = lax.optimization_barrier((slot, prim))
-
-    outgoing = pl.pallas_call(
-        deposit_kernel,
-        out_shape=shape((slots, 4, length)),
-        in_specs=[SMEM, VMEM, VMEM, VMEM],
+
+    change_x = pl.pallas_call(
+        x_kernel,
+        out_shape=shape(field),
+        in_specs=[VMEM],
         out_specs=VMEM,
-        compiler_params=params(),
-        cost_estimate=cost(21),
-        name="deposit",
-    )(slot, bubble_place, bubble_radius, bubble_speed)
-
+        scratch_shapes=[pltpu.VMEM((7, height, length), F32)] * 2,
+        compiler_params=params(),
+        cost_estimate=cost(16),
+        name="sweep_x",
+    )(prim)
+    returned, change_x = lax.optimization_barrier((returned, change_x))
+
+    asked = returned.reshape(devices, PAIRS, 2, length)[:, 2 * HB, 0, :HB].astype(jnp.int32)
     rows = depth * height
-    asked, outgoing, y_below, y_above, z_below, z_above = lax.optimization_barrier(
-        (asked, outgoing, y_below, y_above, z_below, z_above)
-    )
     served = pl.pallas_call(
         functools.partial(serve_kernel, height=height),
         grid=(1,),
@@ -540,16 +554,17 @@
     )(asked, prim.reshape(7, rows, length))
     fetched = exchange(served)
 
-    change_x = pl.pallas_call(
-        x_kernel,
-        out_shape=shape(field),
-        in_specs=[VMEM],
+    returned, asked, change_x, served = lax.optimization_barrier((returned, asked, change_x, served))
+    source = pl.pallas_call(
+        scatter_kernel,
+        out_shape=shape((depth, height, length)),
+        in_specs=[SMEM, VMEM],
         out_specs=VMEM,
-        scratch_shapes=[pltpu.VMEM((7, height, length), F32)] * 2,
-        compiler_params=params(),
-        cost_estimate=cost(16),
-        name="sweep_x",
-    )(prim)
+        scratch_shapes=[pltpu.VMEM(((depth + 2) * height, length), F32)] * 4,
+        compiler_params=params(),
+        cost_estimate=cost(6),
+        name="scatter",
+    )(asked, returned)
 
     def scratch(rows):
         return [
@@ -566,26 +581,24 @@
         out_shape=shape(field),
         in_specs=[VMEM] * 4,
         out_specs=VMEM,
-        scratch_shapes=scratch(16 + depth * (height + 8) + 56),
-        compiler_params=params(),
-        cost_estimate=cost(19),
+        scratch_shapes=scratch(16 + depth * (height + 8) + 80),
+        compiler_params=params(),
+        cost_estimate=cost(16),
         name="sweep_y",
     )(prim, y_below, y_above, change_x)
-
-    outgoing, fetched, change_xy = lax.optimization_barrier((outgoing, fetched, change_xy))
-    returned = exchange(outgoing)
 
     state_next = pl.pallas_call(
         z_kernel,
         out_shape=shape(field),
-        in_specs=[VMEM] * 5,
+        in_specs=[VMEM] * 6,
         out_specs=VMEM,
         scratch_shapes=scratch((depth + 6) * height),
         compiler_params=params(),
-        cost_estimate=cost(17),
+        cost_estimate=cost(15),
         name="sweep_z",
-    )(prim, z_below, z_above, change_xy, flow_state)
-
+    )(prim, z_below, z_above, change_xy, flow_state, source)
+
+    fetched, state_next = lax.optimization_barrier((fetched, state_next))
     motion = pl.pallas_call(
         sample_kernel,
         out_shape=shape((2, blocks, 128)),
@@ -593,23 +606,9 @@
         out_specs=VMEM,
         scratch_shapes=[pltpu.VMEM((blocks, 128), F32)],
         compiler_params=params(),
-        cost_estimate=cost(15),
+        cost_estimate=cost(7),
         name="sample",
     )(slot, bubble_place, bubble_radius, bubble_speed, rest_ratio, fetched)
-
-    returned, state_next, motion = lax.optimization_barrier((returned, state_next, motion))
-    source, state_next = pl.pallas_call(
-        scatter_kernel,
-        out_shape=(shape((depth, height, length)), shape(field)),
-        in_specs=[SMEM, VMEM, pl.BlockSpec(memory_space=pl.ANY)],
-        out_specs=(VMEM, pl.BlockSpec(memory_space=pl.ANY)),
-        scratch_shapes=[pltpu.VMEM((depth, height, length), F32), pltpu.SemaphoreType.DMA]
-        + [pltpu.VMEM(((depth + 2) * height, length), F32)] * 4,
-        input_output_aliases={2: 1},
-        compiler_params=params(),
-        cost_estimate=cost(6),
-        name="scatter",
-    )(asked, returned, state_next)
     return state_next, source, motion
 
 

time: 143 us -> 119 us (0.83)
  Pallas kernels: 105 us -> 82.1 us
  starting transfers between devices: 35.3 us -> 23 us
  waiting for transfers between devices: 0.02 us -> 7.65 us
  local copies, waits for them, and re-layouts: 0.56 us -> 4.21 us
    pallas_call x3, Pallas kernels: 44.5 us -> 32.4 us  [the longest x1 14.8 us: body(): pl.pallas_call(z_kernel, out_shape=shape(field), in_specs=[VMEM] * 6, out...]
    all_to_all x3 -> x2, starting transfers between devices: 28.9 us -> 18 us  [exchange(): lax.all_to_all(values, ('gz', 'gy'), split_axis=0, concat_axis=0, tiled=T...]
    pallas_call x1, Pallas kernels: 15 us -> 7.14 us  [body(): pl.pallas_call(sample_kernel, out_shape=shape((2, blocks, 128)), in_specs...]
    all_to_all x3 -> x2, waiting for transfers between devices: 0.01 us -> 7.64 us  [exchange(): lax.all_to_all(values, ('gz', 'gy'), split_axis=0, concat_axis=0, tiled=T...]
    unnamed x12, local copies, waits for them, and re-layouts: 0.56 us -> 4.17 us
    pallas_call x1, Pallas kernels: 19 us -> 15.9 us  [body(): pl.pallas_call(y_kernel, out_shape=shape(field), in_specs=[VMEM] * 4, out...]
  transfers between devices with their start and end apart: 7 -> 6, of which waited for: 0 -> 1; matrix products, arithmetic and copies ran while one was open for 0% -> 1% of each run, Pallas kernels for 63% -> 51%
where the time goes in v3:
time: 119 us; the launch traced here: 118 us
  Pallas kernels  82.1 us (69%)
  starting transfers between devices  23 us (19%)
  waiting for transfers between devices  7.65 us (6%)
  local copies, waits for them, and re-layouts  4.21 us (4%)
    all_to_all x2, starting transfers between devices, exchange(): lax.all_to_all(values, ('gz', 'gy'), split_axis=0, concat_axis=0, tiled=T...  18 us
    pallas_call x1, Pallas kernels, body(): pl.pallas_call(y_kernel, out_shape=shape(field), in_specs=[VMEM] * 4, out...  15.9 us
    pallas_call x1, Pallas kernels, body(): pl.pallas_call(x_kernel, out_shape=shape(field), in_specs=[VMEM], out_spe...  15.5 us
    pallas_call x1, Pallas kernels, body(): pl.pallas_call(z_kernel, out_shape=shape(field), in_specs=[VMEM] * 6, out...  14.8 us
    pallas_call x1, Pallas kernels, body(): pl.pallas_call(deposit_kernel, out_shape=shape((devices * PAIRS, 2, lengt...  12.5 us
    all_to_all x2, waiting for transfers between devices, exchange(): lax.all_to_all(values, ('gz', 'gy'), split_axis=0, concat_axis=0, tiled=T...  7.64 us
    pallas_call x1, Pallas kernels, body(): pl.pallas_call(sample_kernel, out_shape=shape((2, blocks, 128)), in_specs...  7.14 us
    pallas_call x1, Pallas kernels, body(): pl.pallas_call(functools.partial(serve_kernel, height=height), grid=(1,),...  5.15 us
  transfers between devices with their start and end apart: 6, of which 1 were waited for; matrix products, arithmetic and copies ran while one was open for 1% of the time, Pallas kernels for 51%

profile of v3, /device:TPU:1, one launch (start us, length us, event | category | flops | bytes accessed | tf_op | source)
XLA Modules:
  0.0 118.4 jit_solution(2786518937125444208)
XLA Ops:
  0.6 1.7 %slots.1 = (s32[2,256]{1,0:T(2,128)}, f32[128,128]{1,0:T(8,128)}) custom-call(s32[4,256]{1,0:T(4,128)} %bitcast.8), custom_call_target="tpu_custom_call" | custom-call | flops 2300000000 | bytes 1000 | tf_op jit(solution)/shard_map/slots/pallas_call | solution.py:493
  2.3 12.5 %deposit.1 = f32[2176,2,128]{2,1,0:T(2,128)} custom-call(s32[2,256]{1,0:T(2,128)} %get-tuple-element.18.slot_ref, f32[128,128]{1,0:T(8,128)} %get-tuple-element.19.wanted_ref, f32[3,256,128]{2,1,0:T(8,128)} %place_ref.3, f32[256,128]{1,0:T(8,128)} %radius_ref.3, f32[256,128]{1,0:T(8,128)} %speed_ref.3), custom_call_target="tpu_custom_call" | custom-call | flops 13799999488 | bytes 1000 | tf_op jit(solution)/shard_map/deposit/pallas_call | solution.py:501
  14.9 11.5 %all-to-all-start = ((f32[2176,2,128]{2,1,0:T(2,128)}), f32[2176,2,128]{2,1,0:T(2,128)S(1)}, u32[]{:S(2)}, u32[]{:S(2)}) async-start(f32[2176,2,128]{2,1,0:T(2,128)} %deposit.1), calls=%async_computation | async-start | bytes 4456448 | tf_op jit(solution)/shard_map/all_to_all | solution.py:482
  26.4 4.3 %primitives.1 = (f32[7,24,32,128]{3,2,1,0:T(8,128)}, f32[7,3,32,128]{3,2,1,0:T(8,128)}, f32[7,3,32,128]{3,2,1,0:T(8,128)}, f32[7,3,24,128]{3,2,1,0:T(8,128)}, f32[7,3,24,128]{3,2,1,0:T(8,128)}) custom-call(f32[7,24,32,128]{3,2,1,0:T(8,128)} %flow_ref.1), custom_call_target="tpu_custom_call" | custom-call | flops 4600000000 | bytes 1000 | tf_op jit(solution)/shard_map/primitives/pallas_call | solution.py:513
  30.7 1.5 %collective-permute-start.2 = (f32[7,3,24,128]{3,2,1,0:T(8,128)}, f32[7,3,24,128]{3,2,1,0:T(8,128)S(1)}, u32[]{:S(2)}, u32[]{:S(2)}) collective-permute-start(f32[7,3,24,128]{3,2,1,0:T(8,128)} %get-tuple-element.25), channel_id=1, source_target_pairs={{0,1},{1,2},{2,3},{3,0},{4,5},{5,6},{6,7},{7,4},{8,9},{9,10},{10,1... | collective-permute-start | bytes 774152 | tf_op jit(solution)/shard_map/ppermute | solution.py:476
  32.2 1.8 %collective-permute-start.3 = (f32[7,3,24,128]{3,2,1,0:T(8,128)}, f32[7,3,24,128]{3,2,1,0:T(8,128)S(1)}, u32[]{:S(2)}, u32[]{:S(2)}) collective-permute-start(f32[7,3,24,128]{3,2,1,0:T(8,128)} %get-tuple-element.26), channel_id=1, source_target_pairs={{1,0},{2,1},{3,2},{0,3},{5,4},{6,5},{7,6},{4,7},{9,8},{10,9},{11,1... | collective-permute-start | bytes 774152 | tf_op jit(solution)/shard_map/ppermute | solution.py:477
  33.9 1.7 %collective-permute-start = (f32[7,3,32,128]{3,2,1,0:T(8,128)}, f32[7,3,32,128]{3,2,1,0:T(8,128)S(1)}, u32[]{:S(2)}, u32[]{:S(2)}) collective-permute-start(f32[7,3,32,128]{3,2,1,0:T(8,128)} %get-tuple-element.23), channel_id=1, source_target_pairs={{0,4},{4,8},{8,12},{12,16},{16,20},{20,24},{24,28},{28,32},{32,36}... | collective-permute-start | bytes 1032200 | tf_op jit(solution)/shard_map/ppermute | solution.py:476
  35.6 0.0 collective-permute-start.1
  35.7 15.5 %sweep_x.1.before_ref = f32[7,24,32,128]{3,2,1,0:T(8,128)} custom-call(f32[7,24,32,128]{3,2,1,0:T(8,128)} %get-tuple-element.21.prim_ref), custom_call_target="tpu_custom_call" | custom-call | flops 18400000000 | bytes 1000 | tf_op jit(solution)/shard_map/sweep_x/pallas_call | solution.py:531
  51.2 7.6 %all-to-all-done.returned_ref = f32[2176,2,128]{2,1,0:T(2,128)S(1)} async-done(((f32[2176,2,128]{2,1,0:T(2,128)}), f32[2176,2,128]{2,1,0:T(2,128)S(1)}, u32[]{:S(2)}, u32[]{:S(2)}) %all-to-all-start) | async-done | bytes 2228256 | tf_op jit(solution)/shard_map/all_to_all | solution.py:482
  58.8 0.0 copy-start
  58.8 0.7 convert_bitcast_fusion.asked_ref
  59.6 5.1 %serve.1 = f32[1024,4,128]{2,1,0:T(4,128)} custom-call(s32[128,8]{1,0:T(8,128)} %convert_bitcast_fusion.asked_ref, f32[7,768,128]{2,1,0:T(8,128)} %bitcast.9), custom_call_target="tpu_custom_call" | custom-call | flops 5750000128 | bytes 1000 | tf_op jit(solution)/shard_map/serve/pallas_call | solution.py:545
  64.7 0.0 copy-done
  64.7 6.5 %all-to-all-start.1 = ((f32[1024,4,128]{2,1,0:T(4,128)}), f32[1024,4,128]{2,1,0:T(4,128)S(1)}, u32[]{:S(2)}, u32[]{:S(2)}) async-start(f32[1024,4,128]{2,1,0:T(4,128)} %serve.1), calls=%async_computation.1 | async-start | bytes 4194304 | tf_op jit(solution)/shard_map/all_to_all | solution.py:482
  71.2 0.0 collective-permute-done.2.low_ref
  71.2 0.0 copy-start.4
  71.2 0.0 collective-permute-done.3.high_ref
  71.2 0.7 copy-done.4
  71.9 0.0 copy-start.5
  71.9 0.7 copy-done.5
  72.6 15.9 %sweep_y.1.before_ref = f32[7,24,32,128]{3,2,1,0:T(8,128)} custom-call(f32[7,24,32,128]{3,2,1,0:T(8,128)} %get-tuple-element.21.prim_ref, f32[7,3,24,128]{3,2,1,0:T(8,128)} %copy-done.4, f32[7,3,24,128]{3,2,1,0:T(8,128)} %copy-done.5, f32[7,24,32,128]{3,2,1,0:T(8,128)} %sweep_x.1.before_ref), custom_call_target="tpu_custom_call" | custom-call | flops 18400000000 | bytes 1000 | tf_op jit(solution)/shard_map/sweep_y/pallas_call | solution.py:579
  88.5 5.1 %scatter.1.source_ref = f32[24,32,128]{2,1,0:T(8,128)} custom-call(s32[128,8]{1,0:T(8,128)} %convert_bitcast_fusion.asked_ref, f32[2176,2,128]{2,1,0:T(2,128)} %copy-done), custom_call_target="tpu_custom_call" | custom-call | flops 6899999744 | bytes 1000 | tf_op jit(solution)/shard_map/scatter/pallas_call | solution.py:558
  93.7 0.0 collective-permute-done.low_ref
  93.7 0.0 copy-start.2
  93.7 0.0 collective-permute-done.1.high_ref
  93.7 0.7 copy-done.2
  94.4 0.0 copy-start.3
  94.4 0.7 copy-done.3
  95.1 14.8 %sweep_z.1 = f32[7,24,32,128]{3,2,1,0:T(8,128)} custom-call(f32[7,24,32,128]{3,2,1,0:T(8,128)} %get-tuple-element.21.prim_ref, f32[7,3,32,128]{3,2,1,0:T(8,128)} %copy-done.2, f32[7,3,32,128]{3,2,1,0:T(8,128)} %copy-done.3, f32[7,24,32,128]{3,2,1,0:T(8,128)} %sweep_y.1.before_ref, f32[7,24,32,128]{3,2,1,0:T(8,128)} %flow_ref.1, f32[24,32,128]{2,1,0:T(8,128)} %scatter.1.source_ref), custom_call_target="tpu_custom_call" | custom-call | flops 17250000896 | bytes 1000 | tf_op jit(solution)/shard_map/sweep_z/pallas_call | solution.py:590
  109.9 0.0 all-to-all-done.1.rows_ref
  109.9 0.0 copy-start.1
  109.9 1.3 %copy-done.1 = f32[1024,4,128]{2,1,0:T(4,128)} copy-done((f32[1024,4,128]{2,1,0:T(4,128)}, f32[1024,4,128]{2,1,0:T(4,128)S(1)}, u32[]{:S(2)}) %copy-start.1) | copy-done | bytes 2097176
  111.2 7.1 %sample.1 = f32[2,256,128]{2,1,0:T(8,128)} custom-call(s32[2,256]{1,0:T(2,128)} %get-tuple-element.18.slot_ref, f32[3,256,128]{2,1,0:T(8,128)} %place_ref.3, f32[256,128]{1,0:T(8,128)} %radius_ref.3, f32[256,128]{1,0:T(8,128)} %speed_ref.3, f32[256,128]{1,0:T(8,128)} %rest_ref.1, f32[1024,4,128]{2,1,0:T(4,128)} %copy-done.1), custom_call_target="tpu_custom_call" | custom-call | flops 8049999872 | bytes 1000 | tf_op jit(solution)/shard_map/sample/pallas_call | solution.py:602
  (1 shorter events, 0.0 us)
Async XLA Ops:
  14.9 43.9 %all-to-all-start = ((f32[2176,2,128]{2,1,0:T(2,128)}), f32[2176,2,128]{2,1,0:T(2,128)S(1)}, u32[]{:S(2)}, u32[]{:S(2)}) async-start(f32[2176,2,128]{2,1,0:T(2,128)} %deposit.1), calls=%async_computation | async-start | bytes 4456448 | tf_op jit(solution)/shard_map/all_to_all | solution.py:482
  30.7 40.5 %collective-permute-start.2 = (f32[7,3,24,128]{3,2,1,0:T(8,128)}, f32[7,3,24,128]{3,2,1,0:T(8,128)S(1)}, u32[]{:S(2)}, u32[]{:S(2)}) collective-permute-start(f32[7,3,24,128]{3,2,1,0:T(8,128)} %get-tuple-element.25), channel_id=1, source_target_pairs={{0,1},{1,2},{2,3},{3,0},{4,5},{5,6},{6,7},{7,4},{8,9},{9,10},{10,1... | collective-permute-start | bytes 774152 | tf_op jit(solution)/shard_map/ppermute | solution.py:476
  32.2 39.1 %collective-permute-start.3 = (f32[7,3,24,128]{3,2,1,0:T(8,128)}, f32[7,3,24,128]{3,2,1,0:T(8,128)S(1)}, u32[]{:S(2)}, u32[]{:S(2)}) collective-permute-start(f32[7,3,24,128]{3,2,1,0:T(8,128)} %get-tuple-element.26), channel_id=1, source_target_pairs={{1,0},{2,1},{3,2},{0,3},{5,4},{6,5},{7,6},{4,7},{9,8},{10,9},{11,1... | collective-permute-start | bytes 774152 | tf_op jit(solution)/shard_map/ppermute | solution.py:477
  33.9 59.7 %collective-permute-start = (f32[7,3,32,128]{3,2,1,0:T(8,128)}, f32[7,3,32,128]{3,2,1,0:T(8,128)S(1)}, u32[]{:S(2)}, u32[]{:S(2)}) collective-permute-start(f32[7,3,32,128]{3,2,1,0:T(8,128)} %get-tuple-element.23), channel_id=1, source_target_pairs={{0,4},{4,8},{8,12},{12,16},{16,20},{20,24},{24,28},{28,32},{32,36}... | collective-permute-start | bytes 1032200 | tf_op jit(solution)/shard_map/ppermute | solution.py:476
  35.6 58.0 %collective-permute-start.1 = (f32[7,3,32,128]{3,2,1,0:T(8,128)}, f32[7,3,32,128]{3,2,1,0:T(8,128)S(1)}, u32[]{:S(2)}, u32[]{:S(2)}) collective-permute-start(f32[7,3,32,128]{3,2,1,0:T(8,128)} %get-tuple-element.24), channel_id=1, source_target_pairs={{4,0},{8,4},{12,8},{16,12},{20,16},{24,20},{28,24},{32,28},{36,32}... | collective-permute-start | bytes 1032200 | tf_op jit(solution)/shard_map/ppermute | solution.py:477
  58.8 5.9 %copy-start = (f32[2176,2,128]{2,1,0:T(2,128)}, f32[2176,2,128]{2,1,0:T(2,128)S(1)}, u32[]{:S(2)}) copy-start(f32[2176,2,128]{2,1,0:T(2,128)S(1)} %all-to-all-done.returned_ref) | copy-start | bytes 6684676
  64.7 45.2 %all-to-all-start.1 = ((f32[1024,4,128]{2,1,0:T(4,128)}), f32[1024,4,128]{2,1,0:T(4,128)S(1)}, u32[]{:S(2)}, u32[]{:S(2)}) async-start(f32[1024,4,128]{2,1,0:T(4,128)} %serve.1), calls=%async_computation.1 | async-start | bytes 4194304 | tf_op jit(solution)/shard_map/all_to_all | solution.py:482
  71.2 0.7 copy-start.4
  71.9 0.7 copy-start.5
  93.7 0.7 copy-start.2
  94.4 0.7 copy-start.3
  109.9 1.3 %copy-start.1 = (f32[1024,4,128]{2,1,0:T(4,128)}, f32[1024,4,128]{2,1,0:T(4,128)S(1)}, u32[]{:S(2)}) copy-start(f32[1024,4,128]{2,1,0:T(4,128)S(1)} %all-to-all-done.1.rows_ref) | copy-start | bytes 6291460

commit v4 on v3

--- a/solution.py
+++ b/solution.py
@@ -26,6 +26,7 @@
 
 VMEM = pl.BlockSpec(memory_space=pltpu.VMEM)
 SMEM = pl.BlockSpec(memory_space=pltpu.SMEM)
+ANY = pl.BlockSpec(memory_space=pl.ANY)
 F32 = jnp.float32
 BF16 = jnp.bfloat16
 
@@ -88,31 +89,16 @@
     wanted_ref[...] = jnp.where(level > 0.0, row, -1.0)
 
 
-def primitive_kernel(flow_ref, prim_ref, z_low_ref, z_high_ref, y_low_ref, y_high_ref):
-    depth, height = flow_ref.shape[1], flow_ref.shape[2]
-
-    def slab(z, carry):
-        first, second = flow_ref[0, z], flow_ref[1, z]
-        density = first + second
-        inv_density = inverse(density)
-        mom = [flow_ref[2 + i, z] for i in range(3)]
-        vel = [m * inv_density for m in mom]
-        kinetic = 0.5 * (mom[0] * vel[0] + mom[1] * vel[1] + mom[2] * vel[2])
-        fraction = flow_ref[6, z]
-        stiffness = stiff_base + stiff_slope * fraction
-        pressure = (flow_ref[5, z] - kinetic - offset_slope * fraction) * inverse(stiffness)
-        for i, value in enumerate([first, second] + vel + [pressure, fraction]):
-            prim_ref[i, z] = value
-            for j in range(3):
-                y_low_ref[i, j, pl.ds(z, 1), :] = value[j : j + 1]
-                y_high_ref[i, j, pl.ds(z, 1), :] = value[height - 3 + j : height - 2 + j]
-        return carry
-
-    lax.fori_loop(0, depth, slab, 0)
-    for i in range(7):
-        for j in range(3):
-            z_low_ref[i, j] = prim_ref[i, j]
-            z_high_ref[i, j] = prim_ref[i, depth - 3 + j]
+def primitives(value):
+    first, second = value[0], value[1]
+    density = first + second
+    inv_density = inverse(density)
+    vel = [value[2 + i] * inv_density for i in range(3)]
+    kinetic = 0.5 * (value[2] * vel[0] + value[3] * vel[1] + value[4] * vel[2])
+    fraction = value[6]
+    stiffness = stiff_base + stiff_slope * fraction
+    pressure = (value[5] - kinetic - offset_slope * fraction) * inverse(stiffness)
+    return [first, second] + vel + [pressure, fraction]
 
 
 def weno_pair(cell, dm2, dm1, d0, dp1, zm, z0, zp):
@@ -180,51 +166,75 @@
     return flux, middle
 
 
-def x_kernel(prim_ref, change_ref, left_ref, right_ref):
-    depth, height, length = prim_ref.shape[1:]
+def x_kernel(
+    flow_in, change_out, pressure_ref, z_low_ref, z_high_ref, y_low_ref, y_high_ref,
+    flow_ref, prim_ref, cells_ref, step_ref, curve_ref, left_ref, right_ref, flux_ref, load_sems, save_sems,
+):
+    depth, height, length = flow_ref.shape[1:]
+    groups = load_sems.shape[0]
+    slabs = depth // groups
+    width = slabs * height
+    pitch = length + 8
+    first = 16
+    loads = []
+    for g in range(groups):
+        here = pl.ds(g * slabs, slabs)
+        loads.append(pltpu.make_async_copy(flow_in.at[:, here], flow_ref.at[:, here], load_sems.at[g]))
+        loads[-1].start()
 
     def slab(z, carry):
+        rows = pl.ds(pl.multiple_of(z * height, 8), height)
+        values = primitives([flow_ref[i, z] for i in range(7)])
+        pressure_ref[z] = values[5]
+        for i, value in enumerate(values):
+            prim_ref[i, rows] = value
+            for j in range(3):
+                y_low_ref[i, j, pl.ds(z, 1), :] = value[j : j + 1]
+                y_high_ref[i, j, pl.ds(z, 1), :] = value[height - 3 + j : height - 2 + j]
+        return carry
+
+    for g in range(groups):
+        loads[g].wait()
+        lax.fori_loop(g * slabs, (g + 1) * slabs, slab, 0)
+        base = first + g * pitch
         for i in range(7):
-            cell = prim_ref[i, z]
-            d0 = pltpu.roll(cell, length - 1, 1) - cell
-            dm1 = pltpu.roll(d0, 1, 1)
-            dm2 = pltpu.roll(d0, 2, 1)
-            dp1 = pltpu.roll(d0, length - 1, 1)
-            z0 = curvature(d0 - dm1)
-            zm = pltpu.roll(z0, 1, 1)
-            zp = pltpu.roll(z0, length - 1, 1)
-            up, down = weno_pair(cell, dm2, dm1, d0, dp1, zm, z0, zp)
-            left_ref[i] = up
-            right_ref[i] = pltpu.roll(down, length - 1, 1)
-        for part in range(height // 16):
-            rows = pl.ds(16 * part, 16)
-            left = [left_ref[i, rows] for i in range(7)]
-            right = [right_ref[i, rows] for i in range(7)]
-            flux, middle = hllc(left, right, 0)
-            for i in range(6):
-                change_ref[i, z, rows] = pltpu.roll(flux[i], 1, 1) - flux[i]
-            fraction = prim_ref[6, z, rows]
-            change_ref[6, z, rows] = (pltpu.roll(flux[6], 1, 1) - flux[6]) + fraction * (
-                middle - pltpu.roll(middle, 1, 1)
-            )
-        return carry
-
-    lax.fori_loop(0, depth, slab, 0)
-
-
-def row_sweep(cells_ref, step_ref, curve_ref, left_ref, right_ref, flux_ref, stride, first, last, normal):
-    def chunk_of(begin, end, size):
-        count = -(-(end - begin) // size)
-        return count, lambda k: pl.multiple_of(begin + k * size, 8)
-
+            tile = prim_ref[i, pl.ds(g * width, width)].T
+            cells_ref[i, pl.ds(base, length)] = tile
+            cells_ref[i, pl.ds(base - 3, 3)] = tile[length - 3 :]
+            cells_ref[i, pl.ds(base + length, 3)] = tile[:3]
+    for i in range(7):
+        z_low_ref[i] = prim_ref[i, pl.ds(0, 3 * height)]
+        z_high_ref[i] = prim_ref[i, pl.ds((depth - 3) * height, 3 * height)]
+
+    last = first + groups * pitch
+    row_states(cells_ref, step_ref, curve_ref, left_ref, right_ref, 1, first, last)
+    row_faces(left_ref, right_ref, flux_ref, 1, first - 8, -(-(last - first + 8) // 32), 0)
+
+    saves = []
+    for g in range(groups):
+        here, under = pl.ds(first + g * pitch, length), pl.ds(first + g * pitch - 1, length)
+        out = pl.ds(g * width, width)
+        for i in range(7):
+            diff = flux_ref[i, under] - flux_ref[i, here]
+            if i == 6:
+                diff = diff + cells_ref[6, here] * (flux_ref[7, here] - flux_ref[7, under])
+            prim_ref[i, out] = diff.T
+        saves.append(pltpu.make_async_copy(prim_ref.at[:, out], change_out.at[:, out], save_sems.at[g]))
+        saves[-1].start()
+    for save in saves:
+        save.wait()
+
+
+def row_states(cells_ref, step_ref, curve_ref, left_ref, right_ref, stride, first, last):
     size = 64
-    begin = first - 2 * stride if stride % 8 == 0 else first - 8
-    count, at = chunk_of(begin, last + 2 * stride, size)
+    reach = -(-stride // 8) * 8
+
+    def loop(begin, end, step):
+        lax.fori_loop(0, -(-(end - begin) // size), lambda k, c: step(pl.multiple_of(begin + k * size, 8), c), 0)
 
     for i in range(7):
 
-        def prepare(k, carry, i=i):
-            row = at(k)
+        def prepare(row, carry, i=i):
             mid = cells_ref[i, pl.ds(row, size)]
             d0 = cells_ref[i, pl.ds(row + stride, size)] - mid
             dm1 = mid - cells_ref[i, pl.ds(row - stride, size)]
@@ -232,17 +242,14 @@
             curve_ref[pl.ds(row, size)] = curvature(d0 - dm1)
             return carry
 
-        if stride % 8 == 0:
+        if stride == reach:
             edge = pl.ds(first - 3 * stride, size)
             step_ref[edge] = cells_ref[i, pl.ds(first - 2 * stride, size)] - cells_ref[i, edge]
-        lax.fori_loop(0, count, prepare, 0)
-
-        begin_b = first - stride if stride % 8 == 0 else first - 8
-        count_b, at_b = chunk_of(begin_b, last + stride, size)
-
-        def states(k, carry, i=i, at_b=at_b):
-            row = at_b(k)
-
+            loop(first - 2 * stride, last + 2 * stride, prepare)
+        else:
+            loop(first - reach, last + 2 * stride, prepare)
+
+        def states(row, carry, i=i):
             def take(ref, shift):
                 return ref[pl.ds(row + shift * stride, size)]
 
@@ -255,84 +262,106 @@
             right_ref[i, pl.ds(row, size)] = down
             return carry
 
-        lax.fori_loop(0, count_b, states, 0)
-
-    begin_c = first - stride if stride % 8 == 0 else first - 8
-    count_c, at_c = chunk_of(begin_c, last, 32)
+        loop(first - reach, last + stride, states)
+
+
+def row_faces(left_ref, right_ref, flux_ref, stride, begin, count, normal):
+    size = 32
 
     def faces(k, carry):
-        row = at_c(k)
-        left = [left_ref[i, pl.ds(row, 32)] for i in range(7)]
-        right = [right_ref[i, pl.ds(row + stride, 32)] for i in range(7)]
+        row = pl.multiple_of(begin + k * size, 8)
+        left = [left_ref[i, pl.ds(row, size)] for i in range(7)]
+        right = [right_ref[i, pl.ds(row + stride, size)] for i in range(7)]
         flux, middle = hllc(left, right, normal)
         for i in range(7):
-            flux_ref[i, pl.ds(row, 32)] = flux[i]
-        flux_ref[7, pl.ds(row, 32)] = middle
-        return carry
-
-    lax.fori_loop(0, count_c, faces, 0)
-
-
-def y_kernel(prim_ref, low_ref, high_ref, before_ref, change_ref, cells_ref, step_ref, curve_ref, left_ref, right_ref, flux_ref):
-    depth, height = prim_ref.shape[1:3]
+            flux_ref[i, pl.ds(row, size)] = flux[i]
+        flux_ref[7, pl.ds(row, size)] = middle
+        return carry
+
+    lax.fori_loop(0, count, faces, 0)
+
+
+def yz_kernel(
+    flow_in, change_in, source_in, z_below_in, z_above_in, y_below_ref, y_above_ref, next_out,
+    flow_ref, change_ref, source_ref, cells_z, cells_y, step_ref, curve_ref, left_ref, right_ref, flux_ref,
+    flow_sems, side_sems, out_sems,
+):
+    depth, height = flow_ref.shape[1:3]
+    parts = flow_sems.shape[0]
+    part = depth // parts
     pitch = height + 8
-    first = 16
+    first_y = 16
+    first_z = 3 * height
+    rows_z = depth * height
+    loads = []
+    for p in range(parts):
+        here = pl.ds(p * part, part)
+        loads.append(pltpu.make_async_copy(flow_in.at[:, here], flow_ref.at[:, here], flow_sems.at[p]))
+    below = pltpu.make_async_copy(z_below_in, cells_z.at[:, pl.ds(0, first_z)], side_sems.at[0])
+    above = pltpu.make_async_copy(z_above_in, cells_z.at[:, pl.ds(first_z + rows_z, first_z)], side_sems.at[1])
+    change = pltpu.make_async_copy(change_in, change_ref, side_sems.at[2])
+    source = pltpu.make_async_copy(source_in, source_ref, side_sems.at[3])
+    for copy in loads + [below, above, change, source]:
+        copy.start()
 
     def fill(z, carry):
-        base = pl.multiple_of(first + z * pitch, 8)
-        for i in range(7):
-            cells_ref[i, pl.ds(base, height)] = prim_ref[i, z]
+        base = pl.multiple_of(first_y + z * pitch, 8)
+        values = primitives([flow_ref[i, z] for i in range(7)])
+        for i, value in enumerate(values):
+            cells_z[i, pl.ds(pl.multiple_of(first_z + z * height, 8), height)] = value
+            cells_y[i, pl.ds(base, height)] = value
             for j in range(3):
-                cells_ref[i, pl.ds(base - 3 + j, 1)] = low_ref[i, j, pl.ds(z, 1), :]
-                cells_ref[i, pl.ds(base + height + j, 1)] = high_ref[i, j, pl.ds(z, 1), :]
-        return carry
-
-    lax.fori_loop(0, depth, fill, 0)
-    row_sweep(cells_ref, step_ref, curve_ref, left_ref, right_ref, flux_ref, 1, first, first + depth * pitch, 1)
+                cells_y[i, pl.ds(base - 3 + j, 1)] = y_below_ref[i, j, pl.ds(z, 1), :]
+                cells_y[i, pl.ds(base + height + j, 1)] = y_above_ref[i, j, pl.ds(z, 1), :]
+        return carry
+
+    for p in range(parts):
+        loads[p].wait()
+        lax.fori_loop(p * part, (p + 1) * part, fill, 0)
+
+    last_y = first_y + depth * pitch
+    row_states(cells_y, step_ref, curve_ref, left_ref, right_ref, 1, first_y, last_y)
+    row_faces(left_ref, right_ref, flux_ref, 1, first_y - 8, -(-(last_y - first_y + 8) // 32), 1)
+    change.wait()
+
+    def differences(base, lower, z):
+        here, under = pl.ds(base, height), pl.ds(base - lower, height)
+        diff = [flux_ref[i, under] - flux_ref[i, here] for i in range(7)]
+        fraction = cells_z[6, pl.ds(pl.multiple_of(first_z + z * height, 8), height)]
+        diff[6] = diff[6] + fraction * (flux_ref[7, here] - flux_ref[7, under])
+        return diff
 
     def gather(z, carry):
-        base = pl.multiple_of(first + z * pitch, 8)
-        here, below = pl.ds(base, height), pl.ds(base - 1, height)
-        for i in range(6):
-            change_ref[i, z] = before_ref[i, z] + (flux_ref[i, below] - flux_ref[i, here])
-        change_ref[6, z] = before_ref[6, z] + (
-            (flux_ref[6, below] - flux_ref[6, here])
-            + prim_ref[6, z] * (flux_ref[7, here] - flux_ref[7, below])
-        )
+        for i, diff in enumerate(differences(pl.multiple_of(first_y + z * pitch, 8), 1, z)):
+            rows = pl.ds(pl.multiple_of(z * height, 8), height)
+            change_ref[i, rows] = change_ref[i, rows] + diff
         return carry
 
     lax.fori_loop(0, depth, gather, 0)
 
-
-def z_kernel(prim_ref, low_ref, high_ref, before_ref, flow_ref, source_ref, next_ref, cells_ref, step_ref, curve_ref, left_ref, right_ref, flux_ref):
-    depth, height = prim_ref.shape[1:3]
-    first = 3 * height
-    for i in range(7):
-        for j in range(3):
-            cells_ref[i, pl.ds(j * height, height)] = low_ref[i, j]
-            cells_ref[i, pl.ds((depth + 3 + j) * height, height)] = high_ref[i, j]
-
-    def fill(z, carry):
-        base = pl.multiple_of(first + z * height, 8)
-        for i in range(7):
-            cells_ref[i, pl.ds(base, height)] = prim_ref[i, z]
-        return carry
-
-    lax.fori_loop(0, depth, fill, 0)
-    row_sweep(cells_ref, step_ref, curve_ref, left_ref, right_ref, flux_ref, height, first, first + depth * height, 2)
+    below.wait()
+    above.wait()
+    source.wait()
+    row_states(cells_z, step_ref, curve_ref, left_ref, right_ref, height, first_z, first_z + rows_z)
 
     def update(z, carry):
-        base = pl.multiple_of(first + z * height, 8)
-        here, below = pl.ds(base, height), pl.ds(base - height, height)
-        for i in range(7):
-            change = before_ref[i, z] + (flux_ref[i, below] - flux_ref[i, here])
+        for i, diff in enumerate(differences(pl.multiple_of(first_z + z * height, 8), height, z)):
+            total = change_ref[i, pl.ds(pl.multiple_of(z * height, 8), height)] + diff
             if i == 6:
-                change = change + prim_ref[6, z] * (flux_ref[7, here] - flux_ref[7, below])
-                change = change - source_ref[z]
-            next_ref[i, z] = flow_ref[i, z] + time_step * change
-        return carry
-
-    lax.fori_loop(0, depth, update, 0)
+                total = total - source_ref[z]
+            flow_ref[i, z] = flow_ref[i, z] + time_step * total
+        return carry
+
+    saves = []
+    row_faces(left_ref, right_ref, flux_ref, height, first_z - height, height // 32, 2)
+    for p in range(parts):
+        row_faces(left_ref, right_ref, flux_ref, height, first_z + p * part * height, part * height // 32, 2)
+        lax.fori_loop(p * part, (p + 1) * part, update, 0)
+        here = pl.ds(p * part, part)
+        saves.append(pltpu.make_async_copy(flow_ref.at[:, here], next_out.at[:, here], out_sems.at[p]))
+        saves[-1].start()
+    for save in saves:
+        save.wait()
 
 
 def serve_kernel(asked_ref, pressure_ref, served_ref, *, height):
@@ -340,8 +369,8 @@
         for r in range(HB):
             row = jnp.maximum(asked_ref[src, r], 0)
             slot = src * HB + r
-            served_ref[slot, pl.ds(0, 2), :] = pressure_ref[0, pl.ds(row, 2), :]
-            served_ref[slot, pl.ds(2, 2), :] = pressure_ref[0, pl.ds(row + height, 2), :]
+            served_ref[slot, pl.ds(0, 2), :] = pressure_ref[pl.ds(row, 2), :]
+            served_ref[slot, pl.ds(2, 2), :] = pressure_ref[pl.ds(row + height, 2), :]
         return carry
 
     lax.fori_loop(0, asked_ref.shape[0], one, 0)
@@ -510,48 +539,51 @@
     returned = exchange(outgoing)
 
     flow_state, _ = lax.optimization_barrier((flow_state, outgoing))
-    prim, z_low, z_high, y_low, y_high = pl.pallas_call(
-        primitive_kernel,
+    rows = depth * height
+    groups = rows // 128
+    turned = 16 + groups * (length + 8) + 80
+    change_x, pressure, z_low, z_high, y_low, y_high = pl.pallas_call(
+        x_kernel,
         out_shape=(
-            shape(field),
-            shape((7, 3, height, length)),
-            shape((7, 3, height, length)),
+            shape((7, rows, length)),
+            shape((depth, height, length)),
+            shape((7, 3 * height, length)),
+            shape((7, 3 * height, length)),
             shape((7, 3, depth, length)),
             shape((7, 3, depth, length)),
         ),
-        in_specs=[VMEM],
-        out_specs=(VMEM,) * 5,
+        in_specs=[ANY],
+        out_specs=(ANY,) + (VMEM,) * 5,
+        scratch_shapes=[
+            pltpu.VMEM(field, F32),
+            pltpu.VMEM((7, rows, length), F32),
+            pltpu.VMEM((7, turned, 128), F32),
+            pltpu.VMEM((turned, 128), F32),
+            pltpu.VMEM((turned, 128), F32),
+            pltpu.VMEM((7, turned, 128), F32),
+            pltpu.VMEM((7, turned, 128), F32),
+            pltpu.VMEM((8, turned, 128), F32),
+            pltpu.SemaphoreType.DMA((groups,)),
+            pltpu.SemaphoreType.DMA((groups,)),
+        ],
         compiler_params=params(),
-        cost_estimate=cost(4),
-        name="primitives",
+        cost_estimate=cost(14),
+        name="sweep_x",
     )(flow_state)
     y_below, y_above = shift_both(y_low, y_high, "gy")
     z_below, z_above = shift_both(z_low, z_high, "gz")
-
-    change_x = pl.pallas_call(
-        x_kernel,
-        out_shape=shape(field),
-        in_specs=[VMEM],
-        out_specs=VMEM,
-        scratch_shapes=[pltpu.VMEM((7, height, length), F32)] * 2,
-        compiler_params=params(),
-        cost_estimate=cost(16),
-        name="sweep_x",
-    )(prim)
     returned, change_x = lax.optimization_barrier((returned, change_x))
 
     asked = returned.reshape(devices, PAIRS, 2, length)[:, 2 * HB, 0, :HB].astype(jnp.int32)
-    rows = depth * height
     served = pl.pallas_call(
         functools.partial(serve_kernel, height=height),
-        grid=(1,),
         out_shape=shape((slots, 4, length)),
-        in_specs=[SMEM, pl.BlockSpec((1, rows, length), lambda i: (5, 0, 0))],
+        in_specs=[SMEM, VMEM],
         out_specs=VMEM,
         compiler_params=params(),
         cost_estimate=cost(5),
         name="serve",
-    )(asked, prim.reshape(7, rows, length))
+    )(asked, pressure.reshape(rows, length))
     fetched = exchange(served)
 
     returned, asked, change_x, served = lax.optimization_barrier((returned, asked, change_x, served))
@@ -566,37 +598,31 @@
         name="scatter",
     )(asked, returned)
 
-    def scratch(rows):
-        return [
+    padded = 16 + depth * (height + 8) + 80
+    state_next = pl.pallas_call(
+        yz_kernel,
+        out_shape=shape(field),
+        in_specs=[ANY] * 5 + [VMEM] * 2,
+        out_specs=ANY,
+        scratch_shapes=[
+            pltpu.VMEM(field, F32),
             pltpu.VMEM((7, rows, length), F32),
-            pltpu.VMEM((rows, length), F32),
-            pltpu.VMEM((rows, length), F32),
-            pltpu.VMEM((7, rows, length), F32),
-            pltpu.VMEM((7, rows, length), F32),
-            pltpu.VMEM((8, rows, length), F32),
-        ]
-
-    change_xy = pl.pallas_call(
-        y_kernel,
-        out_shape=shape(field),
-        in_specs=[VMEM] * 4,
-        out_specs=VMEM,
-        scratch_shapes=scratch(16 + depth * (height + 8) + 80),
+            pltpu.VMEM((depth, height, length), F32),
+            pltpu.VMEM((7, rows + 6 * height, length), F32),
+            pltpu.VMEM((7, padded, length), F32),
+            pltpu.VMEM((padded, length), F32),
+            pltpu.VMEM((padded, length), F32),
+            pltpu.VMEM((7, padded, length), F32),
+            pltpu.VMEM((7, padded, length), F32),
+            pltpu.VMEM((8, padded, length), F32),
+            pltpu.SemaphoreType.DMA((4,)),
+            pltpu.SemaphoreType.DMA((4,)),
+            pltpu.SemaphoreType.DMA((4,)),
+        ],
         compiler_params=params(),
-        cost_estimate=cost(16),
-        name="sweep_y",
-    )(prim, y_below, y_above, change_x)
-
-    state_next = pl.pallas_call(
-        z_kernel,
-        out_shape=shape(field),
-        in_specs=[VMEM] * 6,
-        out_specs=VMEM,
-        scratch_shapes=scratch((depth + 6) * height),
-        compiler_params=params(),
-        cost_estimate=cost(15),
-        name="sweep_z",
-    )(prim, z_below, z_above, change_xy, flow_state, source)
+        cost_estimate=cost(24),
+        name="sweep_yz",
+    )(flow_state, change_x, source, z_below, z_above, y_below, y_above)
 
     fetched, state_next = lax.optimization_barrier((fetched, state_next))
     motion = pl.pallas_call(

time: 119 us -> 112 us (0.941)
  Pallas kernels: 82.1 us -> 71.1 us
  waiting for transfers between devices: 7.65 us -> 13.4 us
  local copies, waits for them, and re-layouts: 4.21 us -> 2.97 us
    pallas_call x5 -> x3, Pallas kernels: 55.6 us -> 44.6 us  [the longest x1 25.3 us: body(): pl.pallas_call(yz_kernel, out_shape=shape(field), in_specs=[ANY] * 5 + [V...]
    all_to_all x2, waiting for transfers between devices: 7.64 us -> 13.4 us  [exchange(): lax.all_to_all(values, ('gz', 'gy'), split_axis=0, concat_axis=0, tiled=T...]
    unnamed x12, local copies, waits for them, and re-layouts: 4.17 us -> 2.93 us
  transfers between devices with their start and end apart: 6 -> 6, of which waited for: 1 -> 1; matrix products, arithmetic and copies ran while one was open for 1% -> 1% of each run, Pallas kernels for 51% -> 45%
where the time goes in v4:
time: 112 us
  Pallas kernels  71.1 us (63%)
  starting transfers between devices  22.8 us (20%)
  waiting for transfers between devices  13.4 us (12%)
  local copies, waits for them, and re-layouts  2.97 us (3%)
    pallas_call x1, Pallas kernels, body(): pl.pallas_call(yz_kernel, out_shape=shape(field), in_specs=[ANY] * 5 + [V...  25.3 us
    all_to_all x2, starting transfers between devices, exchange(): lax.all_to_all(values, ('gz', 'gy'), split_axis=0, concat_axis=0, tiled=T...  18 us
    pallas_call x1, Pallas kernels, body(): pl.pallas_call(x_kernel, out_shape=(shape((7, rows, length)), shape((dept...  14.2 us
    all_to_all x2, waiting for transfers between devices, exchange(): lax.all_to_all(values, ('gz', 'gy'), split_axis=0, concat_axis=0, tiled=T...  13.4 us
    pallas_call x1, Pallas kernels, body(): pl.pallas_call(deposit_kernel, out_shape=shape((devices * PAIRS, 2, lengt...  12.5 us
    pallas_call x1, Pallas kernels, body(): pl.pallas_call(sample_kernel, out_shape=shape((2, blocks, 128)), in_specs...  7.14 us
    pallas_call x1, Pallas kernels, body(): pl.pallas_call(scatter_kernel, out_shape=shape((depth, height, length)),...  5.13 us
    pallas_call x1, Pallas kernels, body(): pl.pallas_call(functools.partial(serve_kernel, height=height), out_shape=...  5.11 us
  transfers between devices with their start and end apart: 6, of which 1 were waited for; matrix products, arithmetic and copies ran while one was open for 1% of the time, Pallas kernels for 45%

profile of v4, /device:TPU:1, one launch (start us, length us, event | category | flops | bytes accessed | tf_op | source)
XLA Modules:
  0.0 111.7 jit_solution(17185328906311546484)
XLA Ops:
  0.6 1.7 %slots.1 = (s32[2,256]{1,0:T(2,128)}, f32[128,128]{1,0:T(8,128)}) custom-call(s32[4,256]{1,0:T(4,128)} %bitcast.8), custom_call_target="tpu_custom_call" | custom-call | flops 2300000000 | bytes 1000 | tf_op jit(solution)/shard_map/slots/pallas_call | solution.py:522
  2.3 12.5 %deposit.1 = f32[2176,2,128]{2,1,0:T(2,128)} custom-call(s32[2,256]{1,0:T(2,128)} %get-tuple-element.19.slot_ref, f32[128,128]{1,0:T(8,128)} %get-tuple-element.20.wanted_ref, f32[3,256,128]{2,1,0:T(8,128)} %place_ref.3, f32[256,128]{1,0:T(8,128)} %radius_ref.3, f32[256,128]{1,0:T(8,128)} %speed_ref.3), custom_call_target="tpu_custom_call" | custom-call | flops 13799999488 | bytes 1000 | tf_op jit(solution)/shard_map/deposit/pallas_call | solution.py:530
  14.8 11.5 %all-to-all-start = ((f32[2176,2,128]{2,1,0:T(2,128)}), f32[2176,2,128]{2,1,0:T(2,128)S(1)}, u32[]{:S(2)}, u32[]{:S(2)}) async-start(f32[2176,2,128]{2,1,0:T(2,128)} %deposit.1), calls=%async_computation | async-start | bytes 4456448 | tf_op jit(solution)/shard_map/all_to_all | solution.py:511
  26.3 14.2 %sweep_x.1 = (f32[7,768,128]{2,1,0:T(8,128)}, f32[24,32,128]{2,1,0:T(8,128)}, f32[7,96,128]{2,1,0:T(8,128)}, f32[7,96,128]{2,1,0:T(8,128)}, f32[7,3,24,128]{3,2,1,0:T(8,128)}, /*index=5*/f32[7,3,24,128]{3,2,1,0:T(8,128)}) custom-call(f32[7,24,32,128]{3,2,1,0:T(8,128)} %flow_in.1), custom_call_target="tpu_custom_call" | custom-call | flops 16099999744 | bytes 1000 | tf_op jit(solution)/shard_map/sweep_x/pallas_call | solution.py:545
  40.6 1.7 %collective-permute-start = (f32[7,96,128]{2,1,0:T(8,128)}, f32[7,96,128]{2,1,0:T(8,128)S(1)}, u32[]{:S(2)}, u32[]{:S(2)}) collective-permute-start(f32[7,96,128]{2,1,0:T(8,128)} %get-tuple-element.29), channel_id=1, source_target_pairs={{0,4},{4,8},{8,12},{12,16},{16,20},{20,24},{24,28},{28,32},{32,36}... | collective-permute-start | bytes 1032200 | tf_op jit(solution)/shard_map/ppermute | solution.py:505
  42.3 0.0 collective-permute-start.1
  42.3 1.3 %collective-permute-start.2 = (f32[7,3,24,128]{3,2,1,0:T(8,128)}, f32[7,3,24,128]{3,2,1,0:T(8,128)S(1)}, u32[]{:S(2)}, u32[]{:S(2)}) collective-permute-start(f32[7,3,24,128]{3,2,1,0:T(8,128)} %get-tuple-element.31), channel_id=1, source_target_pairs={{0,1},{1,2},{2,3},{3,0},{4,5},{5,6},{6,7},{7,4},{8,9},{9,10},{10,1... | collective-permute-start | bytes 774152 | tf_op jit(solution)/shard_map/ppermute | solution.py:505
  43.6 1.8 %collective-permute-start.3 = (f32[7,3,24,128]{3,2,1,0:T(8,128)}, f32[7,3,24,128]{3,2,1,0:T(8,128)S(1)}, u32[]{:S(2)}, u32[]{:S(2)}) collective-permute-start(f32[7,3,24,128]{3,2,1,0:T(8,128)} %get-tuple-element.32), channel_id=1, source_target_pairs={{1,0},{2,1},{3,2},{0,3},{5,4},{6,5},{7,6},{4,7},{9,8},{10,9},{11,1... | collective-permute-start | bytes 774152 | tf_op jit(solution)/shard_map/ppermute | solution.py:506
  45.4 13.4 %all-to-all-done.returned_ref = f32[2176,2,128]{2,1,0:T(2,128)S(1)} async-done(((f32[2176,2,128]{2,1,0:T(2,128)}), f32[2176,2,128]{2,1,0:T(2,128)S(1)}, u32[]{:S(2)}, u32[]{:S(2)}) %all-to-all-start) | async-done | bytes 2228256 | tf_op jit(solution)/shard_map/all_to_all | solution.py:511
  58.7 0.0 copy-start
  58.8 0.7 convert_bitcast_fusion.asked_ref
  59.5 5.1 %serve.1 = f32[1024,4,128]{2,1,0:T(4,128)} custom-call(s32[128,8]{1,0:T(8,128)} %convert_bitcast_fusion.asked_ref, f32[768,128]{1,0:T(8,128)} %bitcast.9), custom_call_target="tpu_custom_call" | custom-call | flops 5750000128 | bytes 1000 | tf_op jit(solution)/shard_map/serve/pallas_call | solution.py:578
  64.6 0.0 copy-done
  64.6 6.5 %all-to-all-start.1 = ((f32[1024,4,128]{2,1,0:T(4,128)}), f32[1024,4,128]{2,1,0:T(4,128)S(1)}, u32[]{:S(2)}, u32[]{:S(2)}) async-start(f32[1024,4,128]{2,1,0:T(4,128)} %serve.1), calls=%async_computation.1 | async-start | bytes 4194304 | tf_op jit(solution)/shard_map/all_to_all | solution.py:511
  71.1 5.1 %scatter.1.source_in = f32[24,32,128]{2,1,0:T(8,128)} custom-call(s32[128,8]{1,0:T(8,128)} %convert_bitcast_fusion.asked_ref, f32[2176,2,128]{2,1,0:T(2,128)} %copy-done), custom_call_target="tpu_custom_call" | custom-call | flops 6899999744 | bytes 1000 | tf_op jit(solution)/shard_map/scatter/pallas_call | solution.py:590
  76.2 0.0 collective-permute-done.2.y_below_ref
  76.2 0.0 copy-start.4
  76.2 0.0 collective-permute-done.3.y_above_ref
  76.2 0.0 copy-start.5
  76.3 0.0 collective-permute-done.z_below_in
  76.3 0.0 copy-start.2
  76.3 0.0 collective-permute-done.1.z_above_in
  76.3 0.7 copy-done.4
  77.0 0.1 copy-done.5
  77.0 0.1 copy-done.2
  77.2 0.0 copy-start.3
  77.2 0.7 copy-done.3
  77.9 25.3 %sweep_yz.1 = f32[7,24,32,128]{3,2,1,0:T(8,128)} custom-call(f32[7,24,32,128]{3,2,1,0:T(8,128)} %flow_in.1, f32[7,768,128]{2,1,0:T(8,128)} %get-tuple-element.26.change_in, f32[24,32,128]{2,1,0:T(8,128)} %scatter.1.source_in, f32[7,96,128]{2,1,0:T(8,128)} %copy-done.2, f32[7,96,128]{2,1,0:T(8,128)} %copy-done.3, f32[7,3,24,128]{3,2,1,0:T(8,128)} %copy-done.4, ...), custom_call_target="tpu_custom_call" | custom-call | flops 27599998976 | bytes 1000 | tf_op jit(solution)/shard_map/sweep_yz/pallas_call | solution.py:602
  103.2 0.0 all-to-all-done.1.rows_ref
  103.2 0.0 copy-start.1
  103.2 1.3 %copy-done.1 = f32[1024,4,128]{2,1,0:T(4,128)} copy-done((f32[1024,4,128]{2,1,0:T(4,128)}, f32[1024,4,128]{2,1,0:T(4,128)S(1)}, u32[]{:S(2)}) %copy-start.1) | copy-done | bytes 2097176
  104.5 7.1 %sample.1 = f32[2,256,128]{2,1,0:T(8,128)} custom-call(s32[2,256]{1,0:T(2,128)} %get-tuple-element.19.slot_ref, f32[3,256,128]{2,1,0:T(8,128)} %place_ref.3, f32[256,128]{1,0:T(8,128)} %radius_ref.3, f32[256,128]{1,0:T(8,128)} %speed_ref.3, f32[256,128]{1,0:T(8,128)} %rest_ref.1, f32[1024,4,128]{2,1,0:T(4,128)} %copy-done.1), custom_call_target="tpu_custom_call" | custom-call | flops 8049999872 | bytes 1000 | tf_op jit(solution)/shard_map/sample/pallas_call | solution.py:628
  (1 shorter events, 0.0 us)
Async XLA Ops:
  14.8 43.9 %all-to-all-start = ((f32[2176,2,128]{2,1,0:T(2,128)}), f32[2176,2,128]{2,1,0:T(2,128)S(1)}, u32[]{:S(2)}, u32[]{:S(2)}) async-start(f32[2176,2,128]{2,1,0:T(2,128)} %deposit.1), calls=%async_computation | async-start | bytes 4456448 | tf_op jit(solution)/shard_map/all_to_all | solution.py:511
  40.6 35.7 %collective-permute-start = (f32[7,96,128]{2,1,0:T(8,128)}, f32[7,96,128]{2,1,0:T(8,128)S(1)}, u32[]{:S(2)}, u32[]{:S(2)}) collective-permute-start(f32[7,96,128]{2,1,0:T(8,128)} %get-tuple-element.29), channel_id=1, source_target_pairs={{0,4},{4,8},{8,12},{12,16},{16,20},{20,24},{24,28},{28,32},{32,36}... | collective-permute-start | bytes 1032200 | tf_op jit(solution)/shard_map/ppermute | solution.py:505
  42.3 34.0 %collective-permute-start.1 = (f32[7,96,128]{2,1,0:T(8,128)}, f32[7,96,128]{2,1,0:T(8,128)S(1)}, u32[]{:S(2)}, u32[]{:S(2)}) collective-permute-start(f32[7,96,128]{2,1,0:T(8,128)} %get-tuple-element.30), channel_id=1, source_target_pairs={{4,0},{8,4},{12,8},{16,12},{20,16},{24,20},{28,24},{32,28},{36,32}... | collective-permute-start | bytes 1032200 | tf_op jit(solution)/shard_map/ppermute | solution.py:506
  42.3 34.0 %collective-permute-start.2 = (f32[7,3,24,128]{3,2,1,0:T(8,128)}, f32[7,3,24,128]{3,2,1,0:T(8,128)S(1)}, u32[]{:S(2)}, u32[]{:S(2)}) collective-permute-start(f32[7,3,24,128]{3,2,1,0:T(8,128)} %get-tuple-element.31), channel_id=1, source_target_pairs={{0,1},{1,2},{2,3},{3,0},{4,5},{5,6},{6,7},{7,4},{8,9},{9,10},{10,1... | collective-permute-start | bytes 774152 | tf_op jit(solution)/shard_map/ppermute | solution.py:505
  43.6 32.6 %collective-permute-start.3 = (f32[7,3,24,128]{3,2,1,0:T(8,128)}, f32[7,3,24,128]{3,2,1,0:T(8,128)S(1)}, u32[]{:S(2)}, u32[]{:S(2)}) collective-permute-start(f32[7,3,24,128]{3,2,1,0:T(8,128)} %get-tuple-element.32), channel_id=1, source_target_pairs={{1,0},{2,1},{3,2},{0,3},{5,4},{6,5},{7,6},{4,7},{9,8},{10,9},{11,1... | collective-permute-start | bytes 774152 | tf_op jit(solution)/shard_map/ppermute | solution.py:506
  58.7 5.9 %copy-start = (f32[2176,2,128]{2,1,0:T(2,128)}, f32[2176,2,128]{2,1,0:T(2,128)S(1)}, u32[]{:S(2)}) copy-start(f32[2176,2,128]{2,1,0:T(2,128)S(1)} %all-to-all-done.returned_ref) | copy-start | bytes 6684676
  64.6 38.6 %all-to-all-start.1 = ((f32[1024,4,128]{2,1,0:T(4,128)}), f32[1024,4,128]{2,1,0:T(4,128)S(1)}, u32[]{:S(2)}, u32[]{:S(2)}) async-start(f32[1024,4,128]{2,1,0:T(4,128)} %serve.1), calls=%async_computation.1 | async-start | bytes 4194304 | tf_op jit(solution)/shard_map/all_to_all | solution.py:511
  76.2 0.7 copy-start.4
  76.2 0.8 copy-start.5
  76.3 0.9 copy-start.2
  77.2 0.7 copy-start.3
  103.2 1.3 %copy-start.1 = (f32[1024,4,128]{2,1,0:T(4,128)}, f32[1024,4,128]{2,1,0:T(4,128)S(1)}, u32[]{:S(2)}) copy-start(f32[1024,4,128]{2,1,0:T(4,128)S(1)} %all-to-all-done.1.rows_ref) | copy-start | bytes 6291460

commit v5 on v4

--- a/solution.py
+++ b/solution.py
@@ -31,8 +31,8 @@
 BF16 = jnp.bfloat16
 
 
-def params(mib=56):
-    return pltpu.CompilerParams(vmem_limit_bytes=mib * 2**20)
+def params(mib=63.75):
+    return pltpu.CompilerParams(vmem_limit_bytes=int(mib * 2**20))
 
 
 def shape(dims, dtype=F32):
@@ -55,8 +55,7 @@
     return lax.dot_general(left, right, (((1,), (0,)), ((), ())), preferred_element_type=F32)
 
 
-def slot_kernel(tiles_ref, slot_ref, wanted_ref, *, depth, height, across_gy):
-    devices = wanted_ref.shape[0]
+def find_slots(tiles_ref, devices, depth, height, across_gy):
     blocks = tiles_ref.shape[1]
     anchor = tiles_ref[0:1, :].astype(F32)
 
@@ -79,14 +78,14 @@
     rank = jnp.sum(onehot * before, axis=0, keepdims=True)
     rank = jnp.minimum(rank, HB - 1.0)
     rank_int = rank.astype(jnp.int32)
-    slot_ref[...] = jnp.concatenate([home * HB + rank_int, home * PAIRS + 2 * rank_int], axis=0)
-    chosen = lax.broadcasted_iota(jnp.int32, (wanted_ref.shape[1], blocks), 0).astype(F32) == rank
+    slot = jnp.concatenate([home * HB + rank_int, home * PAIRS + 2 * rank_int], axis=0)
+    chosen = lax.broadcasted_iota(jnp.int32, (128, blocks), 0).astype(F32) == rank
     level = jnp.where(chosen, level + 1.0, 0.0).astype(BF16)
     column = jnp.where(chosen, column, 0.0).astype(BF16)
     level = dot_nt(onehot_bf, level)
     column = dot_nt(onehot_bf, column)
     row = (level - 1.0) * float(height) + column
-    wanted_ref[...] = jnp.where(level > 0.0, row, -1.0)
+    return slot, jnp.where(level > 0.0, row, -1.0)
 
 
 def primitives(value):
@@ -230,7 +229,8 @@
     reach = -(-stride // 8) * 8
 
     def loop(begin, end, step):
-        lax.fori_loop(0, -(-(end - begin) // size), lambda k, c: step(pl.multiple_of(begin + k * size, 8), c), 0)
+        count = -(-(end - begin) // size)
+        lax.fori_loop(0, count, lambda k, c: step(pl.multiple_of(begin + k * size, 8), c), 0, unroll=4)
 
     for i in range(7):
 
@@ -278,12 +278,12 @@
         flux_ref[7, pl.ds(row, size)] = middle
         return carry
 
-    lax.fori_loop(0, count, faces, 0)
+    lax.fori_loop(0, count, faces, 0, unroll=2)
 
 
 def yz_kernel(
-    flow_in, change_in, source_in, z_below_in, z_above_in, y_below_ref, y_above_ref, next_out,
-    flow_ref, change_ref, source_ref, cells_z, cells_y, step_ref, curve_ref, left_ref, right_ref, flux_ref,
+    flow_in, change_in, source_in, z_below_in, z_above_in, y_below_in, y_above_in, next_out,
+    y_below_ref, y_above_ref, flow_ref, change_ref, source_ref, cells_z, cells_y, step_ref, curve_ref, left_ref, right_ref, flux_ref,
     flow_sems, side_sems, out_sems,
 ):
     depth, height = flow_ref.shape[1:3]
@@ -301,8 +301,12 @@
     above = pltpu.make_async_copy(z_above_in, cells_z.at[:, pl.ds(first_z + rows_z, first_z)], side_sems.at[1])
     change = pltpu.make_async_copy(change_in, change_ref, side_sems.at[2])
     source = pltpu.make_async_copy(source_in, source_ref, side_sems.at[3])
-    for copy in loads + [below, above, change, source]:
+    y_below = pltpu.make_async_copy(y_below_in, y_below_ref, side_sems.at[4])
+    y_above = pltpu.make_async_copy(y_above_in, y_above_ref, side_sems.at[5])
+    for copy in [y_below, y_above] + loads + [below, above, change, source]:
         copy.start()
+    y_below.wait()
+    y_above.wait()
 
     def fill(z, carry):
         base = pl.multiple_of(first_y + z * pitch, 8)
@@ -364,7 +368,10 @@
         save.wait()
 
 
-def serve_kernel(asked_ref, pressure_ref, served_ref, *, height):
+def serve_kernel(asked_ref, pressure_ref, served_out, served_ref, sems, *, height):
+    parts = sems.shape[0]
+    sources = asked_ref.shape[0] // parts
+
     def one(src, carry):
         for r in range(HB):
             row = jnp.maximum(asked_ref[src, r], 0)
@@ -373,7 +380,14 @@
             served_ref[slot, pl.ds(2, 2), :] = pressure_ref[pl.ds(row + height, 2), :]
         return carry
 
-    lax.fori_loop(0, asked_ref.shape[0], one, 0)
+    saves = []
+    for p in range(parts):
+        lax.fori_loop(p * sources, (p + 1) * sources, one, 0, unroll=4)
+        here = pl.ds(p * sources * HB, sources * HB)
+        saves.append(pltpu.make_async_copy(served_ref.at[here], served_out.at[here], sems.at[p]))
+        saves[-1].start()
+    for save in saves:
+        save.wait()
 
 
 def scatter_kernel(asked_ref, returned_ref, source_ref, *sums):
@@ -397,7 +411,7 @@
             total[far] = total[far] + returned_ref[pair + 1]
         return carry
 
-    lax.fori_loop(0, asked_ref.shape[0], one, 0)
+    lax.fori_loop(0, asked_ref.shape[0], one, 0, unroll=4)
 
     def collect(z, carry):
         rows = pl.ds(pl.multiple_of(z * height, 8), height)
@@ -422,8 +436,15 @@
     return across, across_sum, along
 
 
-def deposit_kernel(slot_ref, wanted_ref, place_ref, radius_ref, speed_ref, out_ref):
+def deposit_kernel(
+    tiles_ref, place_ref, radius_ref, speed_ref, slot_out, out_ref, slot_ref, wanted_ref, sem, *, depth, height, across_gy
+):
     length = out_ref.shape[2]
+    slot, wanted = find_slots(tiles_ref, wanted_ref.shape[0], depth, height, across_gy)
+    slot_out[...] = slot
+    wanted_ref[...] = wanted
+    move = pltpu.make_async_copy(slot_out, slot_ref, sem)
+    move.start()
     upper = lax.broadcasted_iota(jnp.int32, (8, 128), 0) < 4
 
     def ask(k, carry):
@@ -433,6 +454,7 @@
         return carry
 
     lax.fori_loop(0, wanted_ref.shape[0] // 8, ask, 0)
+    move.wait()
 
     def one(block):
         across, across_sum, along = block_weights(place_ref, block, length)
@@ -445,13 +467,15 @@
         share_hi = share.astype(BF16).astype(F32)
         both = jnp.where(upper, share_hi, share - share_hi).astype(BF16)
         only = jnp.where(upper, share_hi, 0.0).astype(BF16)
-        result = dot_nt(both, along_hi) + dot_nt(only, along_lo)
+        result = dot_nt(
+            jnp.concatenate([both, only], axis=1), jnp.concatenate([along_hi, along_lo], axis=1)
+        )
         result = result[0:4] + result[4:8]
         pair = slot_ref[1, block]
         out_ref[pair] = result[0:2]
         out_ref[pair + 1] = result[2:4]
 
-    group = math.gcd(radius_ref.shape[0], 32)
+    group = math.gcd(radius_ref.shape[0], 64)
 
     def several(k, carry):
         for j in range(group):
@@ -461,9 +485,27 @@
     lax.fori_loop(0, radius_ref.shape[0] // group, several, 0)
 
 
-def sample_kernel(slot_ref, place_ref, radius_ref, speed_ref, rest_ref, rows_ref, motion_ref, sampled_ref):
+def sample_kernel(
+    slot_ref, place_ref, radius_ref, speed_ref, rest_ref, fetched_in, motion_ref, sampled_ref, scale_ref, rows_ref, sem
+):
     length = rows_ref.shape[2]
+    load = pltpu.make_async_copy(fetched_in, rows_ref, sem)
+    load.start()
     upper = lax.broadcasted_iota(jnp.int32, (8, 128), 0) < 4
+
+    radius, speed, ratio = radius_ref[...], speed_ref[...], rest_ref[...]
+    inv_radius = 1.0 / radius
+    gas = (1.0 + 2.0 * surface_tension / (ratio * radius)) * jnp.exp(3.0 * polytropic * jnp.log(ratio))
+    wall = gas - (2.0 * surface_tension + 4.0 * liquid_viscosity * speed) * inv_radius
+    gas_rate = -3.0 * polytropic * gas * speed * inv_radius
+    mach = speed / liquid_sound
+    scale = time_step / ((1.0 - mach) * radius)
+    motion_ref[0] = radius + time_step * speed
+    motion_ref[1] = speed + scale * (
+        (1.0 + mach) * wall + radius * gas_rate / liquid_sound - 1.5 * (1.0 - mach / 3.0) * speed * speed
+    )
+    scale_ref[...] = scale * (1.0 + mach)
+    load.wait()
 
     def one(block):
         across, across_sum, along = block_weights(place_ref, block, length)
@@ -476,7 +518,7 @@
         total = jnp.sum(across * result[0:8], axis=0, keepdims=True)
         sampled_ref[pl.ds(block, 1), :] = pressure_mid + total * inverse(across_sum * result[8:9])
 
-    group = math.gcd(radius_ref.shape[0], 32)
+    group = math.gcd(radius_ref.shape[0], 64)
 
     def several(k, carry):
         for j in range(group):
@@ -484,20 +526,7 @@
         return carry
 
     lax.fori_loop(0, radius_ref.shape[0] // group, several, 0)
-
-    radius, speed, ratio = radius_ref[...], speed_ref[...], rest_ref[...]
-    inv_radius = 1.0 / radius
-    gas = (1.0 + 2.0 * surface_tension / (ratio * radius)) * jnp.exp(3.0 * polytropic * jnp.log(ratio))
-    wall = gas - (2.0 * surface_tension + 4.0 * liquid_viscosity * speed) * inv_radius
-    gas_rate = -3.0 * polytropic * gas * speed * inv_radius
-    mach = speed / liquid_sound
-    acceleration = (
-        (1.0 + mach) * (wall - sampled_ref[...])
-        + radius * gas_rate / liquid_sound
-        - 1.5 * (1.0 - mach / 3.0) * speed * speed
-    ) / ((1.0 - mach) * radius)
-    motion_ref[0] = radius + time_step * speed
-    motion_ref[1] = speed + time_step * acceleration
+    motion_ref[1] = motion_ref[1] - scale_ref[...] * sampled_ref[...]
 
 
 def shift_both(low_layers, high_layers, axis):
@@ -519,23 +548,20 @@
     slots = devices * HB
     field = (7, depth, height, length)
 
-    slot, wanted = pl.pallas_call(
-        functools.partial(slot_kernel, depth=depth, height=height, across_gy=across_gy),
-        out_shape=(shape((2, blocks), jnp.int32), shape((devices, 128))),
-        in_specs=[VMEM],
+    slot, outgoing = pl.pallas_call(
+        functools.partial(deposit_kernel, depth=depth, height=height, across_gy=across_gy),
+        out_shape=(shape((2, blocks), jnp.int32), shape((devices * PAIRS, 2, length))),
+        in_specs=[VMEM] * 4,
         out_specs=(VMEM, VMEM),
-        cost_estimate=cost(2),
-        name="slots",
-    )(block_tiles.T)
-    outgoing = pl.pallas_call(
-        deposit_kernel,
-        out_shape=shape((devices * PAIRS, 2, length)),
-        in_specs=[SMEM] + [VMEM] * 4,
-        out_specs=VMEM,
+        scratch_shapes=[
+            pltpu.SMEM((2, blocks), jnp.int32),
+            pltpu.VMEM((devices, 128), F32),
+            pltpu.SemaphoreType.DMA,
+        ],
         compiler_params=params(),
-        cost_estimate=cost(12),
+        cost_estimate=cost(10),
         name="deposit",
-    )(slot, wanted, bubble_place, bubble_radius, bubble_speed)
+    )(block_tiles.T, bubble_place, bubble_radius, bubble_speed)
     returned = exchange(outgoing)
 
     flow_state, _ = lax.optimization_barrier((flow_state, outgoing))
@@ -579,8 +605,9 @@
         functools.partial(serve_kernel, height=height),
         out_shape=shape((slots, 4, length)),
         in_specs=[SMEM, VMEM],
-        out_specs=VMEM,
-        compiler_params=params(),
+        out_specs=ANY,
+        scratch_shapes=[pltpu.VMEM((slots, 4, length), F32), pltpu.SemaphoreType.DMA((4,))],
+        compiler_params=params(56),
         cost_estimate=cost(5),
         name="serve",
     )(asked, pressure.reshape(rows, length))
@@ -593,7 +620,7 @@
         in_specs=[SMEM, VMEM],
         out_specs=VMEM,
         scratch_shapes=[pltpu.VMEM(((depth + 2) * height, length), F32)] * 4,
-        compiler_params=params(),
+        compiler_params=params(56),
         cost_estimate=cost(6),
         name="scatter",
     )(asked, returned)
@@ -602,9 +629,11 @@
     state_next = pl.pallas_call(
         yz_kernel,
         out_shape=shape(field),
-        in_specs=[ANY] * 5 + [VMEM] * 2,
+        in_specs=[ANY] * 7,
         out_specs=ANY,
         scratch_shapes=[
+            pltpu.VMEM((7, 3, depth, length), F32),
+            pltpu.VMEM((7, 3, depth, length), F32),
             pltpu.VMEM(field, F32),
             pltpu.VMEM((7, rows, length), F32),
             pltpu.VMEM((depth, height, length), F32),
@@ -616,7 +645,7 @@
             pltpu.VMEM((7, padded, length), F32),
             pltpu.VMEM((8, padded, length), F32),
             pltpu.SemaphoreType.DMA((4,)),
-            pltpu.SemaphoreType.DMA((4,)),
+            pltpu.SemaphoreType.DMA((6,)),
             pltpu.SemaphoreType.DMA((4,)),
         ],
         compiler_params=params(),
@@ -628,9 +657,14 @@
     motion = pl.pallas_call(
         sample_kernel,
         out_shape=shape((2, blocks, 128)),
-        in_specs=[SMEM] + [VMEM] * 5,
+        in_specs=[SMEM] + [VMEM] * 4 + [ANY],
         out_specs=VMEM,
-        scratch_shapes=[pltpu.VMEM((blocks, 128), F32)],
+        scratch_shapes=[
+            pltpu.VMEM((blocks, 128), F32),
+            pltpu.VMEM((blocks, 128), F32),
+            pltpu.VMEM((slots, 4, length), F32),
+            pltpu.SemaphoreType.DMA,
+        ],
         compiler_params=params(),
         cost_estimate=cost(7),
         name="sample",

time: 112 us -> 105 us (0.938)
  Pallas kernels: 71.1 us -> 60.8 us
  waiting for transfers between devices: 13.4 us -> 17.8 us
  local copies, waits for them, and re-layouts: 2.97 us -> 0.95 us
    pallas_call x3 -> x2, Pallas kernels: 39.5 us -> 31.4 us  [the longest x1 22 us: body(): pl.pallas_call(yz_kernel, out_shape=shape(field), in_specs=[ANY] * 7, out...]
    all_to_all x2, waiting for transfers between devices: 13.4 us -> 17.8 us  [exchange(): lax.all_to_all(values, ('gz', 'gy'), split_axis=0, concat_axis=0, tiled=T...]
    unnamed x12 -> x0, local copies, waits for them, and re-layouts: 2.93 us -> none
  transfers between devices with their start and end apart: 6 -> 6, of which waited for: 1 -> 2; matrix products, arithmetic and copies ran while one was open for 1% -> 2% of each run, Pallas kernels for 45% -> 42%
where the time goes in v5:
time: 105 us
  Pallas kernels  60.8 us (58%)
  starting transfers between devices  23.6 us (22%)
  waiting for transfers between devices  17.8 us (17%)
    pallas_call x1, Pallas kernels, body(): pl.pallas_call(yz_kernel, out_shape=shape(field), in_specs=[ANY] * 7, out...  22 us
    all_to_all x2, starting transfers between devices, exchange(): lax.all_to_all(values, ('gz', 'gy'), split_axis=0, concat_axis=0, tiled=T...  18.9 us
    all_to_all x2, waiting for transfers between devices, exchange(): lax.all_to_all(values, ('gz', 'gy'), split_axis=0, concat_axis=0, tiled=T...  17.8 us
    pallas_call x1, Pallas kernels, body(): pl.pallas_call(x_kernel, out_shape=(shape((7, rows, length)), shape((dept...  13.2 us
    pallas_call x1, Pallas kernels, body(): pl.pallas_call(functools.partial(deposit_kernel, depth=depth, height=heig...  9.46 us
    pallas_call x1, Pallas kernels, body(): pl.pallas_call(sample_kernel, out_shape=shape((2, blocks, 128)), in_specs...  7.46 us
    pallas_call x1, Pallas kernels, body(): pl.pallas_call(scatter_kernel, out_shape=shape((depth, height, length)),...  4.54 us
    pallas_call x1, Pallas kernels, body(): pl.pallas_call(functools.partial(serve_kernel, height=height), out_shape=...  4.13 us
  transfers between devices with their start and end apart: 6, of which 2 were waited for; matrix products, arithmetic and copies ran while one was open for 2% of the time, Pallas kernels for 42%

profile of v5, /device:TPU:1, one launch (start us, length us, event | category | flops | bytes accessed | tf_op | source)
XLA Modules:
  0.0 104.6 jit_solution(9412830466833469410)
XLA Ops:
  0.6 9.5 %deposit.1 = (s32[2,256]{1,0:T(2,128)}, f32[2176,2,128]{2,1,0:T(2,128)}) custom-call(s32[4,256]{1,0:T(4,128)} %bitcast.7, f32[3,256,128]{2,1,0:T(8,128)} %place_ref.3, f32[256,128]{1,0:T(8,128)} %radius_ref.3, f32[256,128]{1,0:T(8,128)} %speed_ref.3), custom_call_target="tpu_custom_call" | custom-call | flops 11500000256 | bytes 1000 | tf_op jit(solution)/shard_map/deposit/pallas_call | solution.py:551
  10.1 11.9 %all-to-all-start = ((f32[2176,2,128]{2,1,0:T(2,128)}), f32[2176,2,128]{2,1,0:T(2,128)}, u32[]{:S(2)}, u32[]{:S(2)}) async-start(f32[2176,2,128]{2,1,0:T(2,128)} %get-tuple-element.19), calls=%async_computation | async-start | bytes 4456448 | tf_op jit(solution)/shard_map/all_to_all | solution.py:540
  22.0 13.2 %sweep_x.1 = (f32[7,768,128]{2,1,0:T(8,128)}, f32[24,32,128]{2,1,0:T(8,128)}, f32[7,96,128]{2,1,0:T(8,128)}, f32[7,96,128]{2,1,0:T(8,128)}, f32[7,3,24,128]{3,2,1,0:T(8,128)}, /*index=5*/f32[7,3,24,128]{3,2,1,0:T(8,128)}) custom-call(f32[7,24,32,128]{3,2,1,0:T(8,128)} %flow_in.1), custom_call_target="tpu_custom_call" | custom-call | flops 16099999744 | bytes 1000 | tf_op jit(solution)/shard_map/sweep_x/pallas_call | solution.py:571
  35.2 1.7 %collective-permute-start = (f32[7,96,128]{2,1,0:T(8,128)}, f32[7,96,128]{2,1,0:T(8,128)}, u32[]{:S(2)}, u32[]{:S(2)}) collective-permute-start(f32[7,96,128]{2,1,0:T(8,128)} %get-tuple-element.28), channel_id=1, source_target_pairs={{0,4},{4,8},{8,12},{12,16},{16,20},{20,24},{24,28},{28,32},{32,36}... | collective-permute-start | bytes 1032200 | tf_op jit(solution)/shard_map/ppermute | solution.py:534
  36.9 0.0 collective-permute-start.1
  36.9 1.3 %collective-permute-start.2 = (f32[7,3,24,128]{3,2,1,0:T(8,128)}, f32[7,3,24,128]{3,2,1,0:T(8,128)}, u32[]{:S(2)}, u32[]{:S(2)}) collective-permute-start(f32[7,3,24,128]{3,2,1,0:T(8,128)} %get-tuple-element.30), channel_id=1, source_target_pairs={{0,1},{1,2},{2,3},{3,0},{4,5},{5,6},{6,7},{7,4},{8,9},{9,10},{10,1... | collective-permute-start | bytes 774152 | tf_op jit(solution)/shard_map/ppermute | solution.py:534
  38.3 1.8 %collective-permute-start.3 = (f32[7,3,24,128]{3,2,1,0:T(8,128)}, f32[7,3,24,128]{3,2,1,0:T(8,128)}, u32[]{:S(2)}, u32[]{:S(2)}) collective-permute-start(f32[7,3,24,128]{3,2,1,0:T(8,128)} %get-tuple-element.31), channel_id=1, source_target_pairs={{1,0},{2,1},{3,2},{0,3},{5,4},{6,5},{7,6},{4,7},{9,8},{10,9},{11,1... | collective-permute-start | bytes 774152 | tf_op jit(solution)/shard_map/ppermute | solution.py:535
  40.0 14.1 %all-to-all-done.returned_ref = f32[2176,2,128]{2,1,0:T(2,128)} async-done(((f32[2176,2,128]{2,1,0:T(2,128)}), f32[2176,2,128]{2,1,0:T(2,128)}, u32[]{:S(2)}, u32[]{:S(2)}) %all-to-all-start) | async-done | bytes 2228256 | tf_op jit(solution)/shard_map/all_to_all | solution.py:540
  54.1 0.9 slice.4
  55.1 0.6 convert_bitcast_fusion.asked_ref
  55.7 4.1 %serve.1 = f32[1024,4,128]{2,1,0:T(4,128)} custom-call(s32[128,8]{1,0:T(8,128)} %convert_bitcast_fusion.asked_ref, f32[768,128]{1,0:T(8,128)} %bitcast.8), custom_call_target="tpu_custom_call" | custom-call | flops 5750000128 | bytes 1000 | tf_op jit(solution)/shard_map/serve/pallas_call | solution.py:604
  59.8 7.0 %all-to-all-start.1 = ((f32[1024,4,128]{2,1,0:T(4,128)}), f32[1024,4,128]{2,1,0:T(4,128)}, u32[]{:S(2)}, u32[]{:S(2)}) async-start(f32[1024,4,128]{2,1,0:T(4,128)} %serve.1), calls=%async_computation.1 | async-start | bytes 4194304 | tf_op jit(solution)/shard_map/all_to_all | solution.py:540
  66.8 4.5 %scatter.1.source_in = f32[24,32,128]{2,1,0:T(8,128)} custom-call(s32[128,8]{1,0:T(8,128)} %convert_bitcast_fusion.asked_ref, f32[2176,2,128]{2,1,0:T(2,128)} %all-to-all-done.returned_ref), custom_call_target="tpu_custom_call" | custom-call | flops 6899999744 | bytes 1000 | tf_op jit(solution)/shard_map/scatter/pallas_call | solution.py:617
  71.3 0.0 collective-permute-done.2.y_below_in
  71.4 0.0 collective-permute-done.3.y_above_in
  71.4 0.0 collective-permute-done.z_below_in
  71.4 0.0 collective-permute-done.1.z_above_in
  71.4 22.0 %sweep_yz.1 = f32[7,24,32,128]{3,2,1,0:T(8,128)} custom-call(f32[7,24,32,128]{3,2,1,0:T(8,128)} %flow_in.1, f32[7,768,128]{2,1,0:T(8,128)} %get-tuple-element.25.change_in, f32[24,32,128]{2,1,0:T(8,128)} %scatter.1.source_in, f32[7,96,128]{2,1,0:T(8,128)} %collective-permute-done.z_below_in, f32[7,96,128]{2,1,0:T(8,128)} %collective-permute-done.1.z_above_in, ...), custom_call_target="tpu_custom_call" | custom-call | flops 27599998976 | bytes 1000 | tf_op jit(solution)/shard_map/sweep_yz/pallas_call | solution.py:629
  93.3 3.7 %all-to-all-done.1.fetched_in = f32[1024,4,128]{2,1,0:T(4,128)} async-done(((f32[1024,4,128]{2,1,0:T(4,128)}), f32[1024,4,128]{2,1,0:T(4,128)}, u32[]{:S(2)}, u32[]{:S(2)}) %all-to-all-start.1) | async-done | bytes 2097184 | tf_op jit(solution)/shard_map/all_to_all | solution.py:540
  97.0 7.5 %sample.1 = f32[2,256,128]{2,1,0:T(8,128)} custom-call(s32[2,256]{1,0:T(2,128)} %get-tuple-element.33.slot_ref, f32[3,256,128]{2,1,0:T(8,128)} %place_ref.3, f32[256,128]{1,0:T(8,128)} %radius_ref.3, f32[256,128]{1,0:T(8,128)} %speed_ref.3, f32[256,128]{1,0:T(8,128)} %rest_ref.1, f32[1024,4,128]{2,1,0:T(4,128)} %all-to-all-done.1.fetched_in), custom_call_target="tpu_custom_call" | custom-call | flops 8049999872 | bytes 1000 | tf_op jit(solution)/shard_map/sample/pallas_call | solution.py:657
Async XLA Ops:
  10.1 44.0 %all-to-all-start = ((f32[2176,2,128]{2,1,0:T(2,128)}), f32[2176,2,128]{2,1,0:T(2,128)}, u32[]{:S(2)}, u32[]{:S(2)}) async-start(f32[2176,2,128]{2,1,0:T(2,128)} %get-tuple-element.19), calls=%async_computation | async-start | bytes 4456448 | tf_op jit(solution)/shard_map/all_to_all | solution.py:540
  35.2 36.1 %collective-permute-start = (f32[7,96,128]{2,1,0:T(8,128)}, f32[7,96,128]{2,1,0:T(8,128)}, u32[]{:S(2)}, u32[]{:S(2)}) collective-permute-start(f32[7,96,128]{2,1,0:T(8,128)} %get-tuple-element.28), channel_id=1, source_target_pairs={{0,4},{4,8},{8,12},{12,16},{16,20},{20,24},{24,28},{28,32},{32,36}... | collective-permute-start | bytes 1032200 | tf_op jit(solution)/shard_map/ppermute | solution.py:534
  36.9 34.4 %collective-permute-start.1 = (f32[7,96,128]{2,1,0:T(8,128)}, f32[7,96,128]{2,1,0:T(8,128)}, u32[]{:S(2)}, u32[]{:S(2)}) collective-permute-start(f32[7,96,128]{2,1,0:T(8,128)} %get-tuple-element.29), channel_id=1, source_target_pairs={{4,0},{8,4},{12,8},{16,12},{20,16},{24,20},{28,24},{32,28},{36,32}... | collective-permute-start | bytes 1032200 | tf_op jit(solution)/shard_map/ppermute | solution.py:535
  36.9 34.4 %collective-permute-start.2 = (f32[7,3,24,128]{3,2,1,0:T(8,128)}, f32[7,3,24,128]{3,2,1,0:T(8,128)}, u32[]{:S(2)}, u32[]{:S(2)}) collective-permute-start(f32[7,3,24,128]{3,2,1,0:T(8,128)} %get-tuple-element.30), channel_id=1, source_target_pairs={{0,1},{1,2},{2,3},{3,0},{4,5},{5,6},{6,7},{7,4},{8,9},{9,10},{10,1... | collective-permute-start | bytes 774152 | tf_op jit(solution)/shard_map/ppermute | solution.py:534
  38.3 33.1 %collective-permute-start.3 = (f32[7,3,24,128]{3,2,1,0:T(8,128)}, f32[7,3,24,128]{3,2,1,0:T(8,128)}, u32[]{:S(2)}, u32[]{:S(2)}) collective-permute-start(f32[7,3,24,128]{3,2,1,0:T(8,128)} %get-tuple-element.31), channel_id=1, source_target_pairs={{1,0},{2,1},{3,2},{0,3},{5,4},{6,5},{7,6},{4,7},{9,8},{10,9},{11,1... | collective-permute-start | bytes 774152 | tf_op jit(solution)/shard_map/ppermute | solution.py:535
  59.8 37.2 %all-to-all-start.1 = ((f32[1024,4,128]{2,1,0:T(4,128)}), f32[1024,4,128]{2,1,0:T(4,128)}, u32[]{:S(2)}, u32[]{:S(2)}) async-start(f32[1024,4,128]{2,1,0:T(4,128)} %serve.1), calls=%async_computation.1 | async-start | bytes 4194304 | tf_op jit(solution)/shard_map/all_to_all | solution.py:540

commit v6 on v5

--- a/solution.py
+++ b/solution.py
@@ -424,27 +424,38 @@
     lax.fori_loop(0, depth, collect, 0)
 
 
-def block_weights(place_ref, block, length):
+half_log2e = 0.5 * math.log2(math.e)
+
+
+def gaussian(distance):
+    return jnp.exp2(-half_log2e * (distance * distance))
+
+
+def across_rows(place_ref, block):
     lateral = lax.broadcasted_iota(jnp.int32, (8, 128), 0) % 4
     shift_z = (lateral // 2).astype(F32) - place_ref[0, pl.ds(block, 1), :]
     shift_y = (lateral % 2).astype(F32) - place_ref[1, pl.ds(block, 1), :]
-    across = jnp.exp(-0.5 * (shift_z * shift_z + shift_y * shift_y))
-    across_sum = 0.5 * jnp.sum(across, axis=0, keepdims=True)
-    offset = place_ref[2, pl.ds(block, 1), :] * float(length - 1)
-    shift_x = lax.broadcasted_iota(jnp.int32, (length, 128), 0).astype(F32) - offset
-    along = jnp.exp2((-0.5 * math.log2(math.e)) * (shift_x * shift_x))
-    return across, across_sum, along
+    return jnp.exp2(-half_log2e * (shift_z * shift_z + shift_y * shift_y))
+
+
+def across_total(place_ref):
+    place_z, place_y = place_ref[0], place_ref[1]
+    return (gaussian(place_z) + gaussian(1.0 - place_z)) * (gaussian(place_y) + gaussian(1.0 - place_y))
 
 
 def deposit_kernel(
-    tiles_ref, place_ref, radius_ref, speed_ref, slot_out, out_ref, slot_ref, wanted_ref, sem, *, depth, height, across_gy
+    tiles_ref, place_ref, radius_ref, speed_ref, slot_out, out_ref,
+    slot_ref, wanted_ref, rate_ref, sem, *, depth, height, across_gy,
 ):
     length = out_ref.shape[2]
+    blocks = radius_ref.shape[0]
     slot, wanted = find_slots(tiles_ref, wanted_ref.shape[0], depth, height, across_gy)
     slot_out[...] = slot
     wanted_ref[...] = wanted
     move = pltpu.make_async_copy(slot_out, slot_ref, sem)
     move.start()
+    radius = radius_ref[...]
+    rate_ref[...] = 4.0 * math.pi * radius * radius * speed_ref[...] * inverse(across_total(place_ref))
     upper = lax.broadcasted_iota(jnp.int32, (8, 128), 0) < 4
 
     def ask(k, carry):
@@ -457,11 +468,11 @@
     move.wait()
 
     def one(block):
-        across, across_sum, along = block_weights(place_ref, block, length)
+        across = across_rows(place_ref, block)
+        offset = place_ref[2, pl.ds(block, 1), :] * float(length - 1)
+        along = gaussian(lax.broadcasted_iota(jnp.int32, (length, 128), 0).astype(F32) - offset)
         along_sum = jnp.sum(along, axis=0, keepdims=True)
-        radius = radius_ref[pl.ds(block, 1), :]
-        rate = 4.0 * math.pi * radius * radius * speed_ref[pl.ds(block, 1), :]
-        share = across * (rate * inverse(across_sum * along_sum))
+        share = across * (rate_ref[pl.ds(block, 1), :] * inverse(along_sum))
         along_hi = along.astype(BF16)
         along_lo = (along - along_hi.astype(F32)).astype(BF16)
         share_hi = share.astype(BF16).astype(F32)
@@ -475,19 +486,21 @@
         out_ref[pair] = result[0:2]
         out_ref[pair + 1] = result[2:4]
 
-    group = math.gcd(radius_ref.shape[0], 64)
+    size = math.gcd(blocks, 64)
 
     def several(k, carry):
-        for j in range(group):
-            one(k * group + j)
-        return carry
-
-    lax.fori_loop(0, radius_ref.shape[0] // group, several, 0)
+        for j in range(size):
+            one(k * size + j)
+        return carry
+
+    lax.fori_loop(0, blocks // size, several, 0)
 
 
 def sample_kernel(
-    slot_ref, place_ref, radius_ref, speed_ref, rest_ref, fetched_in, motion_ref, sampled_ref, scale_ref, rows_ref, sem
+    slot_ref, place_ref, radius_ref, speed_ref, rest_ref, fetched_in, motion_ref,
+    total_ref, width_ref, scale_ref, across_ref, rows_ref, sem,
 ):
+    blocks = radius_ref.shape[0]
     length = rows_ref.shape[2]
     load = pltpu.make_async_copy(fetched_in, rows_ref, sem)
     load.start()
@@ -502,31 +515,38 @@
     scale = time_step / ((1.0 - mach) * radius)
     motion_ref[0] = radius + time_step * speed
     motion_ref[1] = speed + scale * (
-        (1.0 + mach) * wall + radius * gas_rate / liquid_sound - 1.5 * (1.0 - mach / 3.0) * speed * speed
+        (1.0 + mach) * (wall - pressure_mid)
+        + radius * gas_rate / liquid_sound
+        - 1.5 * (1.0 - mach / 3.0) * speed * speed
     )
     scale_ref[...] = scale * (1.0 + mach)
+    across_ref[...] = across_total(place_ref)
     load.wait()
 
     def one(block):
-        across, across_sum, along = block_weights(place_ref, block, length)
         value = rows_ref[slot_ref[0, block]] - pressure_mid
         value = jnp.concatenate([value, value], axis=0)
         high = value.astype(BF16).astype(F32)
         both = jnp.where(upper, high, value - high)
         both = jnp.concatenate([both, jnp.ones_like(both)], axis=0).astype(BF16)
+        offset = place_ref[2, pl.ds(block, 1), :] * float(length - 1)
+        along = gaussian(lax.broadcasted_iota(jnp.int32, (length, 128), 0).astype(F32) - offset)
         result = dot_nn(both, along.astype(BF16))
-        total = jnp.sum(across * result[0:8], axis=0, keepdims=True)
-        sampled_ref[pl.ds(block, 1), :] = pressure_mid + total * inverse(across_sum * result[8:9])
-
-    group = math.gcd(radius_ref.shape[0], 64)
+        total_ref[pl.ds(pl.multiple_of(block * 8, 8), 8)] = across_rows(place_ref, block) * result[0:8]
+        width_ref[pl.ds(block, 1), :] = result[8:9]
+
+    size = math.gcd(blocks, 64)
 
     def several(k, carry):
-        for j in range(group):
-            one(k * group + j)
-        return carry
-
-    lax.fori_loop(0, radius_ref.shape[0] // group, several, 0)
-    motion_ref[1] = motion_ref[1] - scale_ref[...] * sampled_ref[...]
+        for j in range(size):
+            one(k * size + j)
+        return carry
+
+    lax.fori_loop(0, blocks // size, several, 0)
+    total = total_ref[pl.ds(0, blocks, stride=8), :]
+    for row in range(1, 8):
+        total = total + total_ref[pl.ds(row, blocks, stride=8), :]
+    motion_ref[1] = motion_ref[1] - scale_ref[...] * (total * inverse(across_ref[...] * width_ref[...]))
 
 
 def shift_both(low_layers, high_layers, axis):
@@ -550,12 +570,16 @@
 
     slot, outgoing = pl.pallas_call(
         functools.partial(deposit_kernel, depth=depth, height=height, across_gy=across_gy),
-        out_shape=(shape((2, blocks), jnp.int32), shape((devices * PAIRS, 2, length))),
+        out_shape=(
+            shape((2, blocks), jnp.int32),
+            shape((devices * PAIRS, 2, length)),
+        ),
         in_specs=[VMEM] * 4,
         out_specs=(VMEM, VMEM),
         scratch_shapes=[
             pltpu.SMEM((2, blocks), jnp.int32),
             pltpu.VMEM((devices, 128), F32),
+            pltpu.VMEM((blocks, 128), F32),
             pltpu.SemaphoreType.DMA,
         ],
         compiler_params=params(),
@@ -592,7 +616,7 @@
             pltpu.SemaphoreType.DMA((groups,)),
             pltpu.SemaphoreType.DMA((groups,)),
         ],
-        compiler_params=params(),
+        compiler_params=params(56),
         cost_estimate=cost(14),
         name="sweep_x",
     )(flow_state)
@@ -660,6 +684,8 @@
         in_specs=[SMEM] + [VMEM] * 4 + [ANY],
         out_specs=VMEM,
         scratch_shapes=[
+            pltpu.VMEM((blocks * 8, 128), F32),
+            pltpu.VMEM((blocks, 128), F32),
             pltpu.VMEM((blocks, 128), F32),
             pltpu.VMEM((blocks, 128), F32),
             pltpu.VMEM((slots, 4, length), F32),

time: 105 us -> 103 us (0.981)
  transfers between devices with their start and end apart: 6 -> 6, of which waited for: 2 -> 2; matrix products, arithmetic and copies ran while one was open for 2% -> 1% of each run, Pallas kernels for 42% -> 43%
where the time goes in v6:
time: 103 us
  Pallas kernels  60.3 us (59%)
  starting transfers between devices  23.2 us (23%)
  waiting for transfers between devices  17.8 us (17%)
    pallas_call x1, Pallas kernels, body(): pl.pallas_call(yz_kernel, out_shape=shape(field), in_specs=[ANY] * 7, out...  22 us
    all_to_all x2, starting transfers between devices, exchange(): lax.all_to_all(values, ('gz', 'gy'), split_axis=0, concat_axis=0, tiled=T...  18.5 us
    all_to_all x2, waiting for transfers between devices, exchange(): lax.all_to_all(values, ('gz', 'gy'), split_axis=0, concat_axis=0, tiled=T...  17.7 us
    pallas_call x1, Pallas kernels, body(): pl.pallas_call(x_kernel, out_shape=(shape((7, rows, length)), shape((dept...  13.2 us
    pallas_call x1, Pallas kernels, body(): pl.pallas_call(functools.partial(deposit_kernel, depth=depth, height=heig...  9.12 us
    pallas_call x1, Pallas kernels, body(): pl.pallas_call(sample_kernel, out_shape=shape((2, blocks, 128)), in_specs...  7.12 us
    pallas_call x1, Pallas kernels, body(): pl.pallas_call(scatter_kernel, out_shape=shape((depth, height, length)),...  4.83 us
    pallas_call x1, Pallas kernels, body(): pl.pallas_call(functools.partial(serve_kernel, height=height), out_shape=...  4.07 us
  transfers between devices with their start and end apart: 6, of which 2 were waited for; matrix products, arithmetic and copies ran while one was open for 1% of the time, Pallas kernels for 43%

profile of v6, /device:TPU:1, one launch (start us, length us, event | category | flops | bytes accessed | tf_op | source)
XLA Modules:
  0.0 103.0 jit_solution(11525783192889499875)
XLA Ops:
  0.6 9.1 %deposit.1 = (s32[2,256]{1,0:T(2,128)}, f32[2176,2,128]{2,1,0:T(2,128)}) custom-call(s32[4,256]{1,0:T(4,128)} %bitcast.8, f32[3,256,128]{2,1,0:T(8,128)} %place_ref.3, f32[256,128]{1,0:T(8,128)} %radius_ref.3, f32[256,128]{1,0:T(8,128)} %speed_ref.3), custom_call_target="tpu_custom_call" | custom-call | flops 11500000256 | bytes 1000 | tf_op jit(solution)/shard_map/deposit/pallas_call | solution.py:571
  9.8 11.5 %all-to-all-start = ((f32[2176,2,128]{2,1,0:T(2,128)}), f32[2176,2,128]{2,1,0:T(2,128)S(1)}, u32[]{:S(2)}, u32[]{:S(2)}) async-start(f32[2176,2,128]{2,1,0:T(2,128)} %get-tuple-element.19), calls=%async_computation | async-start | bytes 4456448 | tf_op jit(solution)/shard_map/all_to_all | solution.py:560
  21.3 13.2 %sweep_x.1 = (f32[7,768,128]{2,1,0:T(8,128)}, f32[24,32,128]{2,1,0:T(8,128)}, f32[7,96,128]{2,1,0:T(8,128)}, f32[7,96,128]{2,1,0:T(8,128)}, f32[7,3,24,128]{3,2,1,0:T(8,128)}, /*index=5*/f32[7,3,24,128]{3,2,1,0:T(8,128)}) custom-call(f32[7,24,32,128]{3,2,1,0:T(8,128)} %flow_in.1), custom_call_target="tpu_custom_call" | custom-call | flops 16099999744 | bytes 1000 | tf_op jit(solution)/shard_map/sweep_x/pallas_call | solution.py:595
  34.5 1.7 %collective-permute-start = (f32[7,96,128]{2,1,0:T(8,128)}, f32[7,96,128]{2,1,0:T(8,128)}, u32[]{:S(2)}, u32[]{:S(2)}) collective-permute-start(f32[7,96,128]{2,1,0:T(8,128)} %get-tuple-element.28), channel_id=1, source_target_pairs={{0,4},{4,8},{8,12},{12,16},{16,20},{20,24},{24,28},{28,32},{32,36}... | collective-permute-start | bytes 1032200 | tf_op jit(solution)/shard_map/ppermute | solution.py:554
  36.2 0.0 collective-permute-start.1
  36.2 1.3 %collective-permute-start.2 = (f32[7,3,24,128]{3,2,1,0:T(8,128)}, f32[7,3,24,128]{3,2,1,0:T(8,128)}, u32[]{:S(2)}, u32[]{:S(2)}) collective-permute-start(f32[7,3,24,128]{3,2,1,0:T(8,128)} %get-tuple-element.30), channel_id=1, source_target_pairs={{0,1},{1,2},{2,3},{3,0},{4,5},{5,6},{6,7},{7,4},{8,9},{9,10},{10,1... | collective-permute-start | bytes 774152 | tf_op jit(solution)/shard_map/ppermute | solution.py:554
  37.6 1.8 %collective-permute-start.3 = (f32[7,3,24,128]{3,2,1,0:T(8,128)}, f32[7,3,24,128]{3,2,1,0:T(8,128)}, u32[]{:S(2)}, u32[]{:S(2)}) collective-permute-start(f32[7,3,24,128]{3,2,1,0:T(8,128)} %get-tuple-element.31), channel_id=1, source_target_pairs={{1,0},{2,1},{3,2},{0,3},{5,4},{6,5},{7,6},{4,7},{9,8},{10,9},{11,1... | collective-permute-start | bytes 774152 | tf_op jit(solution)/shard_map/ppermute | solution.py:555
  39.3 14.4 %all-to-all-done.returned_ref = f32[2176,2,128]{2,1,0:T(2,128)S(1)} async-done(((f32[2176,2,128]{2,1,0:T(2,128)}), f32[2176,2,128]{2,1,0:T(2,128)S(1)}, u32[]{:S(2)}, u32[]{:S(2)}) %all-to-all-start) | async-done | bytes 2228256 | tf_op jit(solution)/shard_map/all_to_all | solution.py:560
  53.7 0.0 copy-start
  53.7 0.7 convert_bitcast_fusion.asked_ref
  54.4 4.1 %serve.1 = f32[1024,4,128]{2,1,0:T(4,128)} custom-call(s32[128,8]{1,0:T(8,128)} %convert_bitcast_fusion.asked_ref, f32[768,128]{1,0:T(8,128)} %bitcast.9), custom_call_target="tpu_custom_call" | custom-call | flops 5750000128 | bytes 1000 | tf_op jit(solution)/shard_map/serve/pallas_call | solution.py:628
  58.5 0.0 copy-done
  58.5 7.0 %all-to-all-start.1 = ((f32[1024,4,128]{2,1,0:T(4,128)}), f32[1024,4,128]{2,1,0:T(4,128)}, u32[]{:S(2)}, u32[]{:S(2)}) async-start(f32[1024,4,128]{2,1,0:T(4,128)} %serve.1), calls=%async_computation.1 | async-start | bytes 4194304 | tf_op jit(solution)/shard_map/all_to_all | solution.py:560
  65.5 4.8 %scatter.1.source_in = f32[24,32,128]{2,1,0:T(8,128)} custom-call(s32[128,8]{1,0:T(8,128)} %convert_bitcast_fusion.asked_ref, f32[2176,2,128]{2,1,0:T(2,128)} %copy-done), custom_call_target="tpu_custom_call" | custom-call | flops 6899999744 | bytes 1000 | tf_op jit(solution)/shard_map/scatter/pallas_call | solution.py:641
  70.3 0.0 collective-permute-done.2.y_below_in
  70.3 0.0 collective-permute-done.3.y_above_in
  70.3 0.0 collective-permute-done.z_below_in
  70.3 0.0 collective-permute-done.1.z_above_in
  70.3 22.0 %sweep_yz.1 = f32[7,24,32,128]{3,2,1,0:T(8,128)} custom-call(f32[7,24,32,128]{3,2,1,0:T(8,128)} %flow_in.1, f32[7,768,128]{2,1,0:T(8,128)} %get-tuple-element.25.change_in, f32[24,32,128]{2,1,0:T(8,128)} %scatter.1.source_in, f32[7,96,128]{2,1,0:T(8,128)} %collective-permute-done.z_below_in, f32[7,96,128]{2,1,0:T(8,128)} %collective-permute-done.1.z_above_in, ...), custom_call_target="tpu_custom_call" | custom-call | flops 27599998976 | bytes 1000 | tf_op jit(solution)/shard_map/sweep_yz/pallas_call | solution.py:653
  92.3 3.4 %all-to-all-done.1.fetched_in = f32[1024,4,128]{2,1,0:T(4,128)} async-done(((f32[1024,4,128]{2,1,0:T(4,128)}), f32[1024,4,128]{2,1,0:T(4,128)}, u32[]{:S(2)}, u32[]{:S(2)}) %all-to-all-start.1) | async-done | bytes 2097184 | tf_op jit(solution)/shard_map/all_to_all | solution.py:560
  95.7 7.1 %sample.1 = f32[2,256,128]{2,1,0:T(8,128)} custom-call(s32[2,256]{1,0:T(2,128)} %get-tuple-element.33.slot_ref, f32[3,256,128]{2,1,0:T(8,128)} %place_ref.3, f32[256,128]{1,0:T(8,128)} %radius_ref.3, f32[256,128]{1,0:T(8,128)} %speed_ref.3, f32[256,128]{1,0:T(8,128)} %rest_ref.1, f32[1024,4,128]{2,1,0:T(4,128)} %all-to-all-done.1.fetched_in), custom_call_target="tpu_custom_call" | custom-call | flops 8049999872 | bytes 1000 | tf_op jit(solution)/shard_map/sample/pallas_call | solution.py:681
  (1 shorter events, 0.0 us)
Async XLA Ops:
  9.8 43.9 %all-to-all-start = ((f32[2176,2,128]{2,1,0:T(2,128)}), f32[2176,2,128]{2,1,0:T(2,128)S(1)}, u32[]{:S(2)}, u32[]{:S(2)}) async-start(f32[2176,2,128]{2,1,0:T(2,128)} %get-tuple-element.19), calls=%async_computation | async-start | bytes 4456448 | tf_op jit(solution)/shard_map/all_to_all | solution.py:560
  34.5 35.8 %collective-permute-start = (f32[7,96,128]{2,1,0:T(8,128)}, f32[7,96,128]{2,1,0:T(8,128)}, u32[]{:S(2)}, u32[]{:S(2)}) collective-permute-start(f32[7,96,128]{2,1,0:T(8,128)} %get-tuple-element.28), channel_id=1, source_target_pairs={{0,4},{4,8},{8,12},{12,16},{16,20},{20,24},{24,28},{28,32},{32,36}... | collective-permute-start | bytes 1032200 | tf_op jit(solution)/shard_map/ppermute | solution.py:554
  36.2 34.1 %collective-permute-start.1 = (f32[7,96,128]{2,1,0:T(8,128)}, f32[7,96,128]{2,1,0:T(8,128)}, u32[]{:S(2)}, u32[]{:S(2)}) collective-permute-start(f32[7,96,128]{2,1,0:T(8,128)} %get-tuple-element.29), channel_id=1, source_target_pairs={{4,0},{8,4},{12,8},{16,12},{20,16},{24,20},{28,24},{32,28},{36,32}... | collective-permute-start | bytes 1032200 | tf_op jit(solution)/shard_map/ppermute | solution.py:555
  36.2 34.1 %collective-permute-start.2 = (f32[7,3,24,128]{3,2,1,0:T(8,128)}, f32[7,3,24,128]{3,2,1,0:T(8,128)}, u32[]{:S(2)}, u32[]{:S(2)}) collective-permute-start(f32[7,3,24,128]{3,2,1,0:T(8,128)} %get-tuple-element.30), channel_id=1, source_target_pairs={{0,1},{1,2},{2,3},{3,0},{4,5},{5,6},{6,7},{7,4},{8,9},{9,10},{10,1... | collective-permute-start | bytes 774152 | tf_op jit(solution)/shard_map/ppermute | solution.py:554
  37.6 32.8 %collective-permute-start.3 = (f32[7,3,24,128]{3,2,1,0:T(8,128)}, f32[7,3,24,128]{3,2,1,0:T(8,128)}, u32[]{:S(2)}, u32[]{:S(2)}) collective-permute-start(f32[7,3,24,128]{3,2,1,0:T(8,128)} %get-tuple-element.31), channel_id=1, source_target_pairs={{1,0},{2,1},{3,2},{0,3},{5,4},{6,5},{7,6},{4,7},{9,8},{10,9},{11,1... | collective-permute-start | bytes 774152 | tf_op jit(solution)/shard_map/ppermute | solution.py:555
  53.7 4.8 %copy-start = (f32[2176,2,128]{2,1,0:T(2,128)}, f32[2176,2,128]{2,1,0:T(2,128)S(1)}, u32[]{:S(2)}) copy-start(f32[2176,2,128]{2,1,0:T(2,128)S(1)} %all-to-all-done.returned_ref) | copy-start | bytes 6684676
  58.5 37.2 %all-to-all-start.1 = ((f32[1024,4,128]{2,1,0:T(4,128)}), f32[1024,4,128]{2,1,0:T(4,128)}, u32[]{:S(2)}, u32[]{:S(2)}) async-start(f32[1024,4,128]{2,1,0:T(4,128)} %serve.1), calls=%async_computation.1 | async-start | bytes 4194304 | tf_op jit(solution)/shard_map/all_to_all | solution.py:560

commit v7 on v6

--- a/solution.py
+++ b/solution.py
@@ -496,16 +496,7 @@
     lax.fori_loop(0, blocks // size, several, 0)
 
 
-def sample_kernel(
-    slot_ref, place_ref, radius_ref, speed_ref, rest_ref, fetched_in, motion_ref,
-    total_ref, width_ref, scale_ref, across_ref, rows_ref, sem,
-):
-    blocks = radius_ref.shape[0]
-    length = rows_ref.shape[2]
-    load = pltpu.make_async_copy(fetched_in, rows_ref, sem)
-    load.start()
-    upper = lax.broadcasted_iota(jnp.int32, (8, 128), 0) < 4
-
+def ready_kernel(place_ref, radius_ref, speed_ref, rest_ref, ready_ref):
     radius, speed, ratio = radius_ref[...], speed_ref[...], rest_ref[...]
     inv_radius = 1.0 / radius
     gas = (1.0 + 2.0 * surface_tension / (ratio * radius)) * jnp.exp(3.0 * polytropic * jnp.log(ratio))
@@ -513,15 +504,20 @@
     gas_rate = -3.0 * polytropic * gas * speed * inv_radius
     mach = speed / liquid_sound
     scale = time_step / ((1.0 - mach) * radius)
-    motion_ref[0] = radius + time_step * speed
-    motion_ref[1] = speed + scale * (
+    ready_ref[0] = radius + time_step * speed
+    ready_ref[1] = speed + scale * (
         (1.0 + mach) * (wall - pressure_mid)
         + radius * gas_rate / liquid_sound
         - 1.5 * (1.0 - mach / 3.0) * speed * speed
     )
-    scale_ref[...] = scale * (1.0 + mach)
-    across_ref[...] = across_total(place_ref)
-    load.wait()
+    ready_ref[2] = scale * (1.0 + mach) * inverse(across_total(place_ref))
+
+
+def sample_kernel(slot_ref, place_ref, ready_ref, rows_ref, motion_ref, total_ref, width_ref):
+    blocks = width_ref.shape[0]
+    length = rows_ref.shape[2]
+    upper = lax.broadcasted_iota(jnp.int32, (8, 128), 0) < 4
+    motion_ref[0] = ready_ref[0]
 
     def one(block):
         value = rows_ref[slot_ref[0, block]] - pressure_mid
@@ -546,7 +542,7 @@
     total = total_ref[pl.ds(0, blocks, stride=8), :]
     for row in range(1, 8):
         total = total + total_ref[pl.ds(row, blocks, stride=8), :]
-    motion_ref[1] = motion_ref[1] - scale_ref[...] * (total * inverse(across_ref[...] * width_ref[...]))
+    motion_ref[1] = ready_ref[1] - ready_ref[2] * (total * inverse(width_ref[...]))
 
 
 def shift_both(low_layers, high_layers, axis):
@@ -588,7 +584,7 @@
     )(block_tiles.T, bubble_place, bubble_radius, bubble_speed)
     returned = exchange(outgoing)
 
-    flow_state, _ = lax.optimization_barrier((flow_state, outgoing))
+    flow_state, rest_ratio, _ = lax.optimization_barrier((flow_state, rest_ratio, outgoing))
     rows = depth * height
     groups = rows // 128
     turned = 16 + groups * (length + 8) + 80
@@ -622,7 +618,16 @@
     )(flow_state)
     y_below, y_above = shift_both(y_low, y_high, "gy")
     z_below, z_above = shift_both(z_low, z_high, "gz")
-    returned, change_x = lax.optimization_barrier((returned, change_x))
+    ready = pl.pallas_call(
+        ready_kernel,
+        out_shape=shape((3, blocks, 128)),
+        in_specs=[VMEM] * 4,
+        out_specs=VMEM,
+        compiler_params=params(56),
+        cost_estimate=cost(2),
+        name="ready",
+    )(bubble_place, bubble_radius, bubble_speed, rest_ratio)
+    returned, change_x, ready = lax.optimization_barrier((returned, change_x, ready))
 
     asked = returned.reshape(devices, PAIRS, 2, length)[:, 2 * HB, 0, :HB].astype(jnp.int32)
     served = pl.pallas_call(
@@ -681,20 +686,13 @@
     motion = pl.pallas_call(
         sample_kernel,
         out_shape=shape((2, blocks, 128)),
-        in_specs=[SMEM] + [VMEM] * 4 + [ANY],
+        in_specs=[SMEM] + [VMEM] * 3,
         out_specs=VMEM,
-        scratch_shapes=[
-            pltpu.VMEM((blocks * 8, 128), F32),
-            pltpu.VMEM((blocks, 128), F32),
-            pltpu.VMEM((blocks, 128), F32),
-            pltpu.VMEM((blocks, 128), F32),
-            pltpu.VMEM((slots, 4, length), F32),
-            pltpu.SemaphoreType.DMA,
-        ],
+        scratch_shapes=[pltpu.VMEM((blocks * 8, 128), F32), pltpu.VMEM((blocks, 128), F32)],
         compiler_params=params(),
         cost_estimate=cost(7),
         name="sample",
-    )(slot, bubble_place, bubble_radius, bubble_speed, rest_ratio, fetched)
+    )(slot, bubble_place, ready, fetched)
     return state_next, source, motion
 
 

time: 103 us -> 102 us (level)
  waiting for transfers between devices: 17.8 us -> 15.6 us
  Pallas kernels: 60.3 us -> 61.6 us
    pallas_call x0 -> x1, Pallas kernels: none -> 2.16 us  [body(): pl.pallas_call(ready_kernel, out_shape=shape((3, blocks, 128)), in_specs=...]
    all_to_all x2, waiting for transfers between devices: 17.7 us -> 15.6 us  [exchange(): lax.all_to_all(values, ('gz', 'gy'), split_axis=0, concat_axis=0, tiled=T...]
  transfers between devices with their start and end apart: 6 -> 6, of which waited for: 2 -> 2; matrix products, arithmetic and copies ran while one was open for 1% -> 1% of each run, Pallas kernels for 43% -> 45%
where the time goes in v7:
time: 102 us
  Pallas kernels  61.6 us (60%)
  starting transfers between devices  23.2 us (23%)
  waiting for transfers between devices  15.6 us (15%)
    pallas_call x1, Pallas kernels, body(): pl.pallas_call(yz_kernel, out_shape=shape(field), in_specs=[ANY] * 7, out...  22 us
    all_to_all x2, starting transfers between devices, exchange(): lax.all_to_all(values, ('gz', 'gy'), split_axis=0, concat_axis=0, tiled=T...  18.5 us
    all_to_all x2, waiting for transfers between devices, exchange(): lax.all_to_all(values, ('gz', 'gy'), split_axis=0, concat_axis=0, tiled=T...  15.6 us
    pallas_call x1, Pallas kernels, body(): pl.pallas_call(x_kernel, out_shape=(shape((7, rows, length)), shape((dept...  13.2 us
    pallas_call x1, Pallas kernels, body(): pl.pallas_call(functools.partial(deposit_kernel, depth=depth, height=heig...  9.12 us
    pallas_call x1, Pallas kernels, body(): pl.pallas_call(sample_kernel, out_shape=shape((2, blocks, 128)), in_specs...  6.25 us
    pallas_call x1, Pallas kernels, body(): pl.pallas_call(scatter_kernel, out_shape=shape((depth, height, length)),...  4.83 us
    pallas_call x1, Pallas kernels, body(): pl.pallas_call(functools.partial(serve_kernel, height=height), out_shape=...  4.07 us
  transfers between devices with their start and end apart: 6, of which 2 were waited for; matrix products, arithmetic and copies ran while one was open for 1% of the time, Pallas kernels for 45%

profile of v7, /device:TPU:1, one launch (start us, length us, event | category | flops | bytes accessed | tf_op | source)
XLA Modules:
  0.0 102.0 jit_solution(13909975306373821215)
XLA Ops:
  0.6 9.1 %deposit.1 = (s32[2,256]{1,0:T(2,128)}, f32[2176,2,128]{2,1,0:T(2,128)}) custom-call(s32[4,256]{1,0:T(4,128)} %bitcast.8, f32[3,256,128]{2,1,0:T(8,128)} %place_ref.5, f32[256,128]{1,0:T(8,128)} %radius_ref.3, f32[256,128]{1,0:T(8,128)} %speed_ref.3), custom_call_target="tpu_custom_call" | custom-call | flops 11500000256 | bytes 1000 | tf_op jit(solution)/shard_map/deposit/pallas_call | solution.py:567
  9.8 11.5 %all-to-all-start = ((f32[2176,2,128]{2,1,0:T(2,128)}), f32[2176,2,128]{2,1,0:T(2,128)S(1)}, u32[]{:S(2)}, u32[]{:S(2)}) async-start(f32[2176,2,128]{2,1,0:T(2,128)} %get-tuple-element.21), calls=%async_computation | async-start | bytes 4456448 | tf_op jit(solution)/shard_map/all_to_all | solution.py:556
  21.3 13.2 %sweep_x.1 = (f32[7,768,128]{2,1,0:T(8,128)}, f32[24,32,128]{2,1,0:T(8,128)}, f32[7,96,128]{2,1,0:T(8,128)}, f32[7,96,128]{2,1,0:T(8,128)}, f32[7,3,24,128]{3,2,1,0:T(8,128)}, /*index=5*/f32[7,3,24,128]{3,2,1,0:T(8,128)}) custom-call(f32[7,24,32,128]{3,2,1,0:T(8,128)} %flow_in.1), custom_call_target="tpu_custom_call" | custom-call | flops 16099999744 | bytes 1000 | tf_op jit(solution)/shard_map/sweep_x/pallas_call | solution.py:591
  34.5 1.7 %collective-permute-start = (f32[7,96,128]{2,1,0:T(8,128)}, f32[7,96,128]{2,1,0:T(8,128)}, u32[]{:S(2)}, u32[]{:S(2)}) collective-permute-start(f32[7,96,128]{2,1,0:T(8,128)} %get-tuple-element.31), channel_id=1, source_target_pairs={{0,4},{4,8},{8,12},{12,16},{16,20},{20,24},{24,28},{28,32},{32,36}... | collective-permute-start | bytes 1032200 | tf_op jit(solution)/shard_map/ppermute | solution.py:550
  36.2 0.0 collective-permute-start.1
  36.2 1.3 %collective-permute-start.2 = (f32[7,3,24,128]{3,2,1,0:T(8,128)}, f32[7,3,24,128]{3,2,1,0:T(8,128)}, u32[]{:S(2)}, u32[]{:S(2)}) collective-permute-start(f32[7,3,24,128]{3,2,1,0:T(8,128)} %get-tuple-element.33), channel_id=1, source_target_pairs={{0,1},{1,2},{2,3},{3,0},{4,5},{5,6},{6,7},{7,4},{8,9},{9,10},{10,1... | collective-permute-start | bytes 774152 | tf_op jit(solution)/shard_map/ppermute | solution.py:550
  37.5 1.8 %collective-permute-start.3 = (f32[7,3,24,128]{3,2,1,0:T(8,128)}, f32[7,3,24,128]{3,2,1,0:T(8,128)}, u32[]{:S(2)}, u32[]{:S(2)}) collective-permute-start(f32[7,3,24,128]{3,2,1,0:T(8,128)} %get-tuple-element.34), channel_id=1, source_target_pairs={{1,0},{2,1},{3,2},{0,3},{5,4},{6,5},{7,6},{4,7},{9,8},{10,9},{11,1... | collective-permute-start | bytes 774152 | tf_op jit(solution)/shard_map/ppermute | solution.py:551
  39.3 2.2 %ready.1.ready_ref = f32[3,256,128]{2,1,0:T(8,128)} custom-call(f32[3,256,128]{2,1,0:T(8,128)} %place_ref.5, f32[256,128]{1,0:T(8,128)} %radius_ref.3, f32[256,128]{1,0:T(8,128)} %speed_ref.3, f32[256,128]{1,0:T(8,128)} %rest_ref), custom_call_target="tpu_custom_call" | custom-call | flops 2300000000 | bytes 1000 | tf_op jit(solution)/shard_map/ready/pallas_call | solution.py:621
  41.5 12.2 %all-to-all-done.returned_ref = f32[2176,2,128]{2,1,0:T(2,128)S(1)} async-done(((f32[2176,2,128]{2,1,0:T(2,128)}), f32[2176,2,128]{2,1,0:T(2,128)S(1)}, u32[]{:S(2)}, u32[]{:S(2)}) %all-to-all-start) | async-done | bytes 2228256 | tf_op jit(solution)/shard_map/all_to_all | solution.py:556
  53.7 0.0 copy-start
  53.7 0.7 convert_bitcast_fusion.asked_ref
  54.4 4.1 %serve.1 = f32[1024,4,128]{2,1,0:T(4,128)} custom-call(s32[128,8]{1,0:T(8,128)} %convert_bitcast_fusion.asked_ref, f32[768,128]{1,0:T(8,128)} %bitcast.9), custom_call_target="tpu_custom_call" | custom-call | flops 5750000128 | bytes 1000 | tf_op jit(solution)/shard_map/serve/pallas_call | solution.py:633
  58.5 0.0 copy-done
  58.5 7.0 %all-to-all-start.1 = ((f32[1024,4,128]{2,1,0:T(4,128)}), f32[1024,4,128]{2,1,0:T(4,128)}, u32[]{:S(2)}, u32[]{:S(2)}) async-start(f32[1024,4,128]{2,1,0:T(4,128)} %serve.1), calls=%async_computation.1 | async-start | bytes 4194304 | tf_op jit(solution)/shard_map/all_to_all | solution.py:556
  65.5 4.8 %scatter.1.source_in = f32[24,32,128]{2,1,0:T(8,128)} custom-call(s32[128,8]{1,0:T(8,128)} %convert_bitcast_fusion.asked_ref, f32[2176,2,128]{2,1,0:T(2,128)} %copy-done), custom_call_target="tpu_custom_call" | custom-call | flops 6899999744 | bytes 1000 | tf_op jit(solution)/shard_map/scatter/pallas_call | solution.py:646
  70.3 0.0 collective-permute-done.2.y_below_in
  70.3 0.0 collective-permute-done.3.y_above_in
  70.3 0.0 collective-permute-done.z_below_in
  70.3 0.0 collective-permute-done.1.z_above_in
  70.4 22.0 %sweep_yz.1 = f32[7,24,32,128]{3,2,1,0:T(8,128)} custom-call(f32[7,24,32,128]{3,2,1,0:T(8,128)} %flow_in.1, f32[7,768,128]{2,1,0:T(8,128)} %get-tuple-element.28.change_in, f32[24,32,128]{2,1,0:T(8,128)} %scatter.1.source_in, f32[7,96,128]{2,1,0:T(8,128)} %collective-permute-done.z_below_in, f32[7,96,128]{2,1,0:T(8,128)} %collective-permute-done.1.z_above_in, ...), custom_call_target="tpu_custom_call" | custom-call | flops 27599998976 | bytes 1000 | tf_op jit(solution)/shard_map/sweep_yz/pallas_call | solution.py:658
  92.3 3.4 %all-to-all-done.1.rows_ref = f32[1024,4,128]{2,1,0:T(4,128)} async-done(((f32[1024,4,128]{2,1,0:T(4,128)}), f32[1024,4,128]{2,1,0:T(4,128)}, u32[]{:S(2)}, u32[]{:S(2)}) %all-to-all-start.1) | async-done | bytes 2097184 | tf_op jit(solution)/shard_map/all_to_all | solution.py:556
  95.7 6.3 %sample.1 = f32[2,256,128]{2,1,0:T(8,128)} custom-call(s32[2,256]{1,0:T(2,128)} %get-tuple-element.36.slot_ref, f32[3,256,128]{2,1,0:T(8,128)} %place_ref.5, f32[3,256,128]{2,1,0:T(8,128)} %ready.1.ready_ref, f32[1024,4,128]{2,1,0:T(4,128)} %all-to-all-done.1.rows_ref), custom_call_target="tpu_custom_call" | custom-call | flops 8049999872 | bytes 1000 | tf_op jit(solution)/shard_map/sample/pallas_call | solution.py:686
  (1 shorter events, 0.0 us)
Async XLA Ops:
  9.8 43.9 %all-to-all-start = ((f32[2176,2,128]{2,1,0:T(2,128)}), f32[2176,2,128]{2,1,0:T(2,128)S(1)}, u32[]{:S(2)}, u32[]{:S(2)}) async-start(f32[2176,2,128]{2,1,0:T(2,128)} %get-tuple-element.21), calls=%async_computation | async-start | bytes 4456448 | tf_op jit(solution)/shard_map/all_to_all | solution.py:556
  34.5 35.8 %collective-permute-start = (f32[7,96,128]{2,1,0:T(8,128)}, f32[7,96,128]{2,1,0:T(8,128)}, u32[]{:S(2)}, u32[]{:S(2)}) collective-permute-start(f32[7,96,128]{2,1,0:T(8,128)} %get-tuple-element.31), channel_id=1, source_target_pairs={{0,4},{4,8},{8,12},{12,16},{16,20},{20,24},{24,28},{28,32},{32,36}... | collective-permute-start | bytes 1032200 | tf_op jit(solution)/shard_map/ppermute | solution.py:550
  36.2 34.1 %collective-permute-start.1 = (f32[7,96,128]{2,1,0:T(8,128)}, f32[7,96,128]{2,1,0:T(8,128)}, u32[]{:S(2)}, u32[]{:S(2)}) collective-permute-start(f32[7,96,128]{2,1,0:T(8,128)} %get-tuple-element.32), channel_id=1, source_target_pairs={{4,0},{8,4},{12,8},{16,12},{20,16},{24,20},{28,24},{32,28},{36,32}... | collective-permute-start | bytes 1032200 | tf_op jit(solution)/shard_map/ppermute | solution.py:551
  36.2 34.1 %collective-permute-start.2 = (f32[7,3,24,128]{3,2,1,0:T(8,128)}, f32[7,3,24,128]{3,2,1,0:T(8,128)}, u32[]{:S(2)}, u32[]{:S(2)}) collective-permute-start(f32[7,3,24,128]{3,2,1,0:T(8,128)} %get-tuple-element.33), channel_id=1, source_target_pairs={{0,1},{1,2},{2,3},{3,0},{4,5},{5,6},{6,7},{7,4},{8,9},{9,10},{10,1... | collective-permute-start | bytes 774152 | tf_op jit(solution)/shard_map/ppermute | solution.py:550
  37.5 32.8 %collective-permute-start.3 = (f32[7,3,24,128]{3,2,1,0:T(8,128)}, f32[7,3,24,128]{3,2,1,0:T(8,128)}, u32[]{:S(2)}, u32[]{:S(2)}) collective-permute-start(f32[7,3,24,128]{3,2,1,0:T(8,128)} %get-tuple-element.34), channel_id=1, source_target_pairs={{1,0},{2,1},{3,2},{0,3},{5,4},{6,5},{7,6},{4,7},{9,8},{10,9},{11,1... | collective-permute-start | bytes 774152 | tf_op jit(solution)/shard_map/ppermute | solution.py:551
  53.7 4.9 %copy-start = (f32[2176,2,128]{2,1,0:T(2,128)}, f32[2176,2,128]{2,1,0:T(2,128)S(1)}, u32[]{:S(2)}) copy-start(f32[2176,2,128]{2,1,0:T(2,128)S(1)} %all-to-all-done.returned_ref) | copy-start | bytes 6684676
  58.5 37.2 %all-to-all-start.1 = ((f32[1024,4,128]{2,1,0:T(4,128)}), f32[1024,4,128]{2,1,0:T(4,128)}, u32[]{:S(2)}, u32[]{:S(2)}) async-start(f32[1024,4,128]{2,1,0:T(4,128)} %serve.1), calls=%async_computation.1 | async-start | bytes 4194304 | tf_op jit(solution)/shard_map/all_to_all | solution.py:556

commit v8 on v7

--- a/solution.py
+++ b/solution.py
@@ -486,7 +486,7 @@
         out_ref[pair] = result[0:2]
         out_ref[pair + 1] = result[2:4]
 
-    size = math.gcd(blocks, 64)
+    size = math.gcd(blocks, 128)
 
     def several(k, carry):
         for j in range(size):
@@ -531,7 +531,7 @@
         total_ref[pl.ds(pl.multiple_of(block * 8, 8), 8)] = across_rows(place_ref, block) * result[0:8]
         width_ref[pl.ds(block, 1), :] = result[8:9]
 
-    size = math.gcd(blocks, 64)
+    size = math.gcd(blocks, 256)
 
     def several(k, carry):
         for j in range(size):

time: 102 us -> 102 us (level)
  transfers between devices with their start and end apart: 6 -> 6, of which waited for: 2 -> 2; matrix products, arithmetic and copies ran while one was open for 1% -> 1% of each run, Pallas kernels for 45% -> 46%
where the time goes in v8:
time: 102 us; the launch traced here: 101 us
  Pallas kernels  61 us (60%)
  starting transfers between devices  23.2 us (23%)
  waiting for transfers between devices  15.6 us (15%)
    pallas_call x1, Pallas kernels, body(): pl.pallas_call(yz_kernel, out_shape=shape(field), in_specs=[ANY] * 7, out...  22 us
    all_to_all x2, starting transfers between devices, exchange(): lax.all_to_all(values, ('gz', 'gy'), split_axis=0, concat_axis=0, tiled=T...  18.5 us
    all_to_all x2, waiting for transfers between devices, exchange(): lax.all_to_all(values, ('gz', 'gy'), split_axis=0, concat_axis=0, tiled=T...  15.6 us
    pallas_call x1, Pallas kernels, body(): pl.pallas_call(x_kernel, out_shape=(shape((7, rows, length)), shape((dept...  13.2 us
    pallas_call x1, Pallas kernels, body(): pl.pallas_call(functools.partial(deposit_kernel, depth=depth, height=heig...  8.88 us
    pallas_call x1, Pallas kernels, body(): pl.pallas_call(sample_kernel, out_shape=shape((2, blocks, 128)), in_specs...  5.86 us
    pallas_call x1, Pallas kernels, body(): pl.pallas_call(scatter_kernel, out_shape=shape((depth, height, length)),...  4.83 us
    pallas_call x1, Pallas kernels, body(): pl.pallas_call(functools.partial(serve_kernel, height=height), out_shape=...  4.07 us
  transfers between devices with their start and end apart: 6, of which 2 were waited for; matrix products, arithmetic and copies ran while one was open for 1% of the time, Pallas kernels for 46%

profile of v8, /device:TPU:1, one launch (start us, length us, event | category | flops | bytes accessed | tf_op | source)
XLA Modules:
  0.0 101.3 jit_solution(9885395304574425153)
XLA Ops:
  0.6 8.9 %deposit.1 = (s32[2,256]{1,0:T(2,128)}, f32[2176,2,128]{2,1,0:T(2,128)}) custom-call(s32[4,256]{1,0:T(4,128)} %bitcast.8, f32[3,256,128]{2,1,0:T(8,128)} %place_ref.5, f32[256,128]{1,0:T(8,128)} %radius_ref.3, f32[256,128]{1,0:T(8,128)} %speed_ref.3), custom_call_target="tpu_custom_call" | custom-call | flops 11500000256 | bytes 1000 | tf_op jit(solution)/shard_map/deposit/pallas_call | solution.py:567
  9.5 11.5 %all-to-all-start = ((f32[2176,2,128]{2,1,0:T(2,128)}), f32[2176,2,128]{2,1,0:T(2,128)S(1)}, u32[]{:S(2)}, u32[]{:S(2)}) async-start(f32[2176,2,128]{2,1,0:T(2,128)} %get-tuple-element.21), calls=%async_computation | async-start | bytes 4456448 | tf_op jit(solution)/shard_map/all_to_all | solution.py:556
  21.0 13.2 %sweep_x.1 = (f32[7,768,128]{2,1,0:T(8,128)}, f32[24,32,128]{2,1,0:T(8,128)}, f32[7,96,128]{2,1,0:T(8,128)}, f32[7,96,128]{2,1,0:T(8,128)}, f32[7,3,24,128]{3,2,1,0:T(8,128)}, /*index=5*/f32[7,3,24,128]{3,2,1,0:T(8,128)}) custom-call(f32[7,24,32,128]{3,2,1,0:T(8,128)} %flow_in.1), custom_call_target="tpu_custom_call" | custom-call | flops 16099999744 | bytes 1000 | tf_op jit(solution)/shard_map/sweep_x/pallas_call | solution.py:591
  34.3 1.7 %collective-permute-start = (f32[7,96,128]{2,1,0:T(8,128)}, f32[7,96,128]{2,1,0:T(8,128)}, u32[]{:S(2)}, u32[]{:S(2)}) collective-permute-start(f32[7,96,128]{2,1,0:T(8,128)} %get-tuple-element.31), channel_id=1, source_target_pairs={{0,4},{4,8},{8,12},{12,16},{16,20},{20,24},{24,28},{28,32},{32,36}... | collective-permute-start | bytes 1032200 | tf_op jit(solution)/shard_map/ppermute | solution.py:550
  36.0 0.0 collective-permute-start.1
  36.0 1.3 %collective-permute-start.2 = (f32[7,3,24,128]{3,2,1,0:T(8,128)}, f32[7,3,24,128]{3,2,1,0:T(8,128)}, u32[]{:S(2)}, u32[]{:S(2)}) collective-permute-start(f32[7,3,24,128]{3,2,1,0:T(8,128)} %get-tuple-element.33), channel_id=1, source_target_pairs={{0,1},{1,2},{2,3},{3,0},{4,5},{5,6},{6,7},{7,4},{8,9},{9,10},{10,1... | collective-permute-start | bytes 774152 | tf_op jit(solution)/shard_map/ppermute | solution.py:550
  37.3 1.8 %collective-permute-start.3 = (f32[7,3,24,128]{3,2,1,0:T(8,128)}, f32[7,3,24,128]{3,2,1,0:T(8,128)}, u32[]{:S(2)}, u32[]{:S(2)}) collective-permute-start(f32[7,3,24,128]{3,2,1,0:T(8,128)} %get-tuple-element.34), channel_id=1, source_target_pairs={{1,0},{2,1},{3,2},{0,3},{5,4},{6,5},{7,6},{4,7},{9,8},{10,9},{11,1... | collective-permute-start | bytes 774152 | tf_op jit(solution)/shard_map/ppermute | solution.py:551
  39.1 2.2 %ready.1.ready_ref = f32[3,256,128]{2,1,0:T(8,128)} custom-call(f32[3,256,128]{2,1,0:T(8,128)} %place_ref.5, f32[256,128]{1,0:T(8,128)} %radius_ref.3, f32[256,128]{1,0:T(8,128)} %speed_ref.3, f32[256,128]{1,0:T(8,128)} %rest_ref), custom_call_target="tpu_custom_call" | custom-call | flops 2300000000 | bytes 1000 | tf_op jit(solution)/shard_map/ready/pallas_call | solution.py:621
  41.2 12.2 %all-to-all-done.returned_ref = f32[2176,2,128]{2,1,0:T(2,128)S(1)} async-done(((f32[2176,2,128]{2,1,0:T(2,128)}), f32[2176,2,128]{2,1,0:T(2,128)S(1)}, u32[]{:S(2)}, u32[]{:S(2)}) %all-to-all-start) | async-done | bytes 2228256 | tf_op jit(solution)/shard_map/all_to_all | solution.py:556
  53.4 0.0 copy-start
  53.5 0.7 convert_bitcast_fusion.asked_ref
  54.2 4.1 %serve.1 = f32[1024,4,128]{2,1,0:T(4,128)} custom-call(s32[128,8]{1,0:T(8,128)} %convert_bitcast_fusion.asked_ref, f32[768,128]{1,0:T(8,128)} %bitcast.9), custom_call_target="tpu_custom_call" | custom-call | flops 5750000128 | bytes 1000 | tf_op jit(solution)/shard_map/serve/pallas_call | solution.py:633
  58.3 0.0 copy-done
  58.3 7.0 %all-to-all-start.1 = ((f32[1024,4,128]{2,1,0:T(4,128)}), f32[1024,4,128]{2,1,0:T(4,128)}, u32[]{:S(2)}, u32[]{:S(2)}) async-start(f32[1024,4,128]{2,1,0:T(4,128)} %serve.1), calls=%async_computation.1 | async-start | bytes 4194304 | tf_op jit(solution)/shard_map/all_to_all | solution.py:556
  65.3 4.8 %scatter.1.source_in = f32[24,32,128]{2,1,0:T(8,128)} custom-call(s32[128,8]{1,0:T(8,128)} %convert_bitcast_fusion.asked_ref, f32[2176,2,128]{2,1,0:T(2,128)} %copy-done), custom_call_target="tpu_custom_call" | custom-call | flops 6899999744 | bytes 1000 | tf_op jit(solution)/shard_map/scatter/pallas_call | solution.py:646
  70.1 0.0 collective-permute-done.2.y_below_in
  70.1 0.0 collective-permute-done.3.y_above_in
  70.1 0.0 collective-permute-done.z_below_in
  70.1 0.0 collective-permute-done.1.z_above_in
  70.1 22.0 %sweep_yz.1 = f32[7,24,32,128]{3,2,1,0:T(8,128)} custom-call(f32[7,24,32,128]{3,2,1,0:T(8,128)} %flow_in.1, f32[7,768,128]{2,1,0:T(8,128)} %get-tuple-element.28.change_in, f32[24,32,128]{2,1,0:T(8,128)} %scatter.1.source_in, f32[7,96,128]{2,1,0:T(8,128)} %collective-permute-done.z_below_in, f32[7,96,128]{2,1,0:T(8,128)} %collective-permute-done.1.z_above_in, ...), custom_call_target="tpu_custom_call" | custom-call | flops 27599998976 | bytes 1000 | tf_op jit(solution)/shard_map/sweep_yz/pallas_call | solution.py:658
  92.1 3.4 %all-to-all-done.1.rows_ref = f32[1024,4,128]{2,1,0:T(4,128)} async-done(((f32[1024,4,128]{2,1,0:T(4,128)}), f32[1024,4,128]{2,1,0:T(4,128)}, u32[]{:S(2)}, u32[]{:S(2)}) %all-to-all-start.1) | async-done | bytes 2097184 | tf_op jit(solution)/shard_map/all_to_all | solution.py:556
  95.5 5.9 %sample.1 = f32[2,256,128]{2,1,0:T(8,128)} custom-call(s32[2,256]{1,0:T(2,128)} %get-tuple-element.36.slot_ref, f32[3,256,128]{2,1,0:T(8,128)} %place_ref.5, f32[3,256,128]{2,1,0:T(8,128)} %ready.1.ready_ref, f32[1024,4,128]{2,1,0:T(4,128)} %all-to-all-done.1.rows_ref), custom_call_target="tpu_custom_call" | custom-call | flops 8049999872 | bytes 1000 | tf_op jit(solution)/shard_map/sample/pallas_call | solution.py:686
  (1 shorter events, 0.0 us)
Async XLA Ops:
  9.5 43.9 %all-to-all-start = ((f32[2176,2,128]{2,1,0:T(2,128)}), f32[2176,2,128]{2,1,0:T(2,128)S(1)}, u32[]{:S(2)}, u32[]{:S(2)}) async-start(f32[2176,2,128]{2,1,0:T(2,128)} %get-tuple-element.21), calls=%async_computation | async-start | bytes 4456448 | tf_op jit(solution)/shard_map/all_to_all | solution.py:556
  34.3 35.8 %collective-permute-start = (f32[7,96,128]{2,1,0:T(8,128)}, f32[7,96,128]{2,1,0:T(8,128)}, u32[]{:S(2)}, u32[]{:S(2)}) collective-permute-start(f32[7,96,128]{2,1,0:T(8,128)} %get-tuple-element.31), channel_id=1, source_target_pairs={{0,4},{4,8},{8,12},{12,16},{16,20},{20,24},{24,28},{28,32},{32,36}... | collective-permute-start | bytes 1032200 | tf_op jit(solution)/shard_map/ppermute | solution.py:550
  36.0 34.1 %collective-permute-start.1 = (f32[7,96,128]{2,1,0:T(8,128)}, f32[7,96,128]{2,1,0:T(8,128)}, u32[]{:S(2)}, u32[]{:S(2)}) collective-permute-start(f32[7,96,128]{2,1,0:T(8,128)} %get-tuple-element.32), channel_id=1, source_target_pairs={{4,0},{8,4},{12,8},{16,12},{20,16},{24,20},{28,24},{32,28},{36,32}... | collective-permute-start | bytes 1032200 | tf_op jit(solution)/shard_map/ppermute | solution.py:551
  36.0 34.1 %collective-permute-start.2 = (f32[7,3,24,128]{3,2,1,0:T(8,128)}, f32[7,3,24,128]{3,2,1,0:T(8,128)}, u32[]{:S(2)}, u32[]{:S(2)}) collective-permute-start(f32[7,3,24,128]{3,2,1,0:T(8,128)} %get-tuple-element.33), channel_id=1, source_target_pairs={{0,1},{1,2},{2,3},{3,0},{4,5},{5,6},{6,7},{7,4},{8,9},{9,10},{10,1... | collective-permute-start | bytes 774152 | tf_op jit(solution)/shard_map/ppermute | solution.py:550
  37.3 32.8 %collective-permute-start.3 = (f32[7,3,24,128]{3,2,1,0:T(8,128)}, f32[7,3,24,128]{3,2,1,0:T(8,128)}, u32[]{:S(2)}, u32[]{:S(2)}) collective-permute-start(f32[7,3,24,128]{3,2,1,0:T(8,128)} %get-tuple-element.34), channel_id=1, source_target_pairs={{1,0},{2,1},{3,2},{0,3},{5,4},{6,5},{7,6},{4,7},{9,8},{10,9},{11,1... | collective-permute-start | bytes 774152 | tf_op jit(solution)/shard_map/ppermute | solution.py:551
  53.4 4.9 %copy-start = (f32[2176,2,128]{2,1,0:T(2,128)}, f32[2176,2,128]{2,1,0:T(2,128)S(1)}, u32[]{:S(2)}) copy-start(f32[2176,2,128]{2,1,0:T(2,128)S(1)} %all-to-all-done.returned_ref) | copy-start | bytes 6684676
  58.3 37.2 %all-to-all-start.1 = ((f32[1024,4,128]{2,1,0:T(4,128)}), f32[1024,4,128]{2,1,0:T(4,128)}, u32[]{:S(2)}, u32[]{:S(2)}) async-start(f32[1024,4,128]{2,1,0:T(4,128)} %serve.1), calls=%async_computation.1 | async-start | bytes 4194304 | tf_op jit(solution)/shard_map/all_to_all | solution.py:556
